TPU v7x, 32 devices: a whole 2x2x4 slice. The times are simulated.
32 devices in a mesh: grp: 2 (over core), dp: 16 (over z, y, x).
Axes of the slice: x: 2, y: 2, z: 4, core: 2. Of those that a mesh axis runs over, the one named last changes fastest.
Arguments:
- pixels: bfloat16 [512, 49, 768], P(('grp', 'dp')), may hold values from -20 to 20
- visible: int32 [512, 49], P(('grp', 'dp')), may hold values from 0 to 195, as said below
- scale_index: int32 [512], P(('grp', 'dp')), may hold values from 0 to 3
- cotangent: bfloat16 [2, 64, 16, 49, 512], P('grp', 'dp'), may hold values from -6 to 6
- pe_weight: float32 [768, 1024], P(None, ('grp', 'dp')), may hold values from -2 to 2
- pe_first: float32 [768, 1024], P(None, ('grp', 'dp')), may hold values from -0.00061035156 to 0.00061035156
- pe_second: float32 [768, 1024], P(None, ('grp', 'dp')), may hold values from 8.573906e-09 to 3.3972082e-08
- qkv_weight: float32 [1024, 3072], P(('grp', 'dp')), may hold values from -0.1875 to 0.1875
- qkv_first: float32 [1024, 3072], P(('grp', 'dp')), may hold values from -0.00036621094 to 0.00036621094
- qkv_second: float32 [1024, 3072], P(('grp', 'dp')), may hold values from 2.4387998e-09 to 9.66317e-09
- out_weight: float32 [1024, 1024], P(None, ('grp', 'dp')), may hold values from -0.5 to 0.5
- out_first: float32 [1024, 1024], P(None, ('grp', 'dp')), may hold values from -0.00036621094 to 0.00036621094
- out_second: float32 [1024, 1024], P(None, ('grp', 'dp')), may hold values from 2.4387998e-09 to 9.66317e-09
- up_weight: float32 [1024, 4096], P(('grp', 'dp')), may hold values from -0.1875 to 0.1875
- up_first: float32 [1024, 4096], P(('grp', 'dp')), may hold values from -0.00036621094 to 0.00036621094
- up_second: float32 [1024, 4096], P(('grp', 'dp')), may hold values from 2.4387998e-09 to 9.66317e-09
- down_weight: float32 [4096, 1024], P(None, ('grp', 'dp')), may hold values from -0.09375 to 0.09375
- down_first: float32 [4096, 1024], P(None, ('grp', 'dp')), may hold values from -0.00036621094 to 0.00036621094
- down_second: float32 [4096, 1024], P(None, ('grp', 'dp')), may hold values from 2.4387998e-09 to 9.66317e-09
- dec_weight: float32 [1024, 512], P(('grp', 'dp')), may hold values from -2 to 2
- dec_first: float32 [1024, 512], P(('grp', 'dp')), may hold values from -0.0008544922 to 0.0008544922
- dec_second: float32 [1024, 512], P(('grp', 'dp')), may hold values from 1.5242499e-08 to 6.039481e-08
- vectors: float32 [14848], P(('grp', 'dp')), may hold values from -4 to 4
- vec_first: float32 [14848], P(('grp', 'dp')), may hold values from -0.0012207031 to 0.0012207031
- vec_second: float32 [14848], P(('grp', 'dp')), may hold values from 3.4295624e-08 to 1.3588833e-07
Outputs:
- decoded: bfloat16 [2, 64, 16, 49, 512], P('grp', 'dp')
- pixel_grad: float32 [512, 49, 768], P(('grp', 'dp'))
- pe_first_new: float32 [768, 1024], P(None, ('grp', 'dp'))
- pe_second_new: float32 [768, 1024], P(None, ('grp', 'dp'))
- pe_new: float32 [768, 1024], P(None, ('grp', 'dp'))
- qkv_first_new: float32 [1024, 3072], P(('grp', 'dp'))
- qkv_second_new: float32 [1024, 3072], P(('grp', 'dp'))
- qkv_new: float32 [1024, 3072], P(('grp', 'dp'))
- out_first_new: float32 [1024, 1024], P(None, ('grp', 'dp'))
- out_second_new: float32 [1024, 1024], P(None, ('grp', 'dp'))
- out_new: float32 [1024, 1024], P(None, ('grp', 'dp'))
- up_first_new: float32 [1024, 4096], P(('grp', 'dp'))
- up_second_new: float32 [1024, 4096], P(('grp', 'dp'))
- up_new: float32 [1024, 4096], P(('grp', 'dp'))
- down_first_new: float32 [4096, 1024], P(None, ('grp', 'dp'))
- down_second_new: float32 [4096, 1024], P(None, ('grp', 'dp'))
- down_new: float32 [4096, 1024], P(None, ('grp', 'dp'))
- dec_first_new: float32 [1024, 512], P(('grp', 'dp'))
- dec_second_new: float32 [1024, 512], P(('grp', 'dp'))
- dec_new: float32 [1024, 512], P(('grp', 'dp'))
- vec_first_new: float32 [14848], P(('grp', 'dp'))
- vec_second_new: float32 [14848], P(('grp', 'dp'))
- vec_new: float32 [14848], P(('grp', 'dp'))
- grad_norm: float32 [], replicated
Inputs may be any that keep to these rules, and one draw needn't show every extreme that they name: `visible`: each image names 49 distinct grid positions in increasing order.
All inputs are finite; a program needn't handle non-finite values.
Results may differ from a plain program's by a relative error of at most 0.013.
The roundings to bfloat16 on the way count: a program that leaves them out, or rounds other values in their place, can miss the bound.
Values may be sent and summed in bfloat16 or wider, within the bound.
No kernel may reach another device: no remote copies, remote signals or barrier semaphores. Data moves between devices by JAX's collectives and lax.ppermute only.
A program may use at most 320 MiB of HBM per device.

v0:
```python
import jax
import jax.numpy as jnp
from jax import lax
from jax.sharding import PartitionSpec as P

D = 1024
FF = 4096
HEADS = 16
HDIM = 64
DDEC = 512
PATCH = 16
SIDE = 14
BANDS = 3
STEP = 10
PIX = 768
GRID = 196
VIS = 49
QUART = 49


EPS_NORM = 1e-05
BETA_ONE = 0.9
BETA_TWO = 0.95
ADAM_EPS = 1e-08
LR_MATRIX = 0.08
LR_VECTOR = 0.3
DECAY_MATRIX = 0.05
CLIP_LEVEL = 1.0


def forward_product(left, right):
    return jnp.dot(left, right, preferred_element_type=jnp.float32)


def back_product(left, right):
    return lax.dot_general(
        left, right, (((left.ndim - 1,), (1,)), ((), ())), preferred_element_type=jnp.float32
    )


def weight_product(left, right):
    return lax.dot_general(
        left, right, (((0,), (0,)), ((), ())), preferred_element_type=jnp.float32
    )


def angle_table(grid_rows, grid_cols, ratios, channels):
    quarter = channels // 4
    frequency = jnp.exp(jnp.arange(quarter).astype(jnp.float32) * (-jnp.log(10000.0) / quarter))
    row_angle = (grid_rows * ratios)[..., None] * frequency
    col_angle = (grid_cols * ratios)[..., None] * frequency
    return jnp.concatenate(
        [jnp.sin(row_angle), jnp.cos(row_angle), jnp.sin(col_angle), jnp.cos(col_angle)], axis=-1
    )


def split_vectors(vector_all):
    pieces = tuple((vector_all[number * D : (number + 1) * D] for number in range(10)))
    return (pieces, vector_all[10 * D : 10 * D + FF], vector_all[10 * D + FF :])


def norm_forward(hidden_in, norm_gain, norm_shift):
    center = hidden_in - jnp.mean(hidden_in, axis=-1, keepdims=True)
    inv_std = lax.rsqrt(jnp.mean(center * center, axis=-1, keepdims=True) + EPS_NORM)
    normed = center * inv_std
    return (normed * norm_gain + norm_shift, normed, inv_std)


def norm_backward(grad_out, normed, inv_std, norm_gain):
    scaled = grad_out * norm_gain
    inner = (
        scaled
        - jnp.mean(scaled, axis=-1, keepdims=True)
        - normed * jnp.mean(scaled * normed, axis=-1, keepdims=True)
    )
    return (inner * inv_std, jnp.sum(grad_out * normed, axis=0), jnp.sum(grad_out, axis=0))


def gelu_slope(preact):
    return (
        0.5 * (1.0 + lax.erf(preact * 0.7071067811865476))
        + preact * jnp.exp(-0.5 * preact * preact) * 0.3989422804014327
    )


def adamw_update(weight, moment_one, moment_two, gradient, step_rate, decay_rate):
    new_one = BETA_ONE * moment_one + (1.0 - BETA_ONE) * gradient
    new_two = BETA_TWO * moment_two + (1.0 - BETA_TWO) * gradient * gradient
    fixed_one = new_one / (1.0 - BETA_ONE**STEP)
    fixed_two = new_two / (1.0 - BETA_TWO**STEP)
    new_weight = weight - step_rate * (
        fixed_one / (jnp.sqrt(fixed_two) + ADAM_EPS) + decay_rate * weight
    )
    return (new_one, new_two, new_weight)


def local(
    pixels,
    visible,
    scale_index,
    cotangent,
    pe_weight,
    pe_first,
    pe_second,
    qkv_weight,
    qkv_first,
    qkv_second,
    out_weight,
    out_first,
    out_second,
    up_weight,
    up_first,
    up_second,
    down_weight,
    down_first,
    down_second,
    dec_weight,
    dec_first,
    dec_second,
    vectors,
    vec_first,
    vec_second,
):
    image_count = pixels.shape[0]
    row_count = image_count * VIS
    device_count = lax.axis_size(("grp", "dp"))
    dp_count = lax.axis_size("dp")
    pixel_rows = pixels.astype(jnp.float32).reshape(row_count, BANDS, PATCH * PATCH)
    band_sum, band_square = lax.psum(
        (jnp.sum(pixel_rows, axis=(0, 2)), jnp.sum(pixel_rows * pixel_rows, axis=(0, 2))),
        ("grp", "dp"),
    )
    entry_count = row_count * device_count * PATCH * PATCH
    band_mean = band_sum / entry_count
    band_scale = lax.rsqrt(band_square / entry_count - band_mean * band_mean + EPS_NORM)
    pixel_norm = (pixel_rows - band_mean[None, :, None]) * band_scale[None, :, None]
    pixel_low = pixel_norm.reshape(row_count, PIX).astype(jnp.bfloat16)
    pe_full, qkv_full, out_full, up_full, down_full, dec_full, vector_low = (
        lax.all_gather(pe_weight.astype(jnp.bfloat16), ("grp", "dp"), axis=1, tiled=True),
        lax.all_gather(qkv_weight.astype(jnp.bfloat16), ("grp", "dp"), axis=0, tiled=True),
        lax.all_gather(out_weight.astype(jnp.bfloat16), ("grp", "dp"), axis=1, tiled=True),
        lax.all_gather(up_weight.astype(jnp.bfloat16), ("grp", "dp"), axis=0, tiled=True),
        lax.all_gather(down_weight.astype(jnp.bfloat16), ("grp", "dp"), axis=1, tiled=True),
        lax.all_gather(dec_weight.astype(jnp.bfloat16), ("grp", "dp"), axis=0, tiled=True),
        lax.all_gather(vectors.astype(jnp.bfloat16), ("grp", "dp"), axis=0, tiled=True),
    )
    pieces, up_bias, dec_bias = split_vectors(vector_low.astype(jnp.float32))
    (
        gain_one,
        shift_one,
        gain_two,
        shift_two,
        pe_bias,
        query_bias,
        value_bias,
        out_bias,
        down_bias,
        mask_token,
    ) = pieces
    ratio_image = jnp.power(2.0, scale_index.astype(jnp.float32) - 1.0)
    ratio_rows = jnp.repeat(ratio_image, VIS)
    spots = visible.reshape(row_count)
    enc_table = angle_table(
        (spots // SIDE).astype(jnp.float32), (spots % SIDE).astype(jnp.float32), ratio_rows, D
    )
    stream_in = forward_product(pixel_low, pe_full) + pe_bias + enc_table
    norm_out_one, normed_one, inv_std_one = norm_forward(stream_in, gain_one, shift_one)
    norm_one = norm_out_one.astype(jnp.bfloat16)
    projected = forward_product(norm_one, qkv_full) + jnp.concatenate(
        [query_bias, jnp.zeros_like(query_bias), value_bias]
    )
    projected = projected.astype(jnp.bfloat16).reshape(image_count, VIS, 3, HEADS, HDIM)
    queries = projected[:, :, 0]
    keys_head = projected[:, :, 1]
    values_head = projected[:, :, 2]
    scale_score = HDIM ** (-0.5)
    raw_scores = (
        jnp.einsum("nqhd,nkhd->nhqk", queries, keys_head, preferred_element_type=jnp.float32)
        * scale_score
    )
    score_peak = jnp.max(raw_scores, axis=-1, keepdims=True)
    log_total = score_peak + jnp.log(
        jnp.sum(jnp.exp(raw_scores - score_peak), axis=-1, keepdims=True)
    )
    softmaxed = jnp.exp(raw_scores - log_total)
    mixture = jnp.einsum(
        "nhqk,nkhd->nqhd",
        softmaxed.astype(jnp.bfloat16),
        values_head,
        preferred_element_type=jnp.float32,
    )
    mixture_low = mixture.reshape(row_count, D).astype(jnp.bfloat16)
    stream_mid = stream_in + forward_product(mixture_low, out_full) + out_bias
    norm_out_two, normed_two, inv_std_two = norm_forward(stream_mid, gain_two, shift_two)
    norm_two = norm_out_two.astype(jnp.bfloat16)
    preact = forward_product(norm_two, up_full) + up_bias
    activated = jax.nn.gelu(preact, approximate=False).astype(jnp.bfloat16)
    stream_out = stream_mid + forward_product(activated, down_full) + down_bias
    placement = visible[:, :, None] == jnp.arange(GRID)[None, None, :]
    placement_low = placement.astype(jnp.bfloat16)
    vacant = 1.0 - jnp.sum(placement.astype(jnp.float32), axis=1)
    stream_low = stream_out.astype(jnp.bfloat16).reshape(image_count, VIS, D)
    full_grid = jnp.einsum(
        "nvg,nvd->ngd", placement_low, stream_low, preferred_element_type=jnp.float32
    )
    full_grid = (full_grid + vacant[:, :, None] * mask_token).astype(jnp.bfloat16)
    quarters = full_grid.reshape(4 * image_count, 1, QUART, D)
    ratio_quarter = jnp.repeat(ratio_image, 4).reshape(4 * image_count, 1).astype(jnp.bfloat16)
    received, received_ratio = (
        lax.all_to_all(quarters, "dp", split_axis=0, concat_axis=1, tiled=True),
        lax.all_to_all(ratio_quarter, "dp", split_axis=0, concat_axis=1, tiled=True),
    )
    item_count = received.shape[0]
    dp_index = lax.axis_index("dp")
    quarter_id = dp_index * item_count + jnp.arange(item_count)
    position = (quarter_id % 4)[:, None] * QUART + jnp.arange(QUART)[None, :]
    dec_table = angle_table(
        (position // SIDE).astype(jnp.float32)[:, None, :],
        (position % SIDE).astype(jnp.float32)[:, None, :],
        received_ratio.astype(jnp.float32)[:, :, None],
        DDEC,
    )
    dec_rows = forward_product(received, dec_full)
    decoded = (dec_rows + dec_bias + dec_table).astype(jnp.bfloat16)[None]
    grad_rows = cotangent[0].reshape(-1, DDEC)
    recv_rows = received.reshape(-1, D)
    dec_grad = weight_product(recv_rows, grad_rows)
    dec_bias_grad = jnp.sum(grad_rows.astype(jnp.float32), axis=0)
    grid_grad = (
        back_product(grad_rows, dec_full)
        .astype(jnp.bfloat16)
        .reshape(item_count, dp_count, QUART, D)
    )
    returned = lax.all_to_all(grid_grad, "dp", split_axis=1, concat_axis=0, tiled=True).reshape(
        image_count, GRID, D
    )
    out_grad_rows = jnp.einsum(
        "nvg,ngd->nvd", placement_low, returned, preferred_element_type=jnp.float32
    ).reshape(row_count, D)
    mask_grad = jnp.einsum(
        "ng,ngd->d", vacant.astype(jnp.bfloat16), returned, preferred_element_type=jnp.float32
    )
    out_rows_low = out_grad_rows.astype(jnp.bfloat16)
    down_grad = weight_product(activated, out_rows_low)
    down_bias_grad = jnp.sum(out_grad_rows, axis=0)
    preact_grad = back_product(out_rows_low, down_full) * gelu_slope(preact)
    up_bias_grad = jnp.sum(preact_grad, axis=0)
    preact_low = preact_grad.astype(jnp.bfloat16)
    up_grad = weight_product(norm_two, preact_low)
    two_grad = back_product(preact_low, up_full)
    mid_grad, gain_two_grad, shift_two_grad = norm_backward(
        two_grad, normed_two, inv_std_two, gain_two
    )
    mid_grad = mid_grad + out_grad_rows
    mid_low = mid_grad.astype(jnp.bfloat16)
    out_grad = weight_product(mixture_low, mid_low)
    out_bias_grad = jnp.sum(mid_grad, axis=0)
    mixture_grad = (
        back_product(mid_low, out_full).astype(jnp.bfloat16).reshape(image_count, VIS, HEADS, HDIM)
    )
    again_scores = (
        jnp.einsum("nqhd,nkhd->nhqk", queries, keys_head, preferred_element_type=jnp.float32)
        * scale_score
    )
    again_probs = jnp.exp(again_scores - log_total)
    value_grad = jnp.einsum(
        "nhqk,nqhd->nkhd",
        again_probs.astype(jnp.bfloat16),
        mixture_grad,
        preferred_element_type=jnp.float32,
    )
    probs_grad = jnp.einsum(
        "nqhd,nkhd->nhqk", mixture_grad, values_head, preferred_element_type=jnp.float32
    )
    score_low = (
        again_probs
        * (probs_grad - jnp.sum(probs_grad * again_probs, axis=-1, keepdims=True))
        * scale_score
    ).astype(jnp.bfloat16)
    query_grad = jnp.einsum(
        "nhqk,nkhd->nqhd", score_low, keys_head, preferred_element_type=jnp.float32
    )
    key_grad = jnp.einsum("nhqk,nqhd->nkhd", score_low, queries, preferred_element_type=jnp.float32)
    projected_grad = jnp.stack([query_grad, key_grad, value_grad], axis=2).reshape(row_count, 3 * D)
    query_bias_grad = jnp.sum(projected_grad[:, :D], axis=0)
    value_bias_grad = jnp.sum(projected_grad[:, 2 * D :], axis=0)
    projected_low = projected_grad.astype(jnp.bfloat16)
    qkv_grad = weight_product(norm_one, projected_low)
    one_grad = back_product(projected_low, qkv_full)
    in_grad, gain_one_grad, shift_one_grad = norm_backward(
        one_grad, normed_one, inv_std_one, gain_one
    )
    in_grad = in_grad + mid_grad
    pe_bias_grad = jnp.sum(in_grad, axis=0)
    in_low = in_grad.astype(jnp.bfloat16)
    pe_grad = weight_product(pixel_low, in_low)
    norm_grad = back_product(in_low, pe_full).reshape(row_count, BANDS, PATCH * PATCH)
    pixel_grad = (norm_grad * band_scale[None, :, None]).reshape(image_count, VIS, PIX)
    vec_grad = jnp.concatenate(
        [
            gain_one_grad,
            shift_one_grad,
            gain_two_grad,
            shift_two_grad,
            pe_bias_grad,
            query_bias_grad,
            value_bias_grad,
            out_bias_grad,
            down_bias_grad,
            mask_grad,
            up_bias_grad,
            dec_bias_grad,
        ]
    )
    pe_shard, qkv_shard, out_shard, up_shard, down_shard, dec_shard, vec_shard = (
        lax.psum_scatter(pe_grad, ("grp", "dp"), scatter_dimension=1, tiled=True),
        lax.psum_scatter(qkv_grad, ("grp", "dp"), scatter_dimension=0, tiled=True),
        lax.psum_scatter(out_grad, ("grp", "dp"), scatter_dimension=1, tiled=True),
        lax.psum_scatter(up_grad, ("grp", "dp"), scatter_dimension=0, tiled=True),
        lax.psum_scatter(down_grad, ("grp", "dp"), scatter_dimension=1, tiled=True),
        lax.psum_scatter(dec_grad, ("grp", "dp"), scatter_dimension=0, tiled=True),
        lax.psum_scatter(vec_grad, ("grp", "dp"), scatter_dimension=0, tiled=True),
    )
    shards = (pe_shard, qkv_shard, out_shard, up_shard, down_shard, dec_shard, vec_shard)
    local_squares = sum((jnp.sum(gradient * gradient) for gradient in shards))
    squares = lax.psum(local_squares, ("grp", "dp"))
    grad_norm = jnp.sqrt(squares)
    clip_factor = jnp.minimum(1.0, CLIP_LEVEL / grad_norm)
    params = (pe_weight, qkv_weight, out_weight, up_weight, down_weight, dec_weight, vectors)
    firsts = (pe_first, qkv_first, out_first, up_first, down_first, dec_first, vec_first)
    seconds = (pe_second, qkv_second, out_second, up_second, down_second, dec_second, vec_second)
    results = []
    for number in range(7):
        step_rate = LR_VECTOR if number == 6 else LR_MATRIX
        decay_rate = 0.0 if number == 6 else DECAY_MATRIX
        results.append(
            adamw_update(
                params[number],
                firsts[number],
                seconds[number],
                shards[number] * clip_factor,
                step_rate,
                decay_rate,
            )
        )
    return (
        decoded,
        pixel_grad,
        results[0][0],
        results[0][1],
        results[0][2],
        results[1][0],
        results[1][1],
        results[1][2],
        results[2][0],
        results[2][1],
        results[2][2],
        results[3][0],
        results[3][1],
        results[3][2],
        results[4][0],
        results[4][1],
        results[4][2],
        results[5][0],
        results[5][1],
        results[5][2],
        results[6][0],
        results[6][1],
        results[6][2],
        grad_norm,
    )


def solution(mesh):
    return jax.shard_map(
        local,
        mesh=mesh,
        in_specs=(
            P(("grp", "dp"), None, None),
            P(("grp", "dp"), None),
            P(("grp", "dp")),
            P("grp", "dp", None, None, None),
            P(None, ("grp", "dp")),
            P(None, ("grp", "dp")),
            P(None, ("grp", "dp")),
            P(("grp", "dp"), None),
            P(("grp", "dp"), None),
            P(("grp", "dp"), None),
            P(None, ("grp", "dp")),
            P(None, ("grp", "dp")),
            P(None, ("grp", "dp")),
            P(("grp", "dp"), None),
            P(("grp", "dp"), None),
            P(("grp", "dp"), None),
            P(None, ("grp", "dp")),
            P(None, ("grp", "dp")),
            P(None, ("grp", "dp")),
            P(("grp", "dp"), None),
            P(("grp", "dp"), None),
            P(("grp", "dp"), None),
            P(("grp", "dp")),
            P(("grp", "dp")),
            P(("grp", "dp")),
        ),
        out_specs=(
            P("grp", "dp", None, None, None),
            P(("grp", "dp"), None, None),
            P(None, ("grp", "dp")),
            P(None, ("grp", "dp")),
            P(None, ("grp", "dp")),
            P(("grp", "dp"), None),
            P(("grp", "dp"), None),
            P(("grp", "dp"), None),
            P(None, ("grp", "dp")),
            P(None, ("grp", "dp")),
            P(None, ("grp", "dp")),
            P(("grp", "dp"), None),
            P(("grp", "dp"), None),
            P(("grp", "dp"), None),
            P(None, ("grp", "dp")),
            P(None, ("grp", "dp")),
            P(None, ("grp", "dp")),
            P(("grp", "dp"), None),
            P(("grp", "dp"), None),
            P(("grp", "dp"), None),
            P(("grp", "dp")),
            P(("grp", "dp")),
            P(("grp", "dp")),
            P(),
        ),
        check_vma=False,
    )
```

profile of v0, /device:TPU:0, one launch (start us, length us, event | category | flops | bytes accessed | tf_op | source)
XLA Modules:
  0.0 2111.4 jit_solution(17420247691914707210)
XLA Ops:
  24.5 43.8 %all-gather.17.cloned.1.call-done = bf16[1024,512]{1,0:T(8,128)(2,1)} async-done(((bf16[32,512]{1,0:T(8,128)(2,1)}), bf16[1024,512]{1,0:T(8,128)(2,1)}) %all-gather.17.cloned.1.call-update) | async-done | bytes 1048592 | tf_op jit(solution)/shard_map/all_gather | solution.py:144
  74.9 8.8 reshape.301
  83.7 11.2 copy.107
  101.2 183.6 %all-reduce.2 = (f32[3]{0:T(128)S(1)}, f32[3]{0:T(128)S(1)}) all-reduce(f32[3]{0:T(128)S(1)} %reduce_sum.298, f32[3]{0:T(128)S(1)} %reduce_sum.295), channel_id=1, replica_groups=mesh['grp'=2,'dp'=16] {'grp','dp'}, use_global_device_ids=true, to_apply=%region_5.6 | all-reduce | flops 6 | bytes 48 | tf_op jit(solution)/shard_map/psum | solution.py:129
  288.0 39.9 %all-reduce = bf16[14848]{0:T(1024)(128)(2,1)S(1)} all-reduce(bf16[14848]{0:T(1024)(128)(2,1)S(1)} %dynamic-update-slice), channel_id=1, replica_groups=mesh['grp'=2,'dp'=16] {'grp','dp'}, use_global_device_ids=true, to_apply=%add | all-reduce | flops 14848 | bytes 59392
  343.3 10.6 add_convert_fusion.1
  353.9 12.8 reshape.298
  366.6 16.0 fusion.120
  410.3 10.2 fusion.124
  424.3 8.9 all-gather.13.cloned.1.call-done
  433.2 38.9 %fusion.3 = (bf16[784,4096]{1,0:T(8,128)(2,1)}, f32[784,4096]{1,0:T(8,128)}) fusion(f32[4096]{0:T(1024)S(1)} %slice.79, bf16[1024,4096]{1,0:T(8,128)(2,1)} %all-gather.13.cloned.1.call-done, f32[784,1024]{1,0:T(8,128)S(1)} %copy-done.11, f32[1024]{0:T(1024)S(1)} %get-tuple-element.168, f32[1024]{0:T(1024)S(1)} %get-tuple-element.167, ...), kind=kOutput, calls=%fused_computation.7 | convolution fusion | flops 6792626176 | bytes 30898304 | tf_op jit(solution)/shard_map/dot_general | solution.py:32
  472.1 40.5 %all-gather.15.cloned.1.call-done = bf16[4096,1024]{0,1:T(8,128)(2,1)} async-done(((bf16[4096,32]{0,1:T(8,128)(2,1)}), bf16[4096,1024]{0,1:T(8,128)(2,1)}) %all-gather.15.cloned.1.call-update) | async-done | bytes 8388624 | tf_op jit(solution)/shard_map/all_gather | solution.py:143
  512.7 17.7 fusion.125
  530.4 11.1 multiply_reduce_fusion.2
  567.1 16.8 fusion.54
  583.9 16.8 fusion.57
  600.7 11.6 add_convert_fusion.2
  630.5 16.4 reshape.305
  647.0 12.1 multiply_reduce_fusion.3
  693.2 135.4 %all-to-all-done = bf16[64,1,49,1024]{3,2,1,0:T(8,128)(2,1)} async-done(((bf16[64,1,49,1024]{3,2,1,0:T(8,128)(2,1)}), bf16[64,1,49,1024]{3,2,1,0:T(8,128)(2,1)}, u32[]{:S(2)}, u32[]{:S(2)}) %all-to-all-start) | async-done | bytes 6422560 | tf_op jit(solution)/shard_map/all_to_all | solution.py:210
  835.9 8.8 reshape.307
  853.6 13.7 fusion.60
  869.3 14.8 fusion.47
  886.0 14.4 fusion.74
  901.7 35.6 %all-to-all-start.1 = ((bf16[16,4,1]{1,2,0:T(2,128)(2,1)}), bf16[16,4,1]{1,2,0:T(2,128)(2,1)S(1)}, u32[]{:S(2)}, u32[]{:S(2)}) async-start(bf16[16,4,1]{1,2,0:T(2,128)(2,1)} %broadcast_in_dim.10), calls=%async_computation.1 | async-start | bytes 16384 | tf_op jit(solution)/shard_map/all_to_all | solution.py:211
  944.6 15.2 multiply_sine_fusion.1
  974.6 40.1 %all-reduce.1 = f32[14848]{0:T(1024)S(1)} all-reduce(f32[14848]{0:T(1024)S(1)} %constant_dynamic-update-slice_fusion), channel_id=8, replica_groups=mesh['grp'=2,'dp'=16] {'grp','dp'}, use_global_device_ids=true, to_apply=%region_41.42.clone | all-reduce | flops 14848 | bytes 118784
  1028.2 131.3 %reduce-scatter.17.cloned.1.call-done = f32[32,512]{1,0:T(8,128)} async-done(((f32[1024,512]{1,0:T(8,128)}), f32[32,512]{1,0:T(8,128)}) %reduce-scatter.17.cloned.1.call-update) | async-done | bytes 65552 | tf_op jit(solution)/shard_map/reduce_scatter | solution.py:321
  1161.0 157.9 %reduce-scatter.9.cloned.1.call-done = f32[32,3072]{1,0:T(8,128)} async-done(((f32[1024,3072]{1,0:T(8,128)}), f32[32,3072]{1,0:T(8,128)}) %reduce-scatter.9.cloned.1.call-update) | async-done | bytes 393232 | tf_op jit(solution)/shard_map/reduce_scatter | solution.py:317
  1322.5 355.1 %reduce-scatter.13.cloned.1.call-done = f32[32,4096]{1,0:T(8,128)} async-done(((f32[1024,4096]{1,0:T(8,128)}), f32[32,4096]{1,0:T(8,128)}) %reduce-scatter.13.cloned.1.call-update) | async-done | bytes 524304 | tf_op jit(solution)/shard_map/reduce_scatter | solution.py:319
  1680.1 359.7 %reduce-scatter.15.cloned.1.call-done = f32[4096,32]{0,1:T(8,128)} async-done(((f32[4096,1024]{0,1:T(8,128)}), f32[4096,32]{0,1:T(8,128)}) %reduce-scatter.15.cloned.1.call-update) | async-done | bytes 524304 | tf_op jit(solution)/shard_map/reduce_scatter | solution.py:320
  2048.6 42.4 %psum.23 = f32[]{:T(128)} all-reduce(f32[]{:T(128)S(6)} %add.374), channel_id=1, replica_groups=mesh['grp'=2,'dp'=16] {'grp','dp'}, use_global_device_ids=true, to_apply=%region_43.44 | all-reduce | flops 1 | bytes 8 | tf_op jit(solution)/shard_map/psum | solution.py:326
  (315 shorter events, 237.0 us)
Async XLA Ops:
  7.2 61.0 %all-gather.17.cloned.1.call-start = ((), (), s32[]{:S(2)}) async-start(), calls=%async_computation.14 | async-start | bytes 1081344 | tf_op jit(solution)/shard_map/all_gather | solution.py:144
  8.7 329.3 %all-gather.7.cloned.1.call-start = ((), (), s32[]{:S(2)}) async-start(), calls=%async_computation.9 | async-start | bytes 1622016 | tf_op jit(solution)/shard_map/all_gather | solution.py:139
  10.3 332.9 %all-gather.9.cloned.1.call-start = ((), (), s32[]{:S(2)}) async-start(), calls=%async_computation.10 | async-start | bytes 6488064 | tf_op jit(solution)/shard_map/all_gather | solution.py:140
  12.1 386.8 %all-gather.11.cloned.1.call-start = ((), (), s32[]{:S(2)}) async-start(), calls=%async_computation.11 | async-start | bytes 2162688 | tf_op jit(solution)/shard_map/all_gather | solution.py:141
  13.7 419.5 %all-gather.13.cloned.1.call-start = ((), (), s32[]{:S(2)}) async-start(), calls=%async_computation.12 | async-start | bytes 8650752 | tf_op jit(solution)/shard_map/all_gather | solution.py:142
  94.9 310.4 %all-to-all-start.2 = ((bf16[4,16,49,1024]{3,0,2,1:T(4,128)(2,1)}), bf16[4,16,49,1024]{3,0,2,1:T(4,128)(2,1)}, u32[]{:S(2)}, u32[]{:S(2)}) async-start(bf16[4,16,49,1024]{3,0,2,1:T(4,128)(2,1)} %copy.107), calls=%async_computation.2 | async-start | bytes 12845056 | tf_op jit(solution)/shard_map/all_to_all | solution.py:234
  99.7 186.8 %copy-start.59 = (f32[464]{0:T(512)S(1)}, f32[464]{0:T(512)}, u32[]{:S(2)}) copy-start(f32[464]{0:T(512)} %param.47) | copy-start | bytes 5572
  99.7 186.8 %copy-start.41 = (s32[16,49]{1,0:T(8,128)S(1)}, s32[16,49]{1,0:T(8,128)}, u32[]{:S(2)}) copy-start(s32[16,49]{1,0:T(8,128)} %param.26) | copy-start | bytes 9412
  99.7 186.9 %copy-start.78 = (s32[16]{0:T(128)S(1)}, s32[16]{0:T(128)}, u32[]{:S(2)}) copy-start(s32[16]{0:T(128)} %param.27) | copy-start | bytes 196
  99.7 412.9 %all-gather.15.cloned.1.call-start = ((), (), s32[]{:S(2)}) async-start(), calls=%async_computation.13 | async-start | bytes 8650752 | tf_op jit(solution)/shard_map/all_gather | solution.py:143
  330.1 103.1 %copy-start.61 = (f32[1024]{0:T(1024)}, f32[1024]{0:T(1024)S(1)}, u32[]{:S(2)}) copy-start(f32[1024]{0:T(1024)S(1)} %get-tuple-element.168) | copy-start | bytes 12292
  673.0 155.7 %all-to-all-start = ((bf16[64,1,49,1024]{3,2,1,0:T(8,128)(2,1)}), bf16[64,1,49,1024]{3,2,1,0:T(8,128)(2,1)}, u32[]{:S(2)}, u32[]{:S(2)}) async-start(bf16[64,1,49,1024]{3,2,1,0:T(8,128)(2,1)} %bitcast.100), calls=%async_computation | async-start | bytes 14680064 | tf_op jit(solution)/shard_map/all_to_all | solution.py:210
  677.7 337.6 %reduce-scatter.7.cloned.1.call-start = ((), (), s32[]{:S(2)}) async-start(), calls=%async_computation.15 | async-start | bytes 3244032 | tf_op jit(solution)/shard_map/reduce_scatter | solution.py:316
  686.2 332.0 %reduce-scatter.11.cloned.1.call-start = ((), (), s32[]{:S(2)}) async-start(), calls=%async_computation.17 | async-start | bytes 4325376 | tf_op jit(solution)/shard_map/reduce_scatter | solution.py:318
  693.2 466.3 %reduce-scatter.17.cloned.1.call-start = ((), (), s32[]{:S(2)}) async-start(), calls=%async_computation.20 | async-start | bytes 2162688 | tf_op jit(solution)/shard_map/reduce_scatter | solution.py:321
  853.6 465.3 %reduce-scatter.9.cloned.1.call-start = ((), (), s32[]{:S(2)}) async-start(), calls=%async_computation.16 | async-start | bytes 12976128 | tf_op jit(solution)/shard_map/reduce_scatter | solution.py:317
  867.4 810.3 %reduce-scatter.13.cloned.1.call-start = ((), (), s32[]{:S(2)}) async-start(), calls=%async_computation.18 | async-start | bytes 17301504 | tf_op jit(solution)/shard_map/reduce_scatter | solution.py:319
  884.1 1155.8 %reduce-scatter.15.cloned.1.call-start = ((), (), s32[]{:S(2)}) async-start(), calls=%async_computation.19 | async-start | bytes 17301504 | tf_op jit(solution)/shard_map/reduce_scatter | solution.py:320
  901.7 42.8 %all-to-all-start.1 = ((bf16[16,4,1]{1,2,0:T(2,128)(2,1)}), bf16[16,4,1]{1,2,0:T(2,128)(2,1)S(1)}, u32[]{:S(2)}, u32[]{:S(2)}) async-start(bf16[16,4,1]{1,2,0:T(2,128)(2,1)} %broadcast_in_dim.10), calls=%async_computation.1 | async-start | bytes 16384 | tf_op jit(solution)/shard_map/all_to_all | solution.py:211
  1680.1 411.7 %copy-start.60 = (f32[464]{0:T(512)S(1)}, f32[464]{0:T(512)}, u32[]{:S(2)}) copy-start(f32[464]{0:T(512)} %param.47) | copy-start | bytes 5572
  1680.1 411.7 %copy-start.71 = (f32[464]{0:T(512)S(1)}, f32[464]{0:T(512)}, u32[]{:S(2)}) copy-start(f32[464]{0:T(512)} %param.49) | copy-start | bytes 5572
  1680.1 411.7 %copy-start.72 = (f32[464]{0:T(512)S(1)}, f32[464]{0:T(512)}, u32[]{:S(2)}) copy-start(f32[464]{0:T(512)} %param.48) | copy-start | bytes 5572
  1680.1 412.4 %copy-start.44 = (f32[32,512]{1,0:T(8,128)S(1)}, f32[32,512]{1,0:T(8,128)}, u32[]{:S(2)}) copy-start(f32[32,512]{1,0:T(8,128)} %param.44) | copy-start | bytes 196612
  1680.1 412.4 %copy-start.45 = (f32[32,512]{1,0:T(8,128)S(1)}, f32[32,512]{1,0:T(8,128)}, u32[]{:S(2)}) copy-start(f32[32,512]{1,0:T(8,128)} %reduce-scatter.17.cloned.1.call-done) | copy-start | bytes 196612
  2043.6 52.2 %copy-start.33 = (f32[1024,32]{0,1:T(8,128)S(1)}, f32[1024,32]{0,1:T(8,128)}, u32[]{:S(2)}) copy-start(f32[1024,32]{0,1:T(8,128)} %param.35) | copy-start | bytes 393220
  2043.6 52.2 %copy-start.34 = (f32[1024,32]{0,1:T(8,128)S(1)}, f32[1024,32]{0,1:T(8,128)}, u32[]{:S(2)}) copy-start(f32[1024,32]{0,1:T(8,128)} %reduce-scatter.11.cloned.1.call-done) | copy-start | bytes 393220
  2043.6 54.1 %copy-start.29 = (f32[32,3072]{1,0:T(8,128)S(1)}, f32[32,3072]{1,0:T(8,128)}, u32[]{:S(2)}) copy-start(f32[32,3072]{1,0:T(8,128)} %param.32) | copy-start | bytes 1179652
  2043.6 54.1 %copy-start.30 = (f32[32,3072]{1,0:T(8,128)S(1)}, f32[32,3072]{1,0:T(8,128)}, u32[]{:S(2)}) copy-start(f32[32,3072]{1,0:T(8,128)} %reduce-scatter.9.cloned.1.call-done) | copy-start | bytes 1179652
  2048.6 51.4 %copy-start.20 = (f32[32,4096]{1,0:T(8,128)S(1)}, f32[32,4096]{1,0:T(8,128)}, u32[]{:S(2)}) copy-start(f32[32,4096]{1,0:T(8,128)} %param.38) | copy-start | bytes 1572868
  2048.6 51.4 %copy-start.23 = (f32[32,4096]{1,0:T(8,128)S(1)}, f32[32,4096]{1,0:T(8,128)}, u32[]{:S(2)}) copy-start(f32[32,4096]{1,0:T(8,128)} %reduce-scatter.13.cloned.1.call-done) | copy-start | bytes 1572868
  2048.6 51.4 %copy-start.35 = (f32[32,4096]{1,0:T(8,128)S(1)}, f32[32,4096]{1,0:T(8,128)}, u32[]{:S(2)}) copy-start(f32[32,4096]{1,0:T(8,128)} %param.40) | copy-start | bytes 1572868
  2048.6 51.4 %copy-start.36 = (f32[32,4096]{1,0:T(8,128)S(1)}, f32[32,4096]{1,0:T(8,128)}, u32[]{:S(2)}) copy-start(f32[32,4096]{1,0:T(8,128)} %param.39) | copy-start | bytes 1572868
  (64 other events, 850.3 us)
Sparse Core Ops, SparseCore 0:
  11.7 56.5 all-gather.16
  71.7 125.7 all-gather.6
  201.0 94.0 all-gather.8
  298.4 55.0 all-gather.10
  356.8 76.3 all-gather.12
  436.5 76.1 all-gather.14
  686.4 183.5 reduce-scatter.6
  872.2 146.0 reduce-scatter.10
  1020.5 138.9 reduce-scatter.16
  1166.4 152.4 reduce-scatter.8
  1321.2 356.4 reduce-scatter.12
  1679.8 360.0 reduce-scatter.14
where the time goes:
time: 2120 us; the launch traced here: 2110 us
  waiting for transfers between devices  1240 us (58%)
  blocking collectives  306 us (14%)
  matrix products  265 us (12%)
  local copies, waits for them, and re-layouts  156 us (7%)
  other arithmetic  76.3 us (4%)
  starting transfers between devices  45.9 us (2%)
  between operations  22.2 us (1%)
    reduce_scatter x1, waiting for transfers between devices, local(): lax.psum_scatter(down_grad, ('grp', 'dp'), scatter_dimension=1, tiled=True)  360 us
    reduce_scatter x1, waiting for transfers between devices, local(): lax.psum_scatter(up_grad, ('grp', 'dp'), scatter_dimension=0, tiled=True)  355 us
    psum x1, blocking collectives, local(): lax.psum((jnp.sum(pixel_rows, axis=(0, 2)), jnp.sum(pixel_rows * pixel_ro...  184 us
    reduce_scatter x1, waiting for transfers between devices, local(): lax.psum_scatter(qkv_grad, ('grp', 'dp'), scatter_dimension=0, tiled=True)  158 us
    all_to_all x1, waiting for transfers between devices, local(): lax.all_to_all(quarters, 'dp', split_axis=0, concat_axis=1, tiled=True)  135 us
    reduce_scatter x1, waiting for transfers between devices, local(): lax.psum_scatter(dec_grad, ('grp', 'dp'), scatter_dimension=0, tiled=True)  131 us
    unnamed x2, blocking collectives  79.9 us
    dot_general x6, matrix products, forward_product(): return jnp.dot(left, right, preferred_element_type=jnp.float32)  78.2 us
  transfers between devices with their start and end apart: 15, of which 10 were waited for; matrix products, arithmetic and copies ran while one was open for 15% of the time, Pallas kernels for 0%

commit v1 on v0

v1 whole, which is shorter than its diff:
```python
import jax
import jax.numpy as jnp
import ml_dtypes
import numpy as np
from jax import lax
from jax.experimental import pallas as pl
from jax.experimental.pallas import tpu as pltpu
from jax.sharding import PartitionSpec as P

D = 1024
FF = 4096
HEADS = 16
HDIM = 64
DDEC = 512
PATCH = 16
SIDE = 14
BANDS = 3
STEP = 10
PIX = 768
GRID = 196
VIS = 49
QUART = 49
NSCALE = 4
AXES = ("grp", "dp")
BF = jnp.bfloat16
F32 = jnp.float32

EPS_NORM = 1e-05
BETA_ONE = 0.9
BETA_TWO = 0.95
ADAM_EPS = 1e-08
LR_MATRIX = 0.08
LR_VECTOR = 0.3
DECAY_MATRIX = 0.05
CLIP_LEVEL = 1.0


def forward_product(left, right):
    return jnp.dot(left, right, preferred_element_type=F32)


def back_product(left, right):
    return lax.dot_general(left, right, (((1,), (1,)), ((), ())), preferred_element_type=F32)


def weight_product(left, right):
    return lax.dot_general(left, right, (((0,), (0,)), ((), ())), preferred_element_type=F32)


def angle_pieces(channels, pieces):
    quarter = channels // 4
    step = np.float32(-np.log(np.float32(10000.0))) / np.float32(quarter)
    frequency = np.exp(np.arange(quarter, dtype=np.float32) * step)
    ratio = np.float32(2.0) ** (np.arange(NSCALE, dtype=np.float32) - 1)
    spot = np.arange(SIDE, dtype=np.float32)
    angle = (ratio[:, None] * spot[None, :]).reshape(-1, 1) * frequency[None, :]
    half = np.concatenate([np.sin(angle.astype(np.float64)), np.cos(angle.astype(np.float64))], 1)
    zeros = np.zeros_like(half)
    rest = np.concatenate(
        [np.concatenate([half, zeros], 1), np.concatenate([zeros, half], 1)], 0
    ).astype(np.float32)
    cut = []
    for _ in range(pieces):
        part = rest.astype(ml_dtypes.bfloat16)
        cut.append(part)
        rest = rest - part.astype(np.float32)
    return jnp.asarray(np.concatenate(cut, 0))


def angle_hot(spots, scale_rows, pieces):
    row_at = scale_rows * SIDE + spots // SIDE
    col_at = (NSCALE + scale_rows) * SIDE + spots % SIDE
    slot = jnp.arange(2 * NSCALE * SIDE)[None, :]
    hot = ((slot == row_at[:, None]) | (slot == col_at[:, None])).astype(BF)
    return jnp.concatenate([hot] * pieces, axis=1)


def split_vectors(vector_all):
    pieces = tuple((vector_all[number * D : (number + 1) * D] for number in range(10)))
    return (pieces, vector_all[10 * D : 10 * D + FF], vector_all[10 * D + FF :])


def norm_forward(hidden_in, norm_gain, norm_shift):
    center = hidden_in - jnp.mean(hidden_in, axis=-1, keepdims=True)
    inv_std = lax.rsqrt(jnp.mean(center * center, axis=-1, keepdims=True) + EPS_NORM)
    normed = center * inv_std
    return (normed * norm_gain + norm_shift, normed, inv_std)


def norm_backward(grad_out, normed, inv_std, norm_gain):
    scaled = grad_out * norm_gain
    inner = (
        scaled
        - jnp.mean(scaled, axis=-1, keepdims=True)
        - normed * jnp.mean(scaled * normed, axis=-1, keepdims=True)
    )
    return (inner * inv_std, jnp.sum(grad_out * normed, axis=0), jnp.sum(grad_out, axis=0))


def gelu_slope(preact):
    return (
        0.5 * (1.0 + lax.erf(preact * 0.7071067811865476))
        + preact * jnp.exp(-0.5 * preact * preact) * 0.3989422804014327
    )


def adamw_update(weight, moment_one, moment_two, gradient, step_rate, decay_rate):
    new_one = BETA_ONE * moment_one + (1.0 - BETA_ONE) * gradient
    new_two = BETA_TWO * moment_two + (1.0 - BETA_TWO) * gradient * gradient
    fixed_one = new_one / (1.0 - BETA_ONE**STEP)
    fixed_two = new_two / (1.0 - BETA_TWO**STEP)
    new_weight = weight - step_rate * (
        fixed_one / (jnp.sqrt(fixed_two) + ADAM_EPS) + decay_rate * weight
    )
    return (new_one, new_two, new_weight)


def core_pairs():
    return [(0, 1), (1, 0)]


def dp_pairs(bits):
    return [(i, i ^ bits) for i in range(16)]


def turn_pairs(core_zero, core_one):
    return [(g * 16 + i, g * 16 + (i ^ (core_one if g else core_zero))) for g in range(2) for i in range(16)]


def tiny_sum(value, routed):
    if not routed:
        return lax.psum(value, AXES)
    for bits in (1, 2, 4, 8):
        value = value + lax.ppermute(value, "dp", dp_pairs(bits))
    return value + lax.ppermute(value, "grp", core_pairs())


def take(array, index):
    return lax.dynamic_slice_in_dim(array, index, 1, axis=array.ndim - 3)


def summed_shard(left, right, extra, routed):
    columns = right.shape[1]
    if not routed:
        full = weight_product(left, right)
        if extra is not None:
            full = full + extra(0, D)
        half = lax.psum_scatter(full.astype(BF), "grp", scatter_dimension=0, tiled=True)
        return lax.psum_scatter(half, "dp", scatter_dimension=0, tiled=True).astype(F32)
    core = lax.axis_index("grp")
    chip = lax.axis_index("dp")
    x, y, z = chip % 2, (chip // 2) % 2, chip // 4
    half = D // 2

    def product(at):
        part = weight_product(lax.dynamic_slice_in_dim(left, at, half, axis=1), right)
        return part if extra is None else part + extra(at, half)

    away = product((1 - core) * half).astype(BF)
    came = lax.ppermute(away, "grp", core_pairs())
    held = (product(core * half) + came.astype(F32)).astype(BF)
    held = held.reshape(4, 4, 32, columns)
    first = core == 0
    mine, other = jnp.where(first, x, y), jnp.where(first, 1 - x, 1 - y)
    stride, span = jnp.where(first, 1, 2), jnp.where(first, 2, 1)
    away = jnp.concatenate([take(held, other * stride), take(held, other * stride + span)], axis=1)
    kept = jnp.concatenate([take(held, mine * stride), take(held, mine * stride + span)], axis=1)
    came = lax.ppermute(away, AXES, turn_pairs(1, 2))
    held = (kept.astype(F32) + came.astype(F32)).astype(BF)
    mine = jnp.where(first, y, x)
    came = lax.ppermute(take(held, 1 - mine), AXES, turn_pairs(2, 1))
    held = (take(held, mine).astype(F32) + came.astype(F32)).astype(BF).reshape(4, 32, columns)

    def row(index):
        return lax.dynamic_index_in_dim(held, index, axis=0, keepdims=False)

    came = [lax.ppermute(row(z ^ k), "dp", dp_pairs(4 * k)) for k in (1, 2, 3)]
    total = row(z).astype(F32)
    for part in came:
        total = total + part.astype(F32)
    return total


def local(
    pixels,
    visible,
    scale_index,
    cotangent,
    pe_weight,
    pe_first,
    pe_second,
    qkv_weight,
    qkv_first,
    qkv_second,
    out_weight,
    out_first,
    out_second,
    up_weight,
    up_first,
    up_second,
    down_weight,
    down_first,
    down_second,
    dec_weight,
    dec_first,
    dec_second,
    vectors,
    vec_first,
    vec_second,
):
    image_count = pixels.shape[0]
    row_count = image_count * VIS
    device_count = lax.axis_size(AXES)
    dp_count = lax.axis_size("dp")
    shard_rows = D // device_count
    routed = dp_count == 16 and device_count == 32
    item_count = 4 * image_count // dp_count
    whole_images = item_count % 4 == 0

    early = jnp.concatenate([pe_weight.T, qkv_weight], axis=1).astype(BF)
    late = jnp.concatenate([out_weight.T, up_weight, down_weight.T, dec_weight], axis=1).astype(BF)
    early_full = lax.all_gather(early, AXES, axis=0, tiled=True)
    late_full = lax.all_gather(late, AXES, axis=0, tiled=True)
    pe_full, qkv_full = early_full[:, :PIX], early_full[:, PIX:]
    out_full = late_full[:, :D]
    up_full = late_full[:, D : D + FF]
    down_full = late_full[:, D + FF : D + 2 * FF]
    dec_full = late_full[:, D + 2 * FF :]

    pixel_rows = pixels.astype(F32).reshape(row_count, BANDS, PATCH * PATCH)
    band_sum = jnp.sum(pixel_rows, axis=(0, 2))
    band_square = jnp.sum(pixel_rows * pixel_rows, axis=(0, 2))
    stats = tiny_sum(jnp.concatenate([band_sum, band_square]), routed)
    vector_all = lax.all_gather(vectors.astype(BF), AXES, axis=0, tiled=True)
    entry_count = row_count * device_count * PATCH * PATCH
    band_mean = stats[:BANDS] / entry_count
    band_scale = lax.rsqrt(stats[BANDS:] / entry_count - band_mean * band_mean + EPS_NORM)
    pixel_norm = (pixel_rows - band_mean[None, :, None]) * band_scale[None, :, None]
    pixel_low = pixel_norm.reshape(row_count, PIX).astype(BF)
    pieces, up_bias, dec_bias = split_vectors(vector_all.astype(F32))
    (
        gain_one,
        shift_one,
        gain_two,
        shift_two,
        pe_bias,
        query_bias,
        value_bias,
        out_bias,
        down_bias,
        mask_token,
    ) = pieces

    dp_index = lax.axis_index("dp")
    marks = jnp.concatenate([visible, scale_index[:, None]], axis=1)
    if whole_images:
        marks_in = lax.all_to_all(marks, "dp", split_axis=0, concat_axis=0, tiled=True)
        sent_images = image_count // dp_count
        image_order = marks_in.reshape(dp_count, sent_images, VIS + 1)
        visible_in, scale_in = image_order[:, :, :VIS], image_order[:, :, VIS]
        grids = cotangent[0].reshape(sent_images, 4, dp_count, QUART, DDEC)
        hot_in = (
            visible_in[..., None] == jnp.arange(GRID).reshape(1, 1, 1, GRID)
        ).astype(BF)
        hot_quarter = hot_in.reshape(dp_count, sent_images, VIS, 4, QUART)
        dy_sent = jnp.einsum(
            "skvqr,kqsrc->skvc", hot_quarter, grids, preferred_element_type=F32
        ).astype(BF)
        dy_rows = lax.all_to_all(
            dy_sent.reshape(image_count, VIS, DDEC), "dp", split_axis=0, concat_axis=0, tiled=True
        ).reshape(dp_count, sent_images, VIS, DDEC)
        dy_rows = dy_rows.reshape(row_count, DDEC)
        vacant_in = 1.0 - jnp.sum(hot_quarter.astype(F32), axis=2)
        dy_all = jnp.sum(cotangent[0].astype(F32), axis=(0, 1, 2))
        dy_vacant = jnp.einsum(
            "skqr,kqsrc->c", vacant_in.astype(BF), grids, preferred_element_type=F32
        )

    spots = visible.reshape(row_count)
    scale_rows = jnp.repeat(scale_index, VIS)
    enc_table = forward_product(angle_hot(spots, scale_rows, 3), angle_pieces(D, 3))
    stream_in = back_product(pixel_low, pe_full) + pe_bias + enc_table
    norm_out_one, normed_one, inv_std_one = norm_forward(stream_in, gain_one, shift_one)
    norm_one = norm_out_one.astype(BF)
    projected = forward_product(norm_one, qkv_full) + jnp.concatenate(
        [query_bias, jnp.zeros_like(query_bias), value_bias]
    )
    projected = projected.astype(BF).reshape(image_count, VIS, 3, HEADS, HDIM)
    queries = projected[:, :, 0]
    keys_head = projected[:, :, 1]
    values_head = projected[:, :, 2]
    scale_score = HDIM ** (-0.5)
    raw_scores = (
        jnp.einsum("nqhd,nkhd->nhqk", queries, keys_head, preferred_element_type=F32)
        * scale_score
    )
    score_peak = jnp.max(raw_scores, axis=-1, keepdims=True)
    log_total = score_peak + jnp.log(
        jnp.sum(jnp.exp(raw_scores - score_peak), axis=-1, keepdims=True)
    )
    softmaxed = jnp.exp(raw_scores - log_total)
    mixture = jnp.einsum(
        "nhqk,nkhd->nqhd", softmaxed.astype(BF), values_head, preferred_element_type=F32
    )
    mixture_low = mixture.reshape(row_count, D).astype(BF)
    stream_mid = stream_in + back_product(mixture_low, out_full) + out_bias
    norm_out_two, normed_two, inv_std_two = norm_forward(stream_mid, gain_two, shift_two)
    norm_two = norm_out_two.astype(BF)
    preact = forward_product(norm_two, up_full) + up_bias
    activated = jax.nn.gelu(preact, approximate=False).astype(BF)
    stream_out = stream_mid + back_product(activated, down_full) + down_bias
    stream_low = stream_out.astype(BF)

    if whole_images:
        dec_pieces = angle_pieces(DDEC, 2)
        vis_table = forward_product(angle_hot(spots, scale_rows, 2), dec_pieces)
        vis_rows = (forward_product(stream_low, dec_full) + dec_bias + vis_table).astype(BF)
        vis_in = lax.all_to_all(
            vis_rows.reshape(image_count, VIS, DDEC), "dp", split_axis=0, concat_axis=0, tiled=True
        ).reshape(dp_count, sent_images, VIS, DDEC)
        placed = jnp.einsum(
            "skvqr,skvc->kqsrc", hot_quarter, vis_in, preferred_element_type=F32
        )
        position = jnp.arange(GRID)
        every_hot = angle_hot(
            jnp.tile(position, dp_count * sent_images),
            jnp.repeat(scale_in.reshape(-1), GRID),
            2,
        ).reshape(dp_count, sent_images, 4, QUART, -1)
        every_table = jnp.einsum(
            "skqrt,tc->kqsrc", every_hot, dec_pieces, preferred_element_type=F32
        )
        mask_rows = forward_product(jnp.broadcast_to(mask_token.astype(BF), (8, D)), dec_full)[0]
        empty = vacant_in.transpose(1, 2, 0, 3)[..., None] > 0.5
        decoded = jnp.where(empty, every_table + (mask_rows + dec_bias), placed)
        decoded = decoded.astype(BF).reshape(1, item_count, dp_count, QUART, DDEC)
        out_grad_rows = back_product(dy_rows, dec_full).astype(BF).astype(F32)
        dec_bias_grad = dy_all
        vacant_parts = []
        rest = dy_vacant
        for _ in range(3):
            part = lax.reduce_precision(rest, 8, 7)
            vacant_parts.append(part)
            rest = rest - part
        vacant_low = jnp.stack(vacant_parts).astype(BF)
        mask_grad = jnp.sum(back_product(vacant_low, dec_full), axis=0)

        def dec_extra(at, count):
            token = lax.dynamic_slice_in_dim(mask_token, at, count)
            return token[:, None] * dy_vacant[None, :]

        dec_left, dec_right = stream_low, dy_rows
    else:
        dec_extra = None
        placement = visible[:, :, None] == jnp.arange(GRID)[None, None, :]
        placement_low = placement.astype(BF)
        vacant = 1.0 - jnp.sum(placement.astype(F32), axis=1)
        full_grid = jnp.einsum(
            "nvg,nvd->ngd",
            placement_low,
            stream_low.reshape(image_count, VIS, D),
            preferred_element_type=F32,
        )
        full_grid = (full_grid + vacant[:, :, None] * mask_token).astype(BF)
        quarters = full_grid.reshape(4 * image_count, 1, QUART, D)
        ratio_image = jnp.power(2.0, scale_index.astype(F32) - 1.0)
        ratio_quarter = jnp.repeat(ratio_image, 4).reshape(4 * image_count, 1).astype(BF)
        received = lax.all_to_all(quarters, "dp", split_axis=0, concat_axis=1, tiled=True)
        received_ratio = lax.all_to_all(
            ratio_quarter, "dp", split_axis=0, concat_axis=1, tiled=True
        )
        quarter_id = dp_index * item_count + jnp.arange(item_count)
        position = (quarter_id % 4)[:, None] * QUART + jnp.arange(QUART)[None, :]
        scale_at = jnp.round(jnp.log2(received_ratio.astype(F32))).astype(jnp.int32) + 1
        full = (item_count, dp_count, QUART)
        dec_table = forward_product(
            angle_hot(
                jnp.broadcast_to(position[:, None, :], full).reshape(-1),
                jnp.broadcast_to(scale_at[:, :, None], full).reshape(-1),
                2,
            ),
            angle_pieces(DDEC, 2),
        ).reshape(full + (DDEC,))
        dec_rows = jnp.dot(received, dec_full, preferred_element_type=F32)
        decoded = (dec_rows + dec_bias + dec_table).astype(BF)[None]
        grad_rows = cotangent[0].reshape(-1, DDEC)
        dec_left, dec_right = received.reshape(-1, D), grad_rows
        dec_bias_grad = jnp.sum(grad_rows.astype(F32), axis=0)
        grid_grad = (
            back_product(grad_rows, dec_full).astype(BF).reshape(item_count, dp_count, QUART, D)
        )
        returned = lax.all_to_all(
            grid_grad, "dp", split_axis=1, concat_axis=0, tiled=True
        ).reshape(image_count, GRID, D)
        out_grad_rows = jnp.einsum(
            "nvg,ngd->nvd", placement_low, returned, preferred_element_type=F32
        ).reshape(row_count, D)
        mask_grad = jnp.einsum(
            "ng,ngd->d", vacant.astype(BF), returned, preferred_element_type=F32
        )

    dec_shard = summed_shard(dec_left, dec_right, dec_extra, routed)
    out_rows_low = out_grad_rows.astype(BF)
    down_shard = summed_shard(out_rows_low, activated, None, routed)
    down_bias_grad = jnp.sum(out_grad_rows, axis=0)
    preact_grad = forward_product(out_rows_low, down_full) * gelu_slope(preact)
    up_bias_grad = jnp.sum(preact_grad, axis=0)
    preact_low = preact_grad.astype(BF)
    up_shard = summed_shard(norm_two, preact_low, None, routed)
    two_grad = back_product(preact_low, up_full)
    mid_grad, gain_two_grad, shift_two_grad = norm_backward(
        two_grad, normed_two, inv_std_two, gain_two
    )
    mid_grad = mid_grad + out_grad_rows
    mid_low = mid_grad.astype(BF)
    out_shard = summed_shard(mid_low, mixture_low, None, routed)
    out_bias_grad = jnp.sum(mid_grad, axis=0)
    mixture_grad = (
        forward_product(mid_low, out_full).astype(BF).reshape(image_count, VIS, HEADS, HDIM)
    )
    again_scores = (
        jnp.einsum("nqhd,nkhd->nhqk", queries, keys_head, preferred_element_type=F32)
        * scale_score
    )
    again_probs = jnp.exp(again_scores - log_total)
    value_grad = jnp.einsum(
        "nhqk,nqhd->nkhd", again_probs.astype(BF), mixture_grad, preferred_element_type=F32
    )
    probs_grad = jnp.einsum(
        "nqhd,nkhd->nhqk", mixture_grad, values_head, preferred_element_type=F32
    )
    score_low = (
        again_probs
        * (probs_grad - jnp.sum(probs_grad * again_probs, axis=-1, keepdims=True))
        * scale_score
    ).astype(BF)
    query_grad = jnp.einsum(
        "nhqk,nkhd->nqhd", score_low, keys_head, preferred_element_type=F32
    )
    key_grad = jnp.einsum("nhqk,nqhd->nkhd", score_low, queries, preferred_element_type=F32)
    projected_grad = jnp.stack([query_grad, key_grad, value_grad], axis=2).reshape(row_count, 3 * D)
    query_bias_grad = jnp.sum(projected_grad[:, :D], axis=0)
    value_bias_grad = jnp.sum(projected_grad[:, 2 * D :], axis=0)
    projected_low = projected_grad.astype(BF)
    qkv_shard = summed_shard(norm_one, projected_low, None, routed)
    one_grad = back_product(projected_low, qkv_full)
    in_grad, gain_one_grad, shift_one_grad = norm_backward(
        one_grad, normed_one, inv_std_one, gain_one
    )
    in_grad = in_grad + mid_grad
    pe_bias_grad = jnp.sum(in_grad, axis=0)
    in_low = in_grad.astype(BF)
    pe_shard = summed_shard(in_low, pixel_low, None, routed)
    norm_grad = forward_product(in_low, pe_full).reshape(row_count, BANDS, PATCH * PATCH)
    pixel_grad = (norm_grad * band_scale[None, :, None]).reshape(image_count, VIS, PIX)
    vec_grad = jnp.concatenate(
        [
            gain_one_grad,
            shift_one_grad,
            gain_two_grad,
            shift_two_grad,
            pe_bias_grad,
            query_bias_grad,
            value_bias_grad,
            out_bias_grad,
            down_bias_grad,
            mask_grad,
            up_bias_grad,
            dec_bias_grad,
        ]
    )
    if routed:
        vec_length = vectors.shape[0]
        vec_half = dp_count * vec_length
        core = lax.axis_index("grp")
        away = lax.dynamic_slice_in_dim(vec_grad, (1 - core) * vec_half, vec_half)
        kept = lax.dynamic_slice_in_dim(vec_grad, core * vec_half, vec_half)
        kept = kept + lax.ppermute(away, "grp", core_pairs())
        vec_shard = jnp.sum(
            lax.all_to_all(
                kept.reshape(dp_count, vec_length), "dp", split_axis=0, concat_axis=0, tiled=True
            ),
            axis=0,
        )
    else:
        vec_shard = lax.psum_scatter(vec_grad, AXES, scatter_dimension=0, tiled=True)
    shards = (pe_shard, qkv_shard, out_shard, up_shard, down_shard, dec_shard, vec_shard)
    local_squares = sum((jnp.sum(gradient * gradient) for gradient in shards))
    squares = tiny_sum(local_squares.reshape(1), routed)[0]
    grad_norm = jnp.sqrt(squares)
    clip_factor = jnp.minimum(1.0, CLIP_LEVEL / grad_norm)
    params = (pe_weight, qkv_weight, out_weight, up_weight, down_weight, dec_weight, vectors)
    firsts = (pe_first, qkv_first, out_first, up_first, down_first, dec_first, vec_first)
    seconds = (pe_second, qkv_second, out_second, up_second, down_second, dec_second, vec_second)
    results = []
    for number in range(7):
        step_rate = LR_VECTOR if number == 6 else LR_MATRIX
        decay_rate = 0.0 if number == 6 else DECAY_MATRIX
        gradient = shards[number].T if number in (0, 2, 4) else shards[number]
        results.extend(
            adamw_update(
                params[number],
                firsts[number],
                seconds[number],
                gradient * clip_factor,
                step_rate,
                decay_rate,
            )
        )
    return (decoded, pixel_grad, *results, grad_norm)


def solution(mesh):
    rows = P(AXES, None)
    cols = P(None, AXES)
    vecs = P(AXES)
    images = P(AXES, None, None)
    grids = P("grp", "dp", None, None, None)
    states = (cols,) * 3 + (rows,) * 3 + (cols,) * 3 + (rows,) * 3 + (cols,) * 3 + (rows,) * 3
    states = states + (vecs,) * 3
    return jax.shard_map(
        local,
        mesh=mesh,
        in_specs=(images, rows, vecs, grids) + states,
        out_specs=(grids, images) + states + (P(),),
        check_vma=False,
    )
```

time: 2120 us -> 747 us (0.35)
  waiting for transfers between devices: 1240 us -> 181 us
  blocking collectives: 306 us -> 40.2 us
  local copies, waits for them, and re-layouts: 156 us -> 97.5 us
  starting transfers between devices: 45.9 us -> 76 us
    reduce_scatter x6 -> x0, waiting for transfers between devices: 1010 us -> none  [the longest x1 360 us: local(): lax.psum_scatter(down_grad, ('grp', 'dp'), scatter_dimension=1, tiled=True)]
    psum x2 -> x0, blocking collectives: 226 us -> none  [the longest x1 184 us: local(): lax.psum((jnp.sum(pixel_rows, axis=(0, 2)), jnp.sum(pixel_rows * pixel_ro...]
    ppermute x0 -> x47, waiting for transfers between devices: none -> 125 us  [the longest x6 55.4 us: summed_shard(): came = lax.ppermute(away, AXES, turn_pairs(1, 2))]
    all_to_all x3 -> x4, waiting for transfers between devices: 141 us -> 20.4 us  [the longest x1 18.4 us: local(): lax.all_to_all(dy_sent.reshape(image_count, VIS, DDEC), 'dp', split_axis=...]
    all_gather x6 -> x2, waiting for transfers between devices: 93.3 us -> 35.7 us  [the longest x1 35.7 us: local(): late_full = lax.all_gather(late, AXES, axis=0, tiled=True)]
    ppermute x0 -> x47, starting transfers between devices: none -> 53.7 us  [the longest x18 23.5 us: summed_shard(): came = [lax.ppermute(row(z ^ k), 'dp', dp_pairs(4 * k)) for k in (1, 2, 3)]]
    reshape x11 -> x5, local copies, waits for them, and re-layouts: 65.3 us -> 24.3 us  [the longest x1 12.8 us: local(): projected = projected.astype(BF).reshape(image_count, VIS, 3, HEADS, HDIM)]
    unnamed x2 -> x1, blocking collectives: 79.9 us -> 40.2 us
  transfers between devices with their start and end apart: 15 -> 53, of which waited for: 10 -> 26; matrix products, arithmetic and copies ran while one was open for 15% -> 25% of each run, Pallas kernels for 0% -> 0%
where the time goes in v1:
time: 747 us; the launch traced here: 737 us
  matrix products  246 us (33%)
  waiting for transfers between devices  181 us (24%)
  local copies, waits for them, and re-layouts  97.5 us (13%)
  starting transfers between devices  76 us (10%)
  other arithmetic  70.3 us (9%)
  blocking collectives  40.2 us (5%)
  between operations  25.5 us (3%)
    dot_general x12, matrix products, forward_product(): return jnp.dot(left, right, preferred_element_type=F32)  78.2 us
    ppermute x6, waiting for transfers between devices, summed_shard(): came = lax.ppermute(away, AXES, turn_pairs(1, 2))  55.4 us
    dot_general x12, matrix products, weight_product(): lax.dot_general(left, right, (((0,), (0,)), ((), ())), preferred_element_...  52.6 us
    dot_general x7, matrix products, back_product(): lax.dot_general(left, right, (((1,), (1,)), ((), ())), preferred_element_...  43.5 us
    unnamed x1, blocking collectives  40.2 us
    all_gather x1, waiting for transfers between devices, local(): late_full = lax.all_gather(late, AXES, axis=0, tiled=True)  35.7 us
    ppermute x6, waiting for transfers between devices, summed_shard(): came = lax.ppermute(take(held, 1 - mine), AXES, turn_pairs(2, 1))  33.7 us
    ppermute x18, starting transfers between devices, summed_shard(): came = [lax.ppermute(row(z ^ k), 'dp', dp_pairs(4 * k)) for k in (1, 2, 3)]  23.5 us
  transfers between devices with their start and end apart: 53, of which 26 were waited for; matrix products, arithmetic and copies ran while one was open for 25% of the time, Pallas kernels for 0%

profile of v1, /device:TPU:0, one launch (start us, length us, event | category | flops | bytes accessed | tf_op | source)
XLA Modules:
  0.0 737.0 jit_solution(6766839431040500307)
XLA Ops:
  15.7 8.3 %all-to-all-start = ((s32[16,1,50]{2,1,0:T(1,128)}), s32[16,1,50]{2,1,0:T(1,128)S(1)}, u32[]{:S(2)}, u32[]{:S(2)}) async-start(s32[16,1,50]{2,1,0:T(1,128)} %bitcast.1), calls=%async_computation | async-start | bytes 16384 | tf_op jit(solution)/shard_map/all_to_all | solution.py:257
  26.9 40.2 %all-reduce = bf16[14848]{0:T(1024)(128)(2,1)S(1)} all-reduce(bf16[14848]{0:T(1024)(128)(2,1)S(1)} %dynamic-update-slice), channel_id=1, replica_groups=mesh['grp'=2,'dp'=16] {'grp','dp'}, use_global_device_ids=true, to_apply=%add | all-reduce | flops 14848 | bytes 59392
  99.2 6.9 bitcast_convert_fusion
  106.1 6.4 all-to-all-start.2
  123.6 18.4 %all-to-all-done.2 = bf16[16,49,512]{2,1,0:T(8,128)(2,1)S(1)} async-done(((bf16[16,49,512]{2,1,0:T(8,128)(2,1)}), bf16[16,49,512]{2,1,0:T(8,128)(2,1)S(1)}, u32[]{:S(2)}, u32[]{:S(2)}) %all-to-all-start.2) | async-done | bytes 802848 | tf_op jit(solution)/shard_map/all_to_all | solution.py:269
  150.4 6.9 add_convert_fusion
  157.2 12.8 %reshape.480 = bf16[16,49,3,16,64]{4,3,2,1,0:T(8,128)(2,1)} reshape(bf16[784,3072]{1,0:T(8,128)(2,1)} %add_convert_fusion) | data formatting | bytes 9633792 | tf_op jit(solution)/shard_map/reshape | solution.py:288
  170.0 7.3 fusion.233
  196.7 35.7 %all-gather.3.cloned.1.call-done = bf16[1024,9728]{1,0:T(8,128)(2,1)} async-done(((bf16[32,9728]{1,0:T(8,128)(2,1)}), bf16[1024,9728]{1,0:T(8,128)(2,1)}) %all-gather.3.cloned.1.call-update) | async-done | bytes 19922960 | tf_op jit(solution)/shard_map/all_gather | solution.py:223
  242.9 36.2 %fusion.3 = (bf16[784,4096]{1,0:T(8,128)(2,1)}, f32[784,4096]{1,0:T(8,128)}) fusion(f32[4096]{0:T(1024)S(1)} %slice.139, bf16[784,1024]{1,0:T(8,128)(2,1)S(1)} %add_convert_fusion.7, bf16[1024,9728]{1,0:T(8,128)(2,1)S(1)} %copy-done.60), kind=kOutput, calls=%fused_computation.6 | convolution fusion | flops 6788612096 | bytes 29278208 | tf_op jit(solution)/shard_map/dot_general | solution.py:39
  279.1 13.9 %fusion.238 = (f32[4096]{0:T(1024)S(1)}, bf16[784,4096]{1,0:T(8,128)(2,1)S(1)}) fusion(f32[784,4096]{1,0:T(8,128)} %get-tuple-element.271, f32[4096]{0:T(1024)S(1)} %slice.139, bf16[784,1024]{1,0:T(8,128)(2,1)S(1)} %convolution_convert_fusion.3, bf16[1024,9728]{1,0:T(8,128)(2,1)} %all-gather.3.cloned.1.call-done), kind=kOutput, calls=%fused_computation.402 | convolution fusion | flops 6615199744 | bytes 29294592 | tf_op jit(solution)/shard_map/dot_general | solution.py:39
  293.0 12.5 %multiply_reduce_fusion.2 = (f32[1024]{0:T(1024)S(1)}, f32[784]{0:T(1024)S(1)}, f32[784]{0:T(1024)S(1)}, f32[1024]{0:T(1024)S(1)}, f32[784,1024]{1,0:T(8,128)S(1)}) fusion(f32[784,1024]{1,0:T(8,128)S(1)} %copy-done.8, f32[784]{0:T(1024)S(1)} %copy-done.83, f32[784]{0:T(1024)S(1)} %copy-done.73, f32[1024]{0:T(1024)S(1)} %copy-done.77, ...), kind=kOutput, calls=%fused_computation.85 | convolution fusion | flops 6583889920 | bytes 21258496 | tf_op jit(solution)/shard_map/dot_general | solution.py:43
  322.4 8.4 %fusion.54 = f32[16,16,49,49]{2,3,1,0:T(8,128)} fusion(bf16[16,49,1,16,64]{4,3,2,1,0:T(8,128)(2,1)} %copy-done.3, bf16[16,49,16,64]{3,2,1,0:T(8,128)(2,1)} %reshape.483), kind=kOutput, calls=%fused_computation.77 | convolution fusion | flops 78675968 | bytes 5669888 | tf_op jit(solution)/shard_map/nqhd,nkhd->nhqk/dot_general | solution.py:429
  335.9 16.9 %fusion.62 = f32[16,49,1,16,64]{4,1,3,0,2:T(8,128)} fusion(f32[16,16,49,49]{2,3,1,0:T(8,128)} %fusion.54, f32[16,16,49,49]{2,3,1,0:T(8,128)} %copy-done, f32[16,16,49]{2,1,0:T(8,128)S(1)} %copy-done.48, bf16[16,49,1,16,64]{4,3,2,1,0:T(8,128)(2,1)} %copy-done.12), kind=kOutput, calls=%fused_computation.100 | convolution fusion | flops 84220464 | bytes 9784320 | tf_op jit(solution)/shard_map/nhqk,nkhd->nqhd/dot_general | solution.py:437
  352.9 16.6 %fusion.65 = f32[16,49,1,16,64]{4,1,3,0,2:T(8,128)} fusion(f32[16,16,49,49]{2,3,1,0:T(8,128)} %fusion.54, f32[16,16,49,49]{2,3,1,0:T(8,128)} %copy-done, f32[16,16,49]{2,1,0:T(8,128)S(1)} %copy-done.48, bf16[16,49,1,16,64]{4,3,2,1,0:T(8,128)(2,1)S(1)} %copy-done.11), kind=kOutput, calls=%fused_computation.101 | convolution fusion | flops 84220464 | bytes 9784320 | tf_op jit(solution)/shard_map/nhqk,nqhd->nkhd/dot_general | solution.py:440
  369.4 8.5 %pad_maximum_fusion = f32[16,49,3,16,64]{4,1,3,0,2:T(8,128)S(1)} fusion(f32[16,49,1,16,64]{4,1,3,0,2:T(8,128)} %fusion.59, f32[16,49,1,16,64]{4,1,3,0,2:T(8,128)} %fusion.65, f32[16,49,1,16,64]{4,1,3,0,2:T(8,128)} %fusion.62), kind=kLoop, calls=%fused_computation.1 | loop fusion | flops 4816896 | bytes 19267584 | tf_op jit(solution)/shard_map/stack | solution.py:441
  378.0 7.7 %copy.124 = f32[16,49,3,16,64]{4,3,2,1,0:T(8,128)} copy(f32[16,49,3,16,64]{4,1,3,0,2:T(8,128)S(1)} %pad_maximum_fusion) | data formatting | bytes 19267584 | tf_op jit(solution)/shard_map/stack | solution.py:441
  385.7 16.2 %reshape.484 = f32[784,3072]{1,0:T(8,128)} reshape(f32[16,49,3,16,64]{4,3,2,1,0:T(8,128)} %copy.124) | data formatting | bytes 19267584 | tf_op jit(solution)/shard_map/reshape | solution.py:441
  405.4 9.4 %convolution_convert_fusion.2 = bf16[512,3072]{1,0:T(8,128)(2,1)} fusion(bf16[784,1024]{1,0:T(8,128)(2,1)S(1)} %copy-done.25, s32[]{:T(128)S(6)} %select_n.249, f32[784,3072]{1,0:T(8,128)} %reshape.484), kind=kOutput, calls=%fused_computation.57 | convolution fusion | flops 2470232064 | bytes 13582340 | tf_op jit(solution)/shard_map/dot_general | solution.py:47
  414.9 6.4 convolution_convert_fusion.1
  421.3 6.3 convolution_convert_fusion
  427.6 9.3 %add_convert_fusion.6 = bf16[784,1024]{1,0:T(8,128)(2,1)S(1)} fusion(f32[784,1024]{1,0:T(8,128)S(1)} %copy-done.9, bf16[784,4096]{1,0:T(8,128)(2,1)S(1)} %bitcast.221, bf16[1024,9728]{1,0:T(8,128)(2,1)} %all-gather.3.cloned.1.call-done, f32[1024]{0:T(1024)S(1)} %copy-done.96), kind=kOutput, calls=%fused_computation.90 | convolution fusion | flops 6579077120 | bytes 19632128 | tf_op jit(solution)/shard_map/dot_general | solution.py:43
  445.3 11.4 %multiply_reduce_fusion.3 = (f32[1024]{0:T(1024)S(1)}, f32[784]{0:T(1024)S(1)}, f32[784]{0:T(1024)S(1)}, f32[1024]{0:T(1024)S(1)}, f32[784,1024]{1,0:T(8,128)S(1)}) fusion(f32[784,1024]{1,0:T(8,128)S(1)} %copy-done.2, f32[784]{0:T(1024)S(1)} %copy-done.81, f32[784]{0:T(1024)S(1)} %copy-done.71, f32[1024]{0:T(1024)S(1)} %copy-done.75, ...), kind=kOutput, calls=%fused_computation.86 | convolution fusion | flops 4942131200 | bytes 22372608 | tf_op jit(solution)/shard_map/dot_general | solution.py:43
  499.3 8.5 %collective-permute-done.6 = bf16[4,2,32,768]{3,2,1,0:T(8,128)(2,1)S(1)} collective-permute-done((bf16[4,2,32,768]{3,2,1,0:T(8,128)(2,1)S(1)}, bf16[4,2,32,768]{3,2,1,0:T(8,128)(2,1)S(1)}, u32[]{:S(2)}, u32[]{:S(2)}) %collective-permute-start.6) | collective-permute-done | bytes 393248 | tf_op jit(solution)/shard_map/ppermute | solution.py:168
  509.6 7.5 %collective-permute-done.7 = bf16[4,1,32,768]{3,2,1,0:T(8,128)(2,1)S(1)} collective-permute-done((bf16[4,1,32,768]{3,2,1,0:T(8,128)(2,1)S(1)}, bf16[4,1,32,768]{3,2,1,0:T(8,128)(2,1)S(1)}, u32[]{:S(2)}, u32[]{:S(2)}) %collective-permute-start.7) | collective-permute-done | bytes 196640 | tf_op jit(solution)/shard_map/ppermute | solution.py:171
  555.0 7.1 add_convert_fusion.1
  572.0 7.0 collective-permute-done.12
  593.8 9.0 %collective-permute-done.13 = bf16[4,1,32,3072]{3,2,1,0:T(8,128)(2,1)} collective-permute-done((bf16[4,1,32,3072]{3,2,1,0:T(8,128)(2,1)}, bf16[4,1,32,3072]{3,2,1,0:T(8,128)(2,1)}, u32[]{:S(2)}, u32[]{:S(2)}) %collective-permute-start.13) | collective-permute-done | bytes 786464 | tf_op jit(solution)/shard_map/ppermute | solution.py:171
  607.7 6.4 collective-permute-done.24
  616.7 33.5 %collective-permute-done.30 = bf16[4,2,32,4096]{3,2,1,0:T(8,128)(2,1)S(1)} collective-permute-done((bf16[4,2,32,4096]{3,2,1,0:T(8,128)(2,1)S(1)}, bf16[4,2,32,4096]{3,2,1,0:T(8,128)(2,1)S(1)}, u32[]{:S(2)}, u32[]{:S(2)}) %collective-permute-start.30) | collective-permute-done | bytes 2097184 | tf_op jit(solution)/shard_map/ppermute | solution.py:168
  652.5 13.5 %collective-permute-done.31 = bf16[4,1,32,4096]{3,2,1,0:T(8,128)(2,1)S(1)} collective-permute-done((bf16[4,1,32,4096]{3,2,1,0:T(8,128)(2,1)S(1)}, bf16[4,1,32,4096]{3,2,1,0:T(8,128)(2,1)S(1)}, u32[]{:S(2)}, u32[]{:S(2)}) %collective-permute-start.31) | collective-permute-done | bytes 1048608 | tf_op jit(solution)/shard_map/ppermute | solution.py:171
  676.6 10.5 %collective-permute-done.27 = bf16[32,4096]{1,0:T(8,128)(2,1)} collective-permute-done((bf16[32,4096]{1,0:T(8,128)(2,1)S(1)}, bf16[32,4096]{1,0:T(8,128)(2,1)}, u32[]{:S(2)}, u32[]{:S(2)}) %collective-permute-start.27) | collective-permute-done | bytes 262176 | tf_op jit(solution)/shard_map/ppermute | solution.py:177
  (529 shorter events, 285.9 us)
Async XLA Ops:
  7.2 135.9 %all-gather.5.cloned.1.call-start = ((), (), s32[]{:S(2)}) async-start(), calls=%async_computation.5 | async-start | bytes 8110080 | tf_op jit(solution)/shard_map/all_gather | solution.py:222
  10.0 222.4 %all-gather.3.cloned.1.call-start = ((), (), s32[]{:S(2)}) async-start(), calls=%async_computation.4 | async-start | bytes 20545536 | tf_op jit(solution)/shard_map/all_gather | solution.py:223
  15.7 82.4 %all-to-all-start = ((s32[16,1,50]{2,1,0:T(1,128)}), s32[16,1,50]{2,1,0:T(1,128)S(1)}, u32[]{:S(2)}, u32[]{:S(2)}) async-start(s32[16,1,50]{2,1,0:T(1,128)} %bitcast.1), calls=%async_computation | async-start | bytes 16384 | tf_op jit(solution)/shard_map/all_to_all | solution.py:257
  24.7 58.8 %collective-permute-start = (f32[6]{0:T(128)S(1)}, f32[6]{0:T(128)S(1)}, u32[]{:S(2)}, u32[]{:S(2)}) collective-permute-start(f32[6]{0:T(128)S(1)} %pad_maximum_fusion.10), channel_id=1, source_target_pairs={{0,1},{1,0},{2,3},{3,2},{4,5},{5,4},{6,7},{7,6},{8,9},{9,8},{10,11... | collective-permute-start | bytes 80 | tf_op jit(solution)/shard_map/ppermute | solution.py:134
  106.1 35.9 %all-to-all-start.2 = ((bf16[16,49,512]{2,1,0:T(8,128)(2,1)}), bf16[16,49,512]{2,1,0:T(8,128)(2,1)S(1)}, u32[]{:S(2)}, u32[]{:S(2)}) async-start(bf16[16,49,512]{2,1,0:T(8,128)(2,1)} %bitcast_convert_fusion), calls=%async_computation.2 | async-start | bytes 1835008 | tf_op jit(solution)/shard_map/all_to_all | solution.py:269
  438.5 39.5 %collective-permute-start.35 = (bf16[512,512]{1,0:T(8,128)(2,1)}, bf16[512,512]{1,0:T(8,128)(2,1)}, u32[]{:S(2)}, u32[]{:S(2)}) collective-permute-start(bf16[512,512]{1,0:T(8,128)(2,1)} %fusion.91), channel_id=1, source_target_pairs={{0,16},{16,0},{1,17},{17,1},{2,18},{18,2},{3,19},{19,3},{4,20},{20... | collective-permute-start | bytes 1572872 | tf_op jit(solution)/shard_map/ppermute | solution.py:160
  444.8 50.3 %collective-permute-start.17 = (bf16[512,1024]{1,0:T(8,128)(2,1)}, bf16[512,1024]{1,0:T(8,128)(2,1)}, u32[]{:S(2)}, u32[]{:S(2)}) collective-permute-start(bf16[512,1024]{1,0:T(8,128)(2,1)} %convolution_convert_fusion.4), channel_id=1, source_target_pairs={{0,16},{16,0},{1,17},{17,1},{2,18},{18,2},{3,19},{19,3},{4,20},{20... | collective-permute-start | bytes 3145736 | tf_op jit(solution)/shard_map/ppermute | solution.py:160
  445.2 99.5 %collective-permute-start.11 = (bf16[512,3072]{1,0:T(8,128)(2,1)}, bf16[512,3072]{1,0:T(8,128)(2,1)}, u32[]{:S(2)}, u32[]{:S(2)}) collective-permute-start(bf16[512,3072]{1,0:T(8,128)(2,1)} %convolution_convert_fusion.2), channel_id=1, source_target_pairs={{0,16},{16,0},{1,17},{17,1},{2,18},{18,2},{3,19},{19,3},{4,20},{20... | collective-permute-start | bytes 9437192 | tf_op jit(solution)/shard_map/ppermute | solution.py:160
  473.0 17.2 %collective-permute-start.5 = (bf16[512,768]{1,0:T(8,128)(2,1)}, bf16[512,768]{1,0:T(8,128)(2,1)}, u32[]{:S(2)}, u32[]{:S(2)}) collective-permute-start(bf16[512,768]{1,0:T(8,128)(2,1)} %convolution_convert_fusion.5), channel_id=1, source_target_pairs={{0,16},{16,0},{1,17},{17,1},{2,18},{18,2},{3,19},{19,3},{4,20},{20... | collective-permute-start | bytes 2359304 | tf_op jit(solution)/shard_map/ppermute | solution.py:160
  473.1 80.8 %collective-permute-start.29 = (bf16[512,4096]{1,0:T(8,128)(2,1)}, bf16[512,4096]{1,0:T(8,128)(2,1)}, u32[]{:S(2)}, u32[]{:S(2)}) collective-permute-start(bf16[512,4096]{1,0:T(8,128)(2,1)} %convolution_convert_fusion), channel_id=1, source_target_pairs={{0,16},{16,0},{1,17},{17,1},{2,18},{18,2},{3,19},{19,3},{4,20},{20... | collective-permute-start | bytes 12582920 | tf_op jit(solution)/shard_map/ppermute | solution.py:160
  485.5 96.4 %all-to-all-start.1 = ((bf16[16,49,512]{2,1,0:T(8,128)(2,1)}), bf16[16,49,512]{2,1,0:T(8,128)(2,1)S(1)}, u32[]{:S(2)}, u32[]{:S(2)}) async-start(bf16[16,49,512]{2,1,0:T(8,128)(2,1)} %reshape.481), calls=%async_computation.1 | async-start | bytes 1835008 | tf_op jit(solution)/shard_map/all_to_all | solution.py:318
  490.1 72.1 %collective-permute-start.23 = (bf16[512,4096]{1,0:T(8,128)(2,1)}, bf16[512,4096]{1,0:T(8,128)(2,1)S(1)}, u32[]{:S(2)}, u32[]{:S(2)}) collective-permute-start(bf16[512,4096]{1,0:T(8,128)(2,1)} %convolution_convert_fusion.1), channel_id=1, source_target_pairs={{0,16},{16,0},{1,17},{17,1},{2,18},{18,2},{3,19},{19,3},{4,20},{20... | collective-permute-start | bytes 12582920 | tf_op jit(solution)/shard_map/ppermute | solution.py:160
  490.2 19.2 %collective-permute-start.37 = (bf16[4,1,32,512]{3,2,1,0:T(8,128)(2,1)S(1)}, bf16[4,1,32,512]{3,2,1,0:T(8,128)(2,1)S(1)}, u32[]{:S(2)}, u32[]{:S(2)}) collective-permute-start(bf16[4,1,32,512]{3,2,1,0:T(8,128)(2,1)S(1)} %constant_dynamic-slice_fusion), channel_id=1, source_target_pairs={{0,2},{1,3},{2,0},{3,1},{4,6},{5,7},{6,4},{7,5},{8,10},{9,11},{10,... | collective-permute-start | bytes 393224 | tf_op jit(solution)/shard_map/ppermute | solution.py:171
  495.1 12.7 %collective-permute-start.6 = (bf16[4,2,32,768]{3,2,1,0:T(8,128)(2,1)S(1)}, bf16[4,2,32,768]{3,2,1,0:T(8,128)(2,1)S(1)}, u32[]{:S(2)}, u32[]{:S(2)}) collective-permute-start(bf16[4,2,32,768]{3,2,1,0:T(8,128)(2,1)S(1)} %pad_maximum_fusion.6), channel_id=1, source_target_pairs={{0,1},{1,0},{2,3},{3,2},{4,5},{5,4},{6,7},{7,6},{8,9},{9,8},{10,11... | collective-permute-start | bytes 1179656 | tf_op jit(solution)/shard_map/ppermute | solution.py:168
  507.8 16.5 %collective-permute-start.18 = (bf16[4,2,32,1024]{3,2,1,0:T(8,128)(2,1)S(1)}, bf16[4,2,32,1024]{3,2,1,0:T(8,128)(2,1)S(1)}, u32[]{:S(2)}, u32[]{:S(2)}) collective-permute-start(bf16[4,2,32,1024]{3,2,1,0:T(8,128)(2,1)S(1)} %pad_maximum_fusion.5), channel_id=1, source_target_pairs={{0,1},{1,0},{2,3},{3,2},{4,5},{5,4},{6,7},{7,6},{8,9},{9,8},{10,11... | collective-permute-start | bytes 1572872 | tf_op jit(solution)/shard_map/ppermute | solution.py:168
  543.5 46.8 %collective-permute-start.20 = (bf16[32,1024]{1,0:T(8,128)(2,1)}, bf16[32,1024]{1,0:T(8,128)(2,1)}, u32[]{:S(2)}, u32[]{:S(2)}) collective-permute-start(bf16[32,1024]{1,0:T(8,128)(2,1)} %get-tuple-element.232), channel_id=1, source_target_pairs={{0,4},{1,5},{2,6},{3,7},{4,0},{5,1},{6,2},{7,3},{8,12},{9,13},{10,... | collective-permute-start | bytes 196616 | tf_op jit(solution)/shard_map/ppermute | solution.py:177
  543.5 46.8 %collective-permute-start.22 = (bf16[32,1024]{1,0:T(8,128)(2,1)}, bf16[32,1024]{1,0:T(8,128)(2,1)}, u32[]{:S(2)}, u32[]{:S(2)}) collective-permute-start(bf16[32,1024]{1,0:T(8,128)(2,1)} %get-tuple-element.233), channel_id=1, source_target_pairs={{0,12},{1,13},{2,14},{3,15},{4,8},{5,9},{6,10},{7,11},{8,4},{9,5},... | collective-permute-start | bytes 196616 | tf_op jit(solution)/shard_map/ppermute | solution.py:177
  544.7 45.7 %collective-permute-start.21 = (bf16[32,1024]{1,0:T(8,128)(2,1)}, bf16[32,1024]{1,0:T(8,128)(2,1)}, u32[]{:S(2)}, u32[]{:S(2)}) collective-permute-start(bf16[32,1024]{1,0:T(8,128)(2,1)} %get-tuple-element.234), channel_id=1, source_target_pairs={{0,8},{1,9},{2,10},{3,11},{4,12},{5,13},{6,14},{7,15},{8,0},{9,1},... | collective-permute-start | bytes 196616 | tf_op jit(solution)/shard_map/ppermute | solution.py:177
  553.9 25.1 %collective-permute-start.12 = (bf16[4,2,32,3072]{3,2,1,0:T(8,128)(2,1)S(1)}, bf16[4,2,32,3072]{3,2,1,0:T(8,128)(2,1)}, u32[]{:S(2)}, u32[]{:S(2)}) collective-permute-start(bf16[4,2,32,3072]{3,2,1,0:T(8,128)(2,1)S(1)} %pad_maximum_fusion.3), channel_id=1, source_target_pairs={{0,1},{1,0},{2,3},{3,2},{4,5},{5,4},{6,7},{7,6},{8,9},{9,8},{10,11... | collective-permute-start | bytes 4718600 | tf_op jit(solution)/shard_map/ppermute | solution.py:168
  571.1 43.0 %collective-permute-start.24 = (bf16[4,2,32,4096]{3,2,1,0:T(8,128)(2,1)}, bf16[4,2,32,4096]{3,2,1,0:T(8,128)(2,1)}, u32[]{:S(2)}, u32[]{:S(2)}) collective-permute-start(bf16[4,2,32,4096]{3,2,1,0:T(8,128)(2,1)} %pad_maximum_fusion.1), channel_id=1, source_target_pairs={{0,1},{1,0},{2,3},{3,2},{4,5},{5,4},{6,7},{7,6},{8,9},{9,8},{10,11... | collective-permute-start | bytes 6291464 | tf_op jit(solution)/shard_map/ppermute | solution.py:168
  582.0 20.8 %collective-permute-start.13 = (bf16[4,1,32,3072]{3,2,1,0:T(8,128)(2,1)}, bf16[4,1,32,3072]{3,2,1,0:T(8,128)(2,1)}, u32[]{:S(2)}, u32[]{:S(2)}) collective-permute-start(bf16[4,1,32,3072]{3,2,1,0:T(8,128)(2,1)} %constant_dynamic-slice_fusion.20), channel_id=1, source_target_pairs={{0,2},{1,3},{2,0},{3,1},{4,6},{5,7},{6,4},{7,5},{8,10},{9,11},{10,... | collective-permute-start | bytes 2359304 | tf_op jit(solution)/shard_map/ppermute | solution.py:171
  592.8 57.4 %collective-permute-start.30 = (bf16[4,2,32,4096]{3,2,1,0:T(8,128)(2,1)S(1)}, bf16[4,2,32,4096]{3,2,1,0:T(8,128)(2,1)S(1)}, u32[]{:S(2)}, u32[]{:S(2)}) collective-permute-start(bf16[4,2,32,4096]{3,2,1,0:T(8,128)(2,1)S(1)} %pad_maximum_fusion.2), channel_id=1, source_target_pairs={{0,1},{1,0},{2,3},{3,2},{4,5},{5,4},{6,7},{7,6},{8,9},{9,8},{10,11... | collective-permute-start | bytes 6291464 | tf_op jit(solution)/shard_map/ppermute | solution.py:168
  604.1 63.3 %collective-permute-start.14 = (bf16[32,3072]{1,0:T(8,128)(2,1)S(1)}, bf16[32,3072]{1,0:T(8,128)(2,1)S(1)}, u32[]{:S(2)}, u32[]{:S(2)}) collective-permute-start(bf16[32,3072]{1,0:T(8,128)(2,1)S(1)} %get-tuple-element.221), channel_id=1, source_target_pairs={{0,4},{1,5},{2,6},{3,7},{4,0},{5,1},{6,2},{7,3},{8,12},{9,13},{10,... | collective-permute-start | bytes 589832 | tf_op jit(solution)/shard_map/ppermute | solution.py:177
  604.9 64.7 %collective-permute-start.16 = (bf16[32,3072]{1,0:T(8,128)(2,1)S(1)}, bf16[32,3072]{1,0:T(8,128)(2,1)S(1)}, u32[]{:S(2)}, u32[]{:S(2)}) collective-permute-start(bf16[32,3072]{1,0:T(8,128)(2,1)S(1)} %get-tuple-element.222), channel_id=1, source_target_pairs={{0,12},{1,13},{2,14},{3,15},{4,8},{5,9},{6,10},{7,11},{8,4},{9,5},... | collective-permute-start | bytes 589832 | tf_op jit(solution)/shard_map/ppermute | solution.py:177
  604.9 66.7 %collective-permute-start.15 = (bf16[32,3072]{1,0:T(8,128)(2,1)S(1)}, bf16[32,3072]{1,0:T(8,128)(2,1)S(1)}, u32[]{:S(2)}, u32[]{:S(2)}) collective-permute-start(bf16[32,3072]{1,0:T(8,128)(2,1)S(1)} %get-tuple-element.223), channel_id=1, source_target_pairs={{0,8},{1,9},{2,10},{3,11},{4,12},{5,13},{6,14},{7,15},{8,0},{9,1},... | collective-permute-start | bytes 589832 | tf_op jit(solution)/shard_map/ppermute | solution.py:177
  616.6 34.5 %collective-permute-start.25 = (bf16[4,1,32,4096]{3,2,1,0:T(8,128)(2,1)S(1)}, bf16[4,1,32,4096]{3,2,1,0:T(8,128)(2,1)S(1)}, u32[]{:S(2)}, u32[]{:S(2)}) collective-permute-start(bf16[4,1,32,4096]{3,2,1,0:T(8,128)(2,1)S(1)} %constant_dynamic-slice_fusion.10), channel_id=1, source_target_pairs={{0,2},{1,3},{2,0},{3,1},{4,6},{5,7},{6,4},{7,5},{8,10},{9,11},{10,... | collective-permute-start | bytes 3145736 | tf_op jit(solution)/shard_map/ppermute | solution.py:171
  651.1 14.9 %collective-permute-start.31 = (bf16[4,1,32,4096]{3,2,1,0:T(8,128)(2,1)S(1)}, bf16[4,1,32,4096]{3,2,1,0:T(8,128)(2,1)S(1)}, u32[]{:S(2)}, u32[]{:S(2)}) collective-permute-start(bf16[4,1,32,4096]{3,2,1,0:T(8,128)(2,1)S(1)} %constant_dynamic-slice_fusion.5), channel_id=1, source_target_pairs={{0,2},{1,3},{2,0},{3,1},{4,6},{5,7},{6,4},{7,5},{8,10},{9,11},{10,... | collective-permute-start | bytes 3145736 | tf_op jit(solution)/shard_map/ppermute | solution.py:171
  651.5 21.2 %collective-permute-start.26 = (bf16[32,4096]{1,0:T(8,128)(2,1)S(1)}, bf16[32,4096]{1,0:T(8,128)(2,1)S(1)}, u32[]{:S(2)}, u32[]{:S(2)}) collective-permute-start(bf16[32,4096]{1,0:T(8,128)(2,1)S(1)} %get-tuple-element.214), channel_id=1, source_target_pairs={{0,4},{1,5},{2,6},{3,7},{4,0},{5,1},{6,2},{7,3},{8,12},{9,13},{10,... | collective-permute-start | bytes 786440 | tf_op jit(solution)/shard_map/ppermute | solution.py:177
  667.4 19.7 %collective-permute-start.27 = (bf16[32,4096]{1,0:T(8,128)(2,1)S(1)}, bf16[32,4096]{1,0:T(8,128)(2,1)}, u32[]{:S(2)}, u32[]{:S(2)}) collective-permute-start(bf16[32,4096]{1,0:T(8,128)(2,1)S(1)} %get-tuple-element.216), channel_id=1, source_target_pairs={{0,8},{1,9},{2,10},{3,11},{4,12},{5,13},{6,14},{7,15},{8,0},{9,1},... | collective-permute-start | bytes 786440 | tf_op jit(solution)/shard_map/ppermute | solution.py:177
  669.6 20.1 %collective-permute-start.32 = (bf16[32,4096]{1,0:T(8,128)(2,1)}, bf16[32,4096]{1,0:T(8,128)(2,1)}, u32[]{:S(2)}, u32[]{:S(2)}) collective-permute-start(bf16[32,4096]{1,0:T(8,128)(2,1)} %get-tuple-element.211), channel_id=1, source_target_pairs={{0,4},{1,5},{2,6},{3,7},{4,0},{5,1},{6,2},{7,3},{8,12},{9,13},{10,... | collective-permute-start | bytes 786440 | tf_op jit(solution)/shard_map/ppermute | solution.py:177
  671.6 18.1 %collective-permute-start.34 = (bf16[32,4096]{1,0:T(8,128)(2,1)}, bf16[32,4096]{1,0:T(8,128)(2,1)}, u32[]{:S(2)}, u32[]{:S(2)}) collective-permute-start(bf16[32,4096]{1,0:T(8,128)(2,1)} %get-tuple-element.212), channel_id=1, source_target_pairs={{0,12},{1,13},{2,14},{3,15},{4,8},{5,9},{6,10},{7,11},{8,4},{9,5},... | collective-permute-start | bytes 786440 | tf_op jit(solution)/shard_map/ppermute | solution.py:177
  672.8 20.0 %collective-permute-start.33 = (bf16[32,4096]{1,0:T(8,128)(2,1)}, bf16[32,4096]{1,0:T(8,128)(2,1)}, u32[]{:S(2)}, u32[]{:S(2)}) collective-permute-start(bf16[32,4096]{1,0:T(8,128)(2,1)} %get-tuple-element.213), channel_id=1, source_target_pairs={{0,8},{1,9},{2,10},{3,11},{4,12},{5,13},{6,14},{7,15},{8,0},{9,1},... | collective-permute-start | bytes 786440 | tf_op jit(solution)/shard_map/ppermute | solution.py:177
  (141 other events, 2037.4 us)
Sparse Core Ops, SparseCore 0:
  11.5 78.7 all-gather.4
  93.2 139.2 all-gather.2

commit v2 on v1

v2 whole, which is shorter than its diff:
```python
import jax
import jax.numpy as jnp
import ml_dtypes
import numpy as np
from jax import lax
from jax.experimental import pallas as pl
from jax.experimental.pallas import tpu as pltpu
from jax.sharding import PartitionSpec as P

D = 1024
FF = 4096
HEADS = 16
HDIM = 64
DDEC = 512
PATCH = 16
SIDE = 14
BANDS = 3
STEP = 10
PIX = 768
GRID = 196
VIS = 49
QUART = 49
NSCALE = 4
AXES = ("grp", "dp")
BF = jnp.bfloat16
F32 = jnp.float32

EPS_NORM = 1e-05
BETA_ONE = 0.9
BETA_TWO = 0.95
ADAM_EPS = 1e-08
LR_MATRIX = 0.08
LR_VECTOR = 0.3
DECAY_MATRIX = 0.05
CLIP_LEVEL = 1.0


def forward_product(left, right):
    return jnp.dot(left, right, preferred_element_type=F32)


def back_product(left, right):
    return lax.dot_general(left, right, (((1,), (1,)), ((), ())), preferred_element_type=F32)


def weight_product(left, right):
    return lax.dot_general(left, right, (((0,), (0,)), ((), ())), preferred_element_type=F32)


def angle_pieces(channels, pieces):
    quarter = channels // 4
    step = np.float32(-np.log(np.float32(10000.0))) / np.float32(quarter)
    frequency = np.exp(np.arange(quarter, dtype=np.float32) * step)
    ratio = np.float32(2.0) ** (np.arange(NSCALE, dtype=np.float32) - 1)
    spot = np.arange(SIDE, dtype=np.float32)
    angle = (ratio[:, None] * spot[None, :]).reshape(-1, 1) * frequency[None, :]
    half = np.concatenate([np.sin(angle.astype(np.float64)), np.cos(angle.astype(np.float64))], 1)
    zeros = np.zeros_like(half)
    rest = np.concatenate(
        [np.concatenate([half, zeros], 1), np.concatenate([zeros, half], 1)], 0
    ).astype(np.float32)
    cut = []
    for _ in range(pieces):
        part = rest.astype(ml_dtypes.bfloat16)
        cut.append(part)
        rest = rest - part.astype(np.float32)
    return jnp.asarray(np.concatenate(cut, 0))


def angle_hot(spots, scale_rows, pieces):
    row_at = scale_rows * SIDE + spots // SIDE
    col_at = (NSCALE + scale_rows) * SIDE + spots % SIDE
    slot = jnp.arange(2 * NSCALE * SIDE)[None, :]
    hot = ((slot == row_at[:, None]) | (slot == col_at[:, None])).astype(BF)
    return jnp.concatenate([hot] * pieces, axis=1)


def split_vectors(vector_all):
    pieces = tuple((vector_all[number * D : (number + 1) * D] for number in range(10)))
    return (pieces, vector_all[10 * D : 10 * D + FF], vector_all[10 * D + FF :])


def norm_forward(hidden_in, norm_gain, norm_shift):
    center = hidden_in - jnp.mean(hidden_in, axis=-1, keepdims=True)
    inv_std = lax.rsqrt(jnp.mean(center * center, axis=-1, keepdims=True) + EPS_NORM)
    normed = center * inv_std
    return (normed * norm_gain + norm_shift, normed, inv_std)


def norm_backward(grad_out, normed, inv_std, norm_gain):
    scaled = grad_out * norm_gain
    inner = (
        scaled
        - jnp.mean(scaled, axis=-1, keepdims=True)
        - normed * jnp.mean(scaled * normed, axis=-1, keepdims=True)
    )
    return (inner * inv_std, jnp.sum(grad_out * normed, axis=0), jnp.sum(grad_out, axis=0))


def adamw_update(weight, moment_one, moment_two, gradient, step_rate, decay_rate):
    new_one = BETA_ONE * moment_one + (1.0 - BETA_ONE) * gradient
    new_two = BETA_TWO * moment_two + (1.0 - BETA_TWO) * gradient * gradient
    fixed_one = new_one / (1.0 - BETA_ONE**STEP)
    fixed_two = new_two / (1.0 - BETA_TWO**STEP)
    new_weight = weight - step_rate * (
        fixed_one / (jnp.sqrt(fixed_two) + ADAM_EPS) + decay_rate * weight
    )
    return (new_one, new_two, new_weight)


def core_pairs():
    return [(0, 1), (1, 0)]


def dp_pairs(bits):
    return [(i, i ^ bits) for i in range(16)]


def turn_pairs(core_zero, core_one):
    return [(g * 16 + i, g * 16 + (i ^ (core_one if g else core_zero))) for g in range(2) for i in range(16)]


def tiny_sum(value, routed):
    if not routed:
        return lax.psum(value, AXES)
    for bits in (1, 2, 4, 8):
        value = value + lax.ppermute(value, "dp", dp_pairs(bits))
    return value + lax.ppermute(value, "grp", core_pairs())


def tie(*values):
    return lax.optimization_barrier(values)


def take(array, index):
    return lax.dynamic_slice_in_dim(array, index, 1, axis=array.ndim - 3)


def spot_of_chip():
    chip = lax.axis_index("dp")
    return lax.axis_index("grp"), chip % 2, (chip // 2) % 2, chip // 4


class Gathering:
    def __init__(self, shard, direct):
        self.shard, self.direct = shard, direct
        self.core, self.x, self.y, self.z = spot_of_chip()
        steps = (1, 2, 3) if direct else (1,)
        self.near = [lax.ppermute(shard, "dp", dp_pairs(4 * k)) for k in steps]

    def middle(self, after):
        shard, near = tie(self.shard, after)[0], self.near[0]
        even = self.z % 2 == 0
        self.held = jnp.stack([jnp.where(even, shard, near), jnp.where(even, near, shard)])
        self.near = lax.ppermute(self.held, "dp", dp_pairs(8))
        return self

    def first_turn(self, after):
        if self.direct:
            held = jnp.zeros((4,) + self.shard.shape, self.shard.dtype)
            for k, part in enumerate([self.shard] + self.near):
                held = lax.dynamic_update_slice(held, part[None], (self.z ^ k, 0, 0))
        else:
            held, near = self.held, self.near
            front = self.z < 2
            held = jnp.concatenate([jnp.where(front, held, near), jnp.where(front, near, held)])
        self.held = tie(held, after)[0]
        self.near = lax.ppermute(self.held, AXES, turn_pairs(2, 1))
        return self

    def second_turn(self, after):
        mine = jnp.where(self.core == 0, self.y, self.x) == 0
        held, near = tie(self.held, after)[0], self.near
        self.held = jnp.stack([jnp.where(mine, held, near), jnp.where(mine, near, held)])
        self.near = lax.ppermute(self.held, AXES, turn_pairs(1, 2))
        return self

    def cores(self, after):
        blocks = []
        self.held = tie(self.held, after)[0]
        first = self.core == 0
        for at_y in range(2):
            for at_x in range(2):
                if_first = jnp.where(self.x == at_x, self.held[at_y], self.near[at_y])
                if_second = jnp.where(self.y == at_y, self.held[at_x], self.near[at_x])
                blocks.append(jnp.where(first, if_first, if_second))
        self.held = jnp.stack(blocks, axis=1).reshape(D // 2, self.shard.shape[1])
        self.near = lax.ppermute(self.held, "grp", core_pairs())
        return self

    def total(self):
        first = self.core == 0
        return jnp.concatenate(
            [jnp.where(first, self.held, self.near), jnp.where(first, self.near, self.held)]
        )


class Reduction:
    def __init__(self, product, routed):
        self.product, self.routed = product, routed
        self.core, self.x, self.y, self.z = spot_of_chip()
        self.away = self.kept = None

    def cores(self, after):
        if self.routed:
            half = D // 2
            self.away = self.product((1 - self.core) * half, half, after).astype(BF)
            self.came = lax.ppermute(self.away, "grp", core_pairs())
        return self

    def first_turn(self, after):
        if not self.routed:
            return self
        half = D // 2
        own = self.product(self.core * half, half, after)
        held = (own + self.came.astype(F32)).astype(BF)
        columns = held.shape[1]
        held = held.reshape(4, 4, 32, columns)
        first = self.core == 0
        mine = jnp.where(first, self.x, self.y)
        stride, span = jnp.where(first, 1, 2), jnp.where(first, 2, 1)
        other = 1 - mine
        self.away = jnp.concatenate(
            [take(held, other * stride), take(held, other * stride + span)], axis=1
        )
        self.kept = jnp.concatenate(
            [take(held, mine * stride), take(held, mine * stride + span)], axis=1
        )
        self.came = lax.ppermute(self.away, AXES, turn_pairs(1, 2))
        return self

    def second_turn(self, after):
        if not self.routed:
            return self
        kept, _ = tie(self.kept, after)
        held = (kept.astype(F32) + self.came.astype(F32)).astype(BF)
        mine = jnp.where(self.core == 0, self.y, self.x)
        self.away, self.kept = take(held, 1 - mine), take(held, mine)
        self.came = lax.ppermute(self.away, AXES, turn_pairs(2, 1))
        return self

    def along_z(self, after):
        if not self.routed:
            return self
        kept, _ = tie(self.kept, after)
        held = (kept.astype(F32) + self.came.astype(F32)).astype(BF)
        held = held.reshape(4, 32, held.shape[-1])

        def row(index):
            return lax.dynamic_index_in_dim(held, index, axis=0, keepdims=False)

        self.kept = row(self.z)
        self.away = [row(self.z ^ k) for k in (1, 2, 3)]
        self.came = [lax.ppermute(self.away[k - 1], "dp", dp_pairs(4 * k)) for k in (1, 2, 3)]
        return self

    def second_turn_with(self, other, after):
        if not self.routed:
            mine, theirs = self.product, other.product
            self.product = lambda *at: jnp.concatenate([mine(*at), theirs(*at)], axis=1)
            return self
        self.came = jnp.concatenate([self.came, other.came], axis=-1)
        self.kept = jnp.concatenate([self.kept, other.kept], axis=-1)
        return self.second_turn(after)

    def total(self, after=None):
        if not self.routed:
            half = lax.psum_scatter(
                self.product(0, D, None).astype(BF), "grp", scatter_dimension=0, tiled=True
            )
            return lax.psum_scatter(half, "dp", scatter_dimension=0, tiled=True).astype(F32)
        total = self.kept
        if after is not None:
            total, _ = tie(total, after)
        total = total.astype(F32)
        for part in self.came:
            total = total + part.astype(F32)
        self.kept = total
        return total

    def before(self, value):
        if not self.routed:
            return value
        value, self.kept, self.away = tie(value, self.kept, self.away)
        return value


def product_of(left, right):
    def product(at, count, after):
        held = left if after is None else tie(left, after)[0]
        return weight_product(lax.dynamic_slice_in_dim(held, at, count, axis=1), right)

    return product


SPAN = 128


def windows(rows):
    for pair in range(rows // (2 * VIS)):
        start = min(2 * VIS * pair // 16 * 16, rows - SPAN)
        yield start, 2 * VIS * pair - start


def same_image(offset):
    key = lax.broadcasted_iota(jnp.int32, (SPAN, SPAN), 0) - offset
    query = lax.broadcasted_iota(jnp.int32, (SPAN, SPAN), 1) - offset
    inside = (key >= 0) & (key < 2 * VIS)
    match = inside & (query >= 0) & (query < 2 * VIS) & ((key >= VIS) == (query >= VIS))
    weight = match.astype(F32)
    return jnp.concatenate([weight, weight], axis=1) > 0.5, inside


def head_lanes():
    lane = lax.broadcasted_iota(jnp.int32, (SPAN, SPAN), 1)
    low = (lane < HDIM).astype(F32)
    return low.astype(BF), (1.0 - low).astype(BF), lane < HDIM


def nt(left, right):
    return lax.dot_general(left, right, (((1,), (1,)), ((), ())), preferred_element_type=F32)


def tn(left, right):
    return lax.dot_general(left, right, (((0,), (0,)), ((), ())), preferred_element_type=F32)


SCALE = HDIM ** (-0.5)


def attend_kernel(q_ref, k_ref, v_ref, mix_ref, peak_ref):
    low, high, is_low = head_lanes()
    low, high = low * SCALE, high * SCALE
    for number, (start, offset) in enumerate(windows(mix_ref.shape[0])):
        rows = pl.ds(start, SPAN)
        match, inside = same_image(offset)
        q_win = q_ref[rows, :]
        q_two = jnp.concatenate([q_win * low, q_win * high], axis=0)
        scores = jnp.where(match, nt(k_ref[rows, :], q_two), -1e30)
        peak = jnp.max(scores, axis=0, keepdims=True)
        grown = jnp.exp(scores - peak)
        total = jnp.sum(grown, axis=0, keepdims=True)
        probs = (grown * (1.0 / total)).astype(BF)
        peak_ref[0, number : number + 1, :] = peak + jnp.log(total)
        both = tn(probs, v_ref[rows, :])
        mixed = jnp.where(is_low, both[:SPAN], both[SPAN:])
        held = mix_ref[rows, :].astype(F32)
        mix_ref[rows, :] = jnp.where(inside, mixed, held).astype(BF)


def attend(projected):
    rows = projected.shape[0]
    pairs = HEADS // 2
    count = rows // (2 * VIS)
    block = lambda shift: pl.BlockSpec((rows, SPAN), lambda i: (0, i + shift))
    return pl.pallas_call(
        attend_kernel,
        grid=(pairs,),
        in_specs=[block(0), block(pairs), block(2 * pairs)],
        out_specs=[block(0), pl.BlockSpec((1, count, 2 * SPAN), lambda i: (i, 0, 0))],
        out_shape=[
            jax.ShapeDtypeStruct((rows, D), BF),
            jax.ShapeDtypeStruct((pairs, count, 2 * SPAN), F32),
        ],
        compiler_params=pltpu.CompilerParams(vmem_limit_bytes=32 * 2**20),
        cost_estimate=pl.CostEstimate(
            flops=4 * rows * SPAN * D, bytes_accessed=8 * rows * D, transcendentals=rows * SPAN * HEADS
        ),
        name="attend",
    )(projected, projected, projected)


def attend_back_kernel(q_ref, k_ref, v_ref, mix_ref, peak_ref, grad_ref, sums_ref):
    at = pl.program_id(0) * SPAN
    low, high, is_low = head_lanes()
    q_sum = jnp.zeros((1, SPAN), F32)
    v_sum = jnp.zeros((1, SPAN), F32)

    def put(rows, shift, value, inside):
        cols = pl.ds(pl.multiple_of(at + shift * D, SPAN), SPAN)
        held = grad_ref[rows, cols].astype(F32)
        grad_ref[rows, cols] = jnp.where(inside, value, held).astype(BF)

    for number, (start, offset) in enumerate(windows(q_ref.shape[0])):
        rows = pl.ds(start, SPAN)
        match, inside = same_image(offset)
        q_win, k_win, v_win, mix_win = q_ref[rows, :], k_ref[rows, :], v_ref[rows, :], mix_ref[rows, :]
        q_win = q_win * SCALE
        q_two = jnp.concatenate([q_win * low, q_win * high], axis=0)
        mix_two = jnp.concatenate([mix_win * low, mix_win * high], axis=0)
        scores = nt(k_win, q_two) - peak_ref[0, number : number + 1, :]
        probs = jnp.exp(jnp.where(match, scores, -1e30))
        probs_low = probs.astype(BF)
        v_grad = jnp.dot(probs_low, mix_two, preferred_element_type=F32)
        probs_grad = nt(v_win, mix_two)
        inner = jnp.sum(probs_grad * probs, axis=0, keepdims=True)
        score = (probs * (probs_grad - inner)).astype(BF)
        k_grad = jnp.dot(score, q_two, preferred_element_type=F32)
        q_both = tn(score, k_win * SCALE)
        q_grad = jnp.where(is_low, q_both[:SPAN], q_both[SPAN:])
        put(rows, 0, q_grad, inside)
        put(rows, 1, k_grad, inside)
        put(rows, 2, v_grad, inside)
        q_sum += jnp.sum(jnp.where(inside, q_grad, 0.0), axis=0, keepdims=True)
        v_sum += jnp.sum(jnp.where(inside, v_grad, 0.0), axis=0, keepdims=True)
    sums_ref[...] = jnp.concatenate([q_sum, v_sum, jnp.zeros((6, SPAN), F32)], axis=0)


def attend_back(projected, mixture_grad, peaks):
    rows = projected.shape[0]
    pairs = HEADS // 2
    count = rows // (2 * VIS)
    block = lambda shift: pl.BlockSpec((rows, SPAN), lambda i: (0, i + shift))
    return pl.pallas_call(
        attend_back_kernel,
        grid=(pairs,),
        in_specs=[
            block(0),
            block(pairs),
            block(2 * pairs),
            block(0),
            pl.BlockSpec((1, count, 2 * SPAN), lambda i: (i, 0, 0)),
        ],
        out_specs=[
            pl.BlockSpec((rows, 3 * D), lambda i: (0, 0)),
            pl.BlockSpec((8, SPAN), lambda i: (0, i)),
        ],
        out_shape=[
            jax.ShapeDtypeStruct((rows, 3 * D), BF),
            jax.ShapeDtypeStruct((8, D), F32),
        ],
        compiler_params=pltpu.CompilerParams(vmem_limit_bytes=40 * 2**20),
        cost_estimate=pl.CostEstimate(
            flops=10 * rows * SPAN * D, bytes_accessed=14 * rows * D, transcendentals=rows * SPAN * HEADS
        ),
        name="attend_back",
    )(projected, projected, projected, mixture_grad, peaks)


TAIL_STEP = 0.33
TAIL = (
    0.18636611813641438,
    0.1828371164957563,
    0.20192458123233548,
    0.04500824941716716,
    0.41254593072161144,
    -0.3554434272669394,
    0.46269071975152953,
    -0.1359293701595944,
)


def gelu_and_slope(x):
    t = 1.0 / (1.0 + (TAIL_STEP * 0.7071067811865476) * jnp.abs(x))
    bell = jnp.exp(-0.5 * x * x)
    tail = jnp.full_like(x, 0.5 * TAIL[-1])
    for factor in TAIL[-2::-1]:
        tail = tail * t + 0.5 * factor
    tail = tail * t * bell
    normal = jnp.where(x >= 0.0, 1.0 - tail, tail)
    return x * normal, normal + x * bell * 0.3989422804014327


UP_TILE = 512


def expand_kernel(x_ref, w_ref, bias_ref, act_ref, slope_ref):
    preact = jnp.dot(x_ref[...], w_ref[...], preferred_element_type=F32) + bias_ref[...]
    activated, slope = gelu_and_slope(preact)
    act_ref[...] = activated.astype(BF)
    slope_ref[...] = slope.astype(slope_ref.dtype)


def expand(x, weight_all, first_column, bias):
    rows = x.shape[0]
    shift = first_column // UP_TILE
    tile = pl.BlockSpec((rows, UP_TILE), lambda i: (0, i))
    return pl.pallas_call(
        expand_kernel,
        grid=(FF // UP_TILE,),
        in_specs=[
            pl.BlockSpec((rows, D), lambda i: (0, 0)),
            pl.BlockSpec((D, UP_TILE), lambda i: (0, i + shift)),
            pl.BlockSpec((1, UP_TILE), lambda i: (0, i)),
        ],
        out_specs=[tile, tile],
        out_shape=[jax.ShapeDtypeStruct((rows, FF), BF), jax.ShapeDtypeStruct((rows, FF), BF)],
        compiler_params=pltpu.CompilerParams(vmem_limit_bytes=40 * 2**20),
        cost_estimate=pl.CostEstimate(
            flops=2 * rows * D * FF, bytes_accessed=2 * D * FF + 4 * rows * FF, transcendentals=2 * rows * FF
        ),
        name="expand",
    )(x, weight_all, bias.reshape(1, FF))


def local(
    pixels,
    visible,
    scale_index,
    cotangent,
    pe_weight,
    pe_first,
    pe_second,
    qkv_weight,
    qkv_first,
    qkv_second,
    out_weight,
    out_first,
    out_second,
    up_weight,
    up_first,
    up_second,
    down_weight,
    down_first,
    down_second,
    dec_weight,
    dec_first,
    dec_second,
    vectors,
    vec_first,
    vec_second,
):
    image_count = pixels.shape[0]
    row_count = image_count * VIS
    device_count = lax.axis_size(AXES)
    dp_count = lax.axis_size("dp")
    shard_rows = D // device_count
    routed = dp_count == 16 and device_count == 32
    item_count = 4 * image_count // dp_count
    whole_images = item_count % 4 == 0

    pixel_rows = pixels.astype(F32).reshape(row_count, BANDS, PATCH * PATCH)
    late = jnp.concatenate([up_weight, down_weight.T, out_weight.T, dec_weight], axis=1).astype(BF)
    late_full = lax.all_gather(late, AXES, axis=0, tiled=True)
    sent_images = max(image_count // dp_count, 1)
    if routed:
        vec_length = vectors.shape[0]
        vec_low = jnp.pad(vectors.astype(BF), (0, 4 * SPAN - vec_length)).reshape(4, SPAN)
        vec_low = jnp.pad(vec_low, ((0, shard_rows - 4), (0, 0)))
        pe_shard = jnp.concatenate([pe_weight.T.astype(BF), vec_low], axis=1)
        pe_gather = Gathering(tie(pe_shard, late)[0], True)
        qkv_gather = Gathering(tie(qkv_weight.astype(BF), late)[0], False)
    band_sum = jnp.sum(pixel_rows, axis=(0, 2))
    band_square = jnp.sum(pixel_rows * pixel_rows, axis=(0, 2))
    stats = jnp.concatenate([band_sum, band_square])
    cotangent_rows = cotangent[0]
    if routed:
        pe_gather.first_turn(stats)
        stats = tie(stats, pe_gather.held)[0]
    if whole_images:
        marks = jnp.concatenate([visible, scale_index[:, None]], axis=1).astype(F32)
        marks = marks.reshape(dp_count, sent_images * (VIS + 1))
        marks = jnp.concatenate(
            [marks, jnp.broadcast_to(stats[None], (dp_count, 2 * BANDS))], axis=1
        )
        marks_in = lax.all_to_all(marks, "dp", split_axis=0, concat_axis=0, tiled=True)
        stats = jnp.sum(marks_in[:, -2 * BANDS :], axis=0)
        stats = stats + lax.ppermute(stats, "grp", core_pairs())
    else:
        stats = lax.psum(stats, AXES)
    spots = visible.reshape(row_count)
    scale_rows = jnp.repeat(scale_index, VIS)
    if routed:
        qkv_gather.middle(stats)
        pe_gather.second_turn(qkv_gather.held)
        spots, scale_rows, cotangent_rows, marks_in = tie(
            spots, scale_rows, cotangent_rows, marks_in, pe_gather.held
        )[:4]
    else:
        early = jnp.concatenate([pe_weight.T, qkv_weight], axis=1).astype(BF)
        early_full = lax.all_gather(early, AXES, axis=0, tiled=True)
        pe_full, qkv_full = early_full[:, :PIX], early_full[:, PIX:]
        vector_all = lax.all_gather(vectors.astype(BF), AXES, axis=0, tiled=True)
    up_full, down_full = late_full[:, :FF], late_full[:, FF : 2 * FF]
    out_full, dec_full = late_full[:, 2 * FF : 2 * FF + D], late_full[:, 2 * FF + D :]

    dp_index = lax.axis_index("dp")
    if whole_images:
        image_order = marks_in[:, : -2 * BANDS].astype(jnp.int32)
        image_order = image_order.reshape(dp_count, sent_images, VIS + 1)
        visible_in, scale_in = image_order[:, :, :VIS], image_order[:, :, VIS]
        grids = cotangent_rows.reshape(sent_images, 4, dp_count, QUART, DDEC)
        hot_in = (
            visible_in[..., None] == jnp.arange(GRID).reshape(1, 1, 1, GRID)
        ).astype(BF)
        hot_quarter = hot_in.reshape(dp_count, sent_images, VIS, 4, QUART)
        dy_sent = jnp.einsum(
            "skvqr,kqsrc->skvc", hot_quarter, grids, preferred_element_type=F32
        ).astype(BF)
        dy_rows = lax.all_to_all(
            dy_sent.reshape(image_count, VIS, DDEC), "dp", split_axis=0, concat_axis=0, tiled=True
        )
        dy_rows = dy_rows.reshape(row_count, DDEC)
    if routed:
        qkv_gather.first_turn(dy_sent)
        spots, scale_rows = tie(spots, scale_rows, qkv_gather.held)[:2]
    enc_table = forward_product(angle_hot(spots, scale_rows, 3), angle_pieces(D, 3))
    if routed:
        pe_gather.cores(enc_table)
        first_full = pe_gather.total()
        pe_full = first_full[:, :PIX]
        vector_all = first_full[:, PIX:].reshape(device_count, shard_rows, SPAN)[:, :4]
        vector_all = vector_all.reshape(device_count, 4 * SPAN)[:, :vec_length].reshape(-1)
        qkv_gather.second_turn(first_full)

    entry_count = row_count * device_count * PATCH * PATCH
    band_mean = stats[:BANDS] / entry_count
    band_scale = lax.rsqrt(stats[BANDS:] / entry_count - band_mean * band_mean + EPS_NORM)
    pixel_norm = (pixel_rows - band_mean[None, :, None]) * band_scale[None, :, None]
    pixel_low = pixel_norm.reshape(row_count, PIX).astype(BF)
    pieces, up_bias, dec_bias = split_vectors(vector_all.astype(F32))
    (
        gain_one,
        shift_one,
        gain_two,
        shift_two,
        pe_bias,
        query_bias,
        value_bias,
        out_bias,
        down_bias,
        mask_token,
    ) = pieces

    if whole_images:
        vacant_in = 1.0 - jnp.sum(hot_quarter.astype(F32), axis=2)
        dy_all = jnp.sum(cotangent_rows.astype(F32), axis=(0, 1, 2))
        dy_vacant = jnp.einsum(
            "skqr,kqsrc->c", vacant_in.astype(BF), grids, preferred_element_type=F32
        )

    stream_in = back_product(pixel_low, pe_full) + pe_bias + enc_table
    norm_out_one, normed_one, inv_std_one = norm_forward(stream_in, gain_one, shift_one)
    norm_one = norm_out_one.astype(BF)
    if routed:
        qkv_gather.cores(tie(dy_rows, norm_one)[0])
        qkv_full = qkv_gather.total()
    projected = forward_product(norm_one, qkv_full) + jnp.concatenate(
        [query_bias, jnp.zeros_like(query_bias), value_bias]
    )
    projected = projected.astype(BF)
    mixture_low, peaks = attend(projected)
    stream_mid = stream_in + back_product(mixture_low, out_full) + out_bias
    norm_out_two, normed_two, inv_std_two = norm_forward(stream_mid, gain_two, shift_two)
    norm_two = norm_out_two.astype(BF)
    if whole_images:
        out_low = back_product(dy_rows, dec_full).astype(BF)
        dec_bias_grad = dy_all
        vacant_parts = []
        rest = dy_vacant
        for _ in range(3):
            part = lax.reduce_precision(rest, 8, 7)
            vacant_parts.append(part)
            rest = rest - part
        vacant_low = jnp.stack(vacant_parts).astype(BF)
        mask_grad = jnp.sum(back_product(vacant_low, dec_full), axis=0)
    else:
        placement = visible[:, :, None] == jnp.arange(GRID)[None, None, :]
        placement_low = placement.astype(BF)
        vacant = 1.0 - jnp.sum(placement.astype(F32), axis=1)
        grad_rows = cotangent[0].reshape(-1, DDEC)
        dec_bias_grad = jnp.sum(grad_rows.astype(F32), axis=0)
        grid_grad = (
            back_product(grad_rows, dec_full).astype(BF).reshape(item_count, dp_count, QUART, D)
        )
        returned = lax.all_to_all(
            grid_grad, "dp", split_axis=1, concat_axis=0, tiled=True
        ).reshape(image_count, GRID, D)
        out_low = jnp.einsum(
            "nvg,ngd->nvd", placement_low, returned, preferred_element_type=F32
        )
        out_low = out_low.reshape(row_count, D).astype(BF)
        mask_grad = jnp.einsum(
            "ng,ngd->d", vacant.astype(BF), returned, preferred_element_type=F32
        )
    out_grad_rows = out_low.astype(F32)

    activated, slope = expand(norm_two, late_full, 0, up_bias)
    down_part = Reduction(product_of(out_low, activated), routed).cores(slope)
    out_rows_after = down_part.before(out_low)
    preact_grad = forward_product(out_rows_after, down_full) * slope.astype(F32)
    up_bias_grad = jnp.sum(preact_grad, axis=0)
    preact_low = preact_grad.astype(BF)
    down_part.first_turn(preact_low)
    activated = down_part.before(activated)
    stream_out = stream_mid + back_product(activated, down_full) + down_bias
    stream_low = stream_out.astype(BF)

    if whole_images:
        dec_product = product_of(stream_low, dy_rows)

        def dec_rows_at(at, count, after):
            token = lax.dynamic_slice_in_dim(mask_token, at, count)
            return dec_product(at, count, after) + token[:, None] * dy_vacant[None, :]

    else:
        full_grid = jnp.einsum(
            "nvg,nvd->ngd",
            placement_low,
            stream_low.reshape(image_count, VIS, D),
            preferred_element_type=F32,
        )
        full_grid = (full_grid + vacant[:, :, None] * mask_token).astype(BF)
        quarters = full_grid.reshape(4 * image_count, 1, QUART, D)
        ratio_image = jnp.power(2.0, scale_index.astype(F32) - 1.0)
        ratio_quarter = jnp.repeat(ratio_image, 4).reshape(4 * image_count, 1).astype(BF)
        received = lax.all_to_all(quarters, "dp", split_axis=0, concat_axis=1, tiled=True)
        received_ratio = lax.all_to_all(
            ratio_quarter, "dp", split_axis=0, concat_axis=1, tiled=True
        )
        quarter_id = dp_index * item_count + jnp.arange(item_count)
        position = (quarter_id % 4)[:, None] * QUART + jnp.arange(QUART)[None, :]
        scale_at = jnp.round(jnp.log2(received_ratio.astype(F32))).astype(jnp.int32) + 1
        full = (item_count, dp_count, QUART)
        dec_table = forward_product(
            angle_hot(
                jnp.broadcast_to(position[:, None, :], full).reshape(-1),
                jnp.broadcast_to(scale_at[:, :, None], full).reshape(-1),
                2,
            ),
            angle_pieces(DDEC, 2),
        ).reshape(full + (DDEC,))
        decoded_rows = jnp.dot(received, dec_full, preferred_element_type=F32)
        decoded = (decoded_rows + dec_bias + dec_table).astype(BF)[None]
        dec_rows_at = product_of(received.reshape(-1, D), grad_rows)

    down_bias_grad = jnp.sum(out_grad_rows, axis=0)
    up_part = Reduction(product_of(norm_two, preact_low), routed).cores(stream_low)
    two_grad = back_product(up_part.before(preact_low), up_full)
    mid_grad, gain_two_grad, shift_two_grad = norm_backward(
        two_grad, normed_two, inv_std_two, gain_two
    )
    mid_grad = mid_grad + out_grad_rows
    mid_low = mid_grad.astype(BF)
    out_bias_grad = jnp.sum(mid_grad, axis=0)
    up_part.first_turn(mid_low)
    down_part.second_turn(mid_low)
    mid_after = down_part.before(up_part.before(mid_low))
    mixture_grad = forward_product(mid_after, out_full).astype(BF)
    projected_low, attend_sums = attend_back(projected, mixture_grad, peaks)
    query_bias_grad, value_bias_grad = attend_sums[0], attend_sums[1]
    down_part.along_z(projected_low)
    out_product, qkv_product = product_of(mid_low, mixture_low), product_of(norm_one, projected_low)
    qkv_part = Reduction(
        lambda at, count, after: jnp.concatenate(
            [out_product(at, count, after), qkv_product(at, count, after)], axis=1
        ),
        routed,
    )
    qkv_part.cores(projected_low)
    up_part.second_turn(projected_low)
    projected_after = up_part.before(qkv_part.before(down_part.before(projected_low)))
    one_grad = back_product(projected_after, qkv_full)
    in_grad, gain_one_grad, shift_one_grad = norm_backward(
        one_grad, normed_one, inv_std_one, gain_one
    )
    in_grad = in_grad + mid_grad
    pe_bias_grad = jnp.sum(in_grad, axis=0)
    in_low = in_grad.astype(BF)
    qkv_part.first_turn(in_low)
    down_shard = down_part.total(in_low)
    up_part.along_z(down_shard)
    in_after = up_part.before(qkv_part.before(in_low))
    vec_grad = jnp.concatenate(
        [
            gain_one_grad,
            shift_one_grad,
            gain_two_grad,
            shift_two_grad,
            pe_bias_grad,
            query_bias_grad,
            value_bias_grad,
            out_bias_grad,
            down_bias_grad,
            mask_grad,
            up_bias_grad,
            dec_bias_grad,
        ]
    )
    pe_product = product_of(in_after, pixel_low)
    if routed:
        vec_rows = jnp.pad(
            vec_grad.reshape(device_count, vec_length), ((0, 0), (0, 4 * SPAN - vec_length))
        ).reshape(device_count, 4, SPAN)
        vec_rows = jnp.pad(vec_rows, ((0, 0), (0, shard_rows - 4), (0, 0))).reshape(D, SPAN)
        pe_part = Reduction(
            lambda at, count, after: jnp.concatenate(
                [
                    pe_product(at, count, after),
                    lax.dynamic_slice_in_dim(vec_rows, at, count),
                    dec_rows_at(at, count, after),
                ],
                axis=1,
            ),
            routed,
        )
    else:
        pe_part = Reduction(
            lambda at, count, after: jnp.concatenate(
                [pe_product(at, count, after), dec_rows_at(at, count, after)], axis=1
            ),
            routed,
        )
    pe_part.cores(in_after)
    in_after = pe_part.before(in_after)
    if whole_images:
        stream_late = tie(stream_low, in_after)[0]
        dec_pieces = angle_pieces(DDEC, 2)
        vis_table = forward_product(angle_hot(spots, scale_rows, 2), dec_pieces)
        vis_rows = (forward_product(stream_late, dec_full) + dec_bias + vis_table).astype(BF)
        vis_in = lax.all_to_all(
            vis_rows.reshape(image_count, VIS, DDEC), "dp", split_axis=0, concat_axis=0, tiled=True
        ).reshape(dp_count, sent_images, VIS, DDEC)
        placed = jnp.einsum(
            "skvqr,skvc->kqsrc", hot_quarter, vis_in, preferred_element_type=F32
        )
        position = jnp.arange(GRID)
        every_hot = angle_hot(
            jnp.tile(position, dp_count * sent_images),
            jnp.repeat(scale_in.reshape(-1), GRID),
            2,
        ).reshape(dp_count, sent_images, 4, QUART, -1)
        every_table = jnp.einsum(
            "skqrt,tc->kqsrc", every_hot, dec_pieces, preferred_element_type=F32
        )
        mask_rows = forward_product(jnp.broadcast_to(mask_token.astype(BF), (8, D)), dec_full)[0]
        empty = vacant_in.transpose(1, 2, 0, 3)[..., None] > 0.5
        decoded = jnp.where(empty, every_table + (mask_rows + dec_bias), placed)
        decoded = decoded.astype(BF).reshape(1, item_count, dp_count, QUART, DDEC)
    norm_grad = forward_product(in_after, pe_full)
    pe_part.first_turn(norm_grad)
    norm_grad = pe_part.before(norm_grad).reshape(row_count, BANDS, PATCH * PATCH)
    pixel_grad = (norm_grad * band_scale[None, :, None]).reshape(image_count, VIS, PIX)
    up_shard = up_part.total(pixel_grad)
    qkv_part.second_turn_with(pe_part, up_shard).along_z(up_shard)
    last_total = qkv_part.total()
    out_shard, qkv_shard = last_total[:, :D], last_total[:, D : 4 * D]
    pe_shard, dec_shard = last_total[:, 4 * D : 4 * D + PIX], last_total[:, -DDEC:]
    if routed:
        vec_shard = last_total[:4, 4 * D + PIX : 4 * D + PIX + SPAN].reshape(-1)[:vec_length]
    else:
        vec_shard = lax.psum_scatter(vec_grad, AXES, scatter_dimension=0, tiled=True)
    shards = (pe_shard, qkv_shard, out_shard, up_shard, down_shard, dec_shard, vec_shard)
    local_squares = sum((jnp.sum(gradient * gradient) for gradient in shards))
    squares = tiny_sum(local_squares.reshape(1), routed)[0]
    grad_norm = jnp.sqrt(squares)
    clip_factor = jnp.minimum(1.0, CLIP_LEVEL / grad_norm)
    params = (pe_weight, qkv_weight, out_weight, up_weight, down_weight, dec_weight, vectors)
    firsts = (pe_first, qkv_first, out_first, up_first, down_first, dec_first, vec_first)
    seconds = (pe_second, qkv_second, out_second, up_second, down_second, dec_second, vec_second)
    results = []
    for number in range(7):
        step_rate = LR_VECTOR if number == 6 else LR_MATRIX
        decay_rate = 0.0 if number == 6 else DECAY_MATRIX
        gradient = shards[number].T if number in (0, 2, 4) else shards[number]
        results.extend(
            adamw_update(
                params[number],
                firsts[number],
                seconds[number],
                gradient * clip_factor,
                step_rate,
                decay_rate,
            )
        )
    return (decoded, pixel_grad, *results, grad_norm)


def solution(mesh):
    rows = P(AXES, None)
    cols = P(None, AXES)
    vecs = P(AXES)
    images = P(AXES, None, None)
    grids = P("grp", "dp", None, None, None)
    states = (cols,) * 3 + (rows,) * 3 + (cols,) * 3 + (rows,) * 3 + (cols,) * 3 + (rows,) * 3
    states = states + (vecs,) * 3
    return jax.shard_map(
        local,
        mesh=mesh,
        in_specs=(images, rows, vecs, grids) + states,
        out_specs=(grids, images) + states + (P(),),
        check_vma=False,
    )
```

time: 747 us -> 565 us (0.76)
  matrix products: 246 us -> 133 us
  local copies, waits for them, and re-layouts: 97.5 us -> 38.4 us
  Pallas kernels: 0 us -> 52 us
  waiting for transfers between devices: 181 us -> 132 us
  blocking collectives: 40.2 us -> 0 us
  starting transfers between devices: 76 us -> 93.8 us
  other arithmetic: 70.3 us -> 81.5 us
    dot_general x6 -> x0, matrix products: 53.1 us -> none  [the longest x1 16.9 us: local(): jnp.einsum('nhqk,nkhd->nqhd', score_low, keys_head, preferred_element_typ...]
    pallas_call x0 -> x3, Pallas kernels: none -> 52 us  [the longest x1 22.9 us: expand(): pl.pallas_call(expand_kernel, grid=(FF // UP_TILE,), in_specs=[pl.BlockSp...]
    dot_general x12 -> x11, matrix products: 78.2 us -> 31.4 us  [forward_product(): return jnp.dot(left, right, preferred_element_type=F32)]
    unnamed x1 -> x0, blocking collectives: 40.2 us -> none
    all_gather x1, waiting for transfers between devices: 35.7 us -> 0.01 us  [local(): late_full = lax.all_gather(late, AXES, axis=0, tiled=True)]
    reshape x4 -> x8, local copies, waits for them, and re-layouts: 36.5 us -> 4.59 us  [the longest x1 2.6 us: local(): dy_rows = dy_rows.reshape(row_count, DDEC)]
    ppermute x37 -> x32, starting transfers between devices: 35.4 us -> 61.5 us  [the longest x2 24.9 us: cores(): self.near = lax.ppermute(self.held, 'grp', core_pairs())]
    ppermute x37 -> x32, waiting for transfers between devices: 112 us -> 95.5 us  [the longest x9 23.9 us: along_z(): lax.ppermute(self.away[k - 1], 'dp', dp_pairs(4 * k))]
  transfers between devices with their start and end apart: 53 -> 41, of which waited for: 26 -> 19; matrix products, arithmetic and copies ran while one was open for 25% -> 33% of each run, Pallas kernels for 0% -> 5%
where the time goes in v2:
time: 565 us; the launch traced here: 556 us
  matrix products  133 us (24%)
  waiting for transfers between devices  132 us (23%)
  starting transfers between devices  93.8 us (17%)
  other arithmetic  81.5 us (14%)
  Pallas kernels  52 us (9%)
  local copies, waits for them, and re-layouts  38.4 us (7%)
  between operations  25 us (4%)
    dot_general x7, matrix products, back_product(): lax.dot_general(left, right, (((1,), (1,)), ((), ())), preferred_element_...  44.3 us
    dot_general x12, matrix products, weight_product(): lax.dot_general(left, right, (((0,), (0,)), ((), ())), preferred_element_...  41.1 us
    dot_general x11, matrix products, forward_product(): return jnp.dot(left, right, preferred_element_type=F32)  31.4 us
    ppermute x2, starting transfers between devices, cores(): self.near = lax.ppermute(self.held, 'grp', core_pairs())  24.9 us
    ppermute x9, waiting for transfers between devices, along_z(): lax.ppermute(self.away[k - 1], 'dp', dp_pairs(4 * k))  23.9 us
    all_to_all x1, waiting for transfers between devices, local(): lax.all_to_all(dy_sent.reshape(image_count, VIS, DDEC), 'dp', split_axis=...  23.3 us
    pallas_call x1, Pallas kernels, expand(): pl.pallas_call(expand_kernel, grid=(FF // UP_TILE,), in_specs=[pl.BlockSp...  22.9 us
    pallas_call x1, Pallas kernels, attend_back(): pl.pallas_call(attend_back_kernel, grid=(pairs,), in_specs=[block(0), blo...  19.9 us
  transfers between devices with their start and end apart: 41, of which 19 were waited for; matrix products, arithmetic and copies ran while one was open for 33% of the time, Pallas kernels for 5%

profile of v2, /device:TPU:0, one launch (start us, length us, event | category | flops | bytes accessed | tf_op | source)
XLA Modules:
  0.0 555.7 jit_solution(17351494599470464122)
XLA Ops:
  25.3 4.5 all-to-all-start
  29.8 7.2 %all-to-all-done = f32[16,1,56]{2,1,0:T(1,128)S(1)} async-done(((f32[16,1,56]{2,1,0:T(1,128)}), f32[16,1,56]{2,1,0:T(1,128)S(1)}, u32[]{:S(2)}, u32[]{:S(2)}) %all-to-all-start) | async-done | bytes 3616 | tf_op jit(solution)/shard_map/all_to_all | solution.py:556
  44.0 19.9 %collective-permute-done.6 = bf16[2,32,3072]{2,1,0:T(8,128)(2,1)} collective-permute-done((bf16[2,32,3072]{2,1,0:T(8,128)(2,1)}, bf16[2,32,3072]{2,1,0:T(8,128)(2,1)}, u32[]{:S(2)}, u32[]{:S(2)}) %collective-permute-start.6) | collective-permute-done | bytes 393248 | tf_op jit(solution)/shard_map/ppermute | solution.py:155
  67.7 14.3 %collective-permute-done.9 = bf16[4,32,3072]{2,1,0:T(8,128)(2,1)} collective-permute-done((bf16[4,32,3072]{2,1,0:T(8,128)(2,1)S(1)}, bf16[4,32,3072]{2,1,0:T(8,128)(2,1)}, u32[]{:S(2)}, u32[]{:S(2)}) %collective-permute-start.9) | collective-permute-done | bytes 786464 | tf_op jit(solution)/shard_map/ppermute | solution.py:168
  88.5 8.8 %collective-permute-start.8 = (bf16[512,896]{1,0:T(8,128)(2,1)}, bf16[512,896]{1,0:T(8,128)(2,1)}, u32[]{:S(2)}, u32[]{:S(2)}) collective-permute-start(bf16[512,896]{1,0:T(8,128)(2,1)} %bitcast.32), channel_id=1, source_target_pairs={{0,16},{16,0},{1,17},{17,1},{2,18},{18,2},{3,19},{19,3},{4,20},{20... | collective-permute-start | bytes 2752520 | tf_op jit(solution)/shard_map/ppermute | solution.py:188
  97.3 8.0 %collective-permute-done.10 = bf16[2,4,32,3072]{3,2,1,0:T(8,128)(2,1)S(1)} collective-permute-done((bf16[2,4,32,3072]{3,2,1,0:T(8,128)(2,1)S(1)}, bf16[2,4,32,3072]{3,2,1,0:T(8,128)(2,1)S(1)}, u32[]{:S(2)}, u32[]{:S(2)}) %collective-permute-start.10) | collective-permute-done | bytes 1572896 | tf_op jit(solution)/shard_map/ppermute | solution.py:175
  106.1 16.1 %collective-permute-start.11 = (bf16[512,3072]{1,0:T(8,128)(2,1)S(1)}, bf16[512,3072]{1,0:T(8,128)(2,1)}, u32[]{:S(2)}, u32[]{:S(2)}) collective-permute-start(bf16[512,3072]{1,0:T(8,128)(2,1)S(1)} %bitcast.214), channel_id=1, source_target_pairs={{0,16},{16,0},{1,17},{17,1},{2,18},{18,2},{3,19},{19,3},{4,20},{20... | collective-permute-start | bytes 9437192 | tf_op jit(solution)/shard_map/ppermute | solution.py:188
  122.3 4.8 bitcast_convert_fusion
  127.1 5.5 all-to-all-start.1
  135.7 4.3 fusion.152
  143.4 23.3 %all-to-all-done.1 = bf16[16,49,512]{2,1,0:T(8,128)(2,1)} async-done(((bf16[16,49,512]{2,1,0:T(8,128)(2,1)}), bf16[16,49,512]{2,1,0:T(8,128)(2,1)}, u32[]{:S(2)}, u32[]{:S(2)}) %all-to-all-start.1) | async-done | bytes 802848 | tf_op jit(solution)/shard_map/all_to_all | solution.py:590
  171.8 5.4 add_convert_fusion.q_ref.k_ref.v_ref
  177.2 9.2 %attend.1 = (bf16[784,1024]{1,0:T(8,128)(2,1)S(1)}, f32[8,8,256]{2,1,0:T(8,128)S(1)}) custom-call(bf16[784,3072]{1,0:T(8,128)(2,1)S(1)} %add_convert_fusion.q_ref.k_ref.v_ref, bf16[784,3072]{1,0:T(8,128)(2,1)S(1)} %add_convert_fusion.q_ref.k_ref.v_ref, bf16[784,3072]{1,0:T(8,128)(2,1)S(1)} %add_convert_fusion.q_ref.k_ref.v_ref), custom_call_target="tpu_custom_call" | custom-call | flops 411041792 | bytes 6422528 | tf_op jit(solution)/shard_map/attend/pallas_call | solution.py:356
  188.7 4.5 fusion.153
  197.7 22.9 %expand.1 = (bf16[784,4096]{1,0:T(8,128)(2,1)S(1)}, bf16[784,4096]{1,0:T(8,128)(2,1)S(1)}) custom-call(bf16[784,1024]{1,0:T(8,128)(2,1)S(1)} %add_convert_fusion.7.x_ref, bf16[1024,9728]{1,0:T(8,128)(2,1)} %all-gather.2.cloned.1.call-done.w_ref, f32[1,4096]{1,0:T(1,128)S(1)} %bitcast.207), custom_call_target="tpu_custom_call" | custom-call | flops 6576668672 | bytes 21233664 | tf_op jit(solution)/shard_map/expand/pallas_call | solution.py:478
  220.6 6.4 %convolution_convert_fusion.1 = bf16[512,4096]{1,0:T(8,128)(2,1)} fusion(bf16[784,4096]{1,0:T(8,128)(2,1)S(1)} %get-tuple-element.105, bf16[784,1024]{1,0:T(8,128)(2,1)S(1)} %convolution_convert_fusion.3, s32[]{:T(128)S(6)} %select_n.664), kind=kOutput, calls=%fused_computation.20 | convolution fusion | flops 3290431488 | bytes 11419652 | tf_op jit(solution)/shard_map/dot_general | solution.py:47
  237.2 12.7 %fusion = (f32[4096]{0:T(1024)S(1)}, bf16[784,4096]{1,0:T(8,128)(2,1)}) fusion(bf16[784,4096]{1,0:T(8,128)(2,1)S(1)} %copy-done.5, bf16[784,1024]{1,0:T(8,128)(2,1)} %copy-done.22, bf16[1024,9728]{1,0:T(8,128)(2,1)} %all-gather.2.cloned.1.call-done.w_ref), kind=kOutput, calls=%fused_computation.2 | convolution fusion | flops 6589509632 | bytes 22855680 | tf_op jit(solution)/shard_map/dot_general | solution.py:39
  251.6 6.5 %add_convert_fusion.2 = bf16[512,4096]{1,0:T(8,128)(2,1)S(1)} fusion(bf16[512,4096]{1,0:T(8,128)(2,1)} %collective-permute-done.12, bf16[784,4096]{1,0:T(8,128)(2,1)S(1)} %bitcast.206, bf16[784,1024]{1,0:T(8,128)(2,1)S(1)} %copy-done.23, s32[]{:T(128)S(6)} %select_n.665), kind=kOutput, calls=%fused_computation.9 | convolution fusion | flops 3294625792 | bytes 15613956 | tf_op jit(solution)/shard_map/dot_general | solution.py:47
  261.9 10.8 %add_convert_fusion.6 = bf16[784,1024]{1,0:T(8,128)(2,1)} fusion(f32[784,1024]{1,0:T(8,128)S(1)} %copy-done.10, bf16[784,4096]{1,0:T(8,128)(2,1)S(1)} %bitcast.206, bf16[1024,9728]{1,0:T(8,128)(2,1)} %all-gather.2.cloned.1.call-done.w_ref, f32[1024]{0:T(1024)S(1)} %get-tuple-element.342), kind=kOutput, calls=%fused_computation.41 | convolution fusion | flops 6579077120 | bytes 19632128 | tf_op jit(solution)/shard_map/dot_general | solution.py:43
  272.7 6.3 %convolution_convert_fusion = bf16[512,4096]{1,0:T(8,128)(2,1)} fusion(bf16[784,4096]{1,0:T(8,128)(2,1)S(1)} %bitcast.216, bf16[784,1024]{1,0:T(8,128)(2,1)S(1)} %add_convert_fusion.7.x_ref, s32[]{:T(128)S(6)} %select_n.664), kind=kOutput, calls=%fused_computation.19 | convolution fusion | flops 3290431488 | bytes 11419652 | tf_op jit(solution)/shard_map/dot_general | solution.py:47
  283.1 12.1 %multiply_reduce_fusion = (f32[1024]{0:T(1024)S(1)}, f32[784]{0:T(1024)S(1)}, f32[784]{0:T(1024)S(1)}, f32[1024]{0:T(1024)S(1)}, f32[784,1024]{1,0:T(8,128)S(1)}) fusion(f32[784,1024]{1,0:T(8,128)S(1)} %copy-done.10, f32[784]{0:T(1024)S(1)} %add_rsqrt_fusion, f32[784]{0:T(1024)S(1)} %broadcast_multiply_fusion.5, f32[1024]{0:T(1024)S(1)} %get-tuple-element.344, ...), kind=kOutput, calls=%fused_computation.36 | convolution fusion | flops 6583889920 | bytes 21258496 | tf_op jit(solution)/shard_map/dot_general | solution.py:43
  303.7 6.9 %add_convert_fusion.1 = bf16[512,4096]{1,0:T(8,128)(2,1)S(1)} fusion(bf16[512,4096]{1,0:T(8,128)(2,1)} %collective-permute-done.13, bf16[784,4096]{1,0:T(8,128)(2,1)S(1)} %bitcast.218, bf16[784,1024]{1,0:T(8,128)(2,1)S(1)} %add_convert_fusion.7.x_ref, s32[]{:T(128)S(6)} %select_n.665), kind=kOutput, calls=%fused_computation.8 | convolution fusion | flops 3294625792 | bytes 15613956 | tf_op jit(solution)/shard_map/dot_general | solution.py:47
  317.8 19.9 %attend_back.1 = (bf16[784,3072]{1,0:T(8,128)(2,1)S(1)}, f32[8,1024]{1,0:T(8,128)S(1)}) custom-call(bf16[784,3072]{1,0:T(8,128)(2,1)S(1)} %bitcast.204, bf16[784,3072]{1,0:T(8,128)(2,1)S(1)} %bitcast.204, bf16[784,3072]{1,0:T(8,128)(2,1)S(1)} %bitcast.204, bf16[784,1024]{1,0:T(8,128)(2,1)S(1)} %fusion.26.mix_ref, f32[8,8,256]{2,1,0:T(8,128)S(1)} %get-tuple-element.113.peak_ref), custom_call_target="tpu_custom_call" | custom-call | flops 1027604480 | bytes 11239424 | tf_op jit(solution)/shard_map/attend_back/pallas_call | solution.py:414
  340.9 7.7 %collective-permute-start.18 = (bf16[32,4096]{1,0:T(8,128)(2,1)}, bf16[32,4096]{1,0:T(8,128)(2,1)}, u32[]{:S(2)}, u32[]{:S(2)}) collective-permute-start(bf16[32,4096]{1,0:T(8,128)(2,1)} %get-tuple-element.327), channel_id=1, source_target_pairs={{0,4},{1,5},{2,6},{3,7},{4,0},{5,1},{6,2},{7,3},{8,12},{9,13},{10,... | collective-permute-start | bytes 786440 | tf_op jit(solution)/shard_map/ppermute | solution.py:254
  361.8 8.8 %multiply_reduce_fusion.1 = (f32[1024]{0:T(1024)S(1)}, f32[784]{0:T(1024)S(1)}, f32[784]{0:T(1024)S(1)}, f32[1024]{0:T(1024)S(1)}, f32[784,1024]{1,0:T(8,128)S(1)}) fusion(f32[784,1024]{1,0:T(8,128)S(1)} %copy-done.8, f32[784]{0:T(1024)S(1)} %add_rsqrt_fusion.1, f32[784]{0:T(1024)S(1)} %broadcast_multiply_fusion.6, f32[1024]{0:T(1024)S(1)} %get-tuple-element.349, ...), kind=kOutput, calls=%fused_computation.37 | convolution fusion | flops 4952305664 | bytes 17555712 | tf_op jit(solution)/shard_map/dot_general | solution.py:43
  414.7 7.7 %collective-permute-done.24 = bf16[32,4096]{1,0:T(8,128)(2,1)} collective-permute-done((bf16[32,4096]{1,0:T(8,128)(2,1)}, bf16[32,4096]{1,0:T(8,128)(2,1)}, u32[]{:S(2)}, u32[]{:S(2)}) %collective-permute-start.24) | collective-permute-done | bytes 262176 | tf_op jit(solution)/shard_map/ppermute | solution.py:254
  425.2 6.6 %collective-permute-done.26 = bf16[4,2,32,4096]{3,2,1,0:T(8,128)(2,1)} collective-permute-done((bf16[4,2,32,4096]{3,2,1,0:T(8,128)(2,1)}, bf16[4,2,32,4096]{3,2,1,0:T(8,128)(2,1)}, u32[]{:S(2)}, u32[]{:S(2)}) %collective-permute-start.26) | collective-permute-done | bytes 2097184 | tf_op jit(solution)/shard_map/ppermute | solution.py:229
  431.8 7.7 %collective-permute-done.27 = bf16[4,2,32,1408]{3,2,1,0:T(8,128)(2,1)} collective-permute-done((bf16[4,2,32,1408]{3,2,1,0:T(8,128)(2,1)}, bf16[4,2,32,1408]{3,2,1,0:T(8,128)(2,1)}, u32[]{:S(2)}, u32[]{:S(2)}) %collective-permute-start.27) | collective-permute-done | bytes 720928 | tf_op jit(solution)/shard_map/ppermute | solution.py:229
  453.1 4.6 all-to-all-start.2
  459.8 9.2 %collective-permute-done.28 = bf16[4,1,32,5504]{3,2,1,0:T(8,128)(2,1)} collective-permute-done((bf16[4,1,32,5504]{3,2,1,0:T(8,128)(2,1)}, bf16[4,1,32,5504]{3,2,1,0:T(8,128)(2,1)}, u32[]{:S(2)}, u32[]{:S(2)}) %collective-permute-start.28) | collective-permute-done | bytes 1409056 | tf_op jit(solution)/shard_map/ppermute | solution.py:239
  486.6 16.2 %collective-permute-done.30 = bf16[32,5504]{1,0:T(8,128)(2,1)S(1)} collective-permute-done((bf16[32,5504]{1,0:T(8,128)(2,1)}, bf16[32,5504]{1,0:T(8,128)(2,1)S(1)}, u32[]{:S(2)}, u32[]{:S(2)}) %collective-permute-start.30) | collective-permute-done | bytes 352288 | tf_op jit(solution)/shard_map/ppermute | solution.py:254
  521.0 7.8 %collective-permute-start.34 = (f32[1]{0:T(128)}, f32[1]{0:T(128)}, u32[]{:S(2)}, u32[]{:S(2)}) collective-permute-start(f32[1]{0:T(128)} %add.585), channel_id=1, source_target_pairs={{0,4},{1,5},{2,6},{3,7},{4,0},{5,1},{6,2},{7,3},{8,12},{9,13},{10,... | collective-permute-start | bytes 20 | tf_op jit(solution)/shard_map/ppermute | solution.py:127
  (433 shorter events, 214.1 us)
Async XLA Ops:
  7.3 181.4 %all-gather.2.cloned.1.call-start = ((), (), s32[]{:S(2)}) async-start(), calls=%async_computation.3 | async-start | bytes 20545536 | tf_op jit(solution)/shard_map/all_gather | solution.py:534
  18.0 20.3 %collective-permute-start.4 = (bf16[32,3072]{1,0:T(8,128)(2,1)S(1)}, bf16[32,3072]{1,0:T(8,128)(2,1)S(1)}, u32[]{:S(2)}, u32[]{:S(2)}) collective-permute-start(bf16[32,3072]{1,0:T(8,128)(2,1)S(1)} %convert_element_type.262), channel_id=1, source_target_pairs={{0,4},{1,5},{2,6},{3,7},{4,0},{5,1},{6,2},{7,3},{8,12},{9,13},{10,... | collective-permute-start | bytes 589832 | tf_op jit(solution)/shard_map/ppermute | solution.py:149
  25.3 11.7 %all-to-all-start = ((f32[16,1,56]{2,1,0:T(1,128)}), f32[16,1,56]{2,1,0:T(1,128)S(1)}, u32[]{:S(2)}, u32[]{:S(2)}) async-start(f32[16,1,56]{2,1,0:T(1,128)} %bitcast.10), calls=%async_computation | async-start | bytes 16384 | tf_op jit(solution)/shard_map/all_to_all | solution.py:556
  39.1 24.8 %collective-permute-start.6 = (bf16[2,32,3072]{2,1,0:T(8,128)(2,1)}, bf16[2,32,3072]{2,1,0:T(8,128)(2,1)}, u32[]{:S(2)}, u32[]{:S(2)}) collective-permute-start(bf16[2,32,3072]{2,1,0:T(8,128)(2,1)} %pad_maximum_fusion.21), channel_id=1, source_target_pairs={{0,8},{1,9},{2,10},{3,11},{4,12},{5,13},{6,14},{7,15},{8,0},{9,1},... | collective-permute-start | bytes 1179656 | tf_op jit(solution)/shard_map/ppermute | solution.py:155
  43.3 23.3 %collective-permute-start.5 = (bf16[4,32,896]{2,1,0:T(8,128)(2,1)S(1)}, bf16[4,32,896]{2,1,0:T(8,128)(2,1)}, u32[]{:S(2)}, u32[]{:S(2)}) collective-permute-start(bf16[4,32,896]{2,1,0:T(8,128)(2,1)S(1)} %bitcast_dynamic-update-slice_fusion), channel_id=1, source_target_pairs={{0,2},{1,3},{2,0},{3,1},{4,6},{5,7},{6,4},{7,5},{8,10},{9,11},{10,... | collective-permute-start | bytes 688136 | tf_op jit(solution)/shard_map/ppermute | solution.py:168
  65.0 17.1 %collective-permute-start.9 = (bf16[4,32,3072]{2,1,0:T(8,128)(2,1)S(1)}, bf16[4,32,3072]{2,1,0:T(8,128)(2,1)}, u32[]{:S(2)}, u32[]{:S(2)}) collective-permute-start(bf16[4,32,3072]{2,1,0:T(8,128)(2,1)S(1)} %pad_maximum_fusion.16), channel_id=1, source_target_pairs={{0,2},{1,3},{2,0},{3,1},{4,6},{5,7},{6,4},{7,5},{8,10},{9,11},{10,... | collective-permute-start | bytes 2359304 | tf_op jit(solution)/shard_map/ppermute | solution.py:168
  67.6 19.6 %collective-permute-start.7 = (bf16[2,4,32,896]{3,2,1,0:T(8,128)(2,1)S(1)}, bf16[2,4,32,896]{3,2,1,0:T(8,128)(2,1)S(1)}, u32[]{:S(2)}, u32[]{:S(2)}) collective-permute-start(bf16[2,4,32,896]{3,2,1,0:T(8,128)(2,1)S(1)} %pad_maximum_fusion.20), channel_id=1, source_target_pairs={{0,1},{1,0},{2,3},{3,2},{4,5},{5,4},{6,7},{7,6},{8,9},{9,8},{10,11... | collective-permute-start | bytes 1376264 | tf_op jit(solution)/shard_map/ppermute | solution.py:175
  83.5 21.9 %collective-permute-start.10 = (bf16[2,4,32,3072]{3,2,1,0:T(8,128)(2,1)S(1)}, bf16[2,4,32,3072]{3,2,1,0:T(8,128)(2,1)S(1)}, u32[]{:S(2)}, u32[]{:S(2)}) collective-permute-start(bf16[2,4,32,3072]{3,2,1,0:T(8,128)(2,1)S(1)} %pad_maximum_fusion.13), channel_id=1, source_target_pairs={{0,1},{1,0},{2,3},{3,2},{4,5},{5,4},{6,7},{7,6},{8,9},{9,8},{10,11... | collective-permute-start | bytes 4718600 | tf_op jit(solution)/shard_map/ppermute | solution.py:175
  88.5 44.1 %collective-permute-start.8 = (bf16[512,896]{1,0:T(8,128)(2,1)}, bf16[512,896]{1,0:T(8,128)(2,1)}, u32[]{:S(2)}, u32[]{:S(2)}) collective-permute-start(bf16[512,896]{1,0:T(8,128)(2,1)} %bitcast.32), channel_id=1, source_target_pairs={{0,16},{16,0},{1,17},{17,1},{2,18},{18,2},{3,19},{19,3},{4,20},{20... | collective-permute-start | bytes 2752520 | tf_op jit(solution)/shard_map/ppermute | solution.py:188
  106.1 63.2 %collective-permute-start.11 = (bf16[512,3072]{1,0:T(8,128)(2,1)S(1)}, bf16[512,3072]{1,0:T(8,128)(2,1)}, u32[]{:S(2)}, u32[]{:S(2)}) collective-permute-start(bf16[512,3072]{1,0:T(8,128)(2,1)S(1)} %bitcast.214), channel_id=1, source_target_pairs={{0,16},{16,0},{1,17},{17,1},{2,18},{18,2},{3,19},{19,3},{4,20},{20... | collective-permute-start | bytes 9437192 | tf_op jit(solution)/shard_map/ppermute | solution.py:188
  127.1 39.6 %all-to-all-start.1 = ((bf16[16,49,512]{2,1,0:T(8,128)(2,1)}), bf16[16,49,512]{2,1,0:T(8,128)(2,1)}, u32[]{:S(2)}, u32[]{:S(2)}) async-start(bf16[16,49,512]{2,1,0:T(8,128)(2,1)} %bitcast_convert_fusion), calls=%async_computation.1 | async-start | bytes 1835008 | tf_op jit(solution)/shard_map/all_to_all | solution.py:590
  227.0 24.5 %collective-permute-start.12 = (bf16[512,4096]{1,0:T(8,128)(2,1)}, bf16[512,4096]{1,0:T(8,128)(2,1)}, u32[]{:S(2)}, u32[]{:S(2)}) collective-permute-start(bf16[512,4096]{1,0:T(8,128)(2,1)} %convolution_convert_fusion.1), channel_id=1, source_target_pairs={{0,16},{16,0},{1,17},{17,1},{2,18},{18,2},{3,19},{19,3},{4,20},{20... | collective-permute-start | bytes 12582920 | tf_op jit(solution)/shard_map/ppermute | solution.py:208
  260.0 38.5 %collective-permute-start.14 = (bf16[4,2,32,4096]{3,2,1,0:T(8,128)(2,1)}, bf16[4,2,32,4096]{3,2,1,0:T(8,128)(2,1)}, u32[]{:S(2)}, u32[]{:S(2)}) collective-permute-start(bf16[4,2,32,4096]{3,2,1,0:T(8,128)(2,1)} %pad_maximum_fusion.8), channel_id=1, source_target_pairs={{0,1},{1,0},{2,3},{3,2},{4,5},{5,4},{6,7},{7,6},{8,9},{9,8},{10,11... | collective-permute-start | bytes 6291464 | tf_op jit(solution)/shard_map/ppermute | solution.py:229
  278.9 24.8 %collective-permute-start.13 = (bf16[512,4096]{1,0:T(8,128)(2,1)}, bf16[512,4096]{1,0:T(8,128)(2,1)}, u32[]{:S(2)}, u32[]{:S(2)}) collective-permute-start(bf16[512,4096]{1,0:T(8,128)(2,1)} %convolution_convert_fusion), channel_id=1, source_target_pairs={{0,16},{16,0},{1,17},{17,1},{2,18},{18,2},{3,19},{19,3},{4,20},{20... | collective-permute-start | bytes 12582920 | tf_op jit(solution)/shard_map/ppermute | solution.py:208
  301.5 36.3 %collective-permute-start.15 = (bf16[4,1,32,4096]{3,2,1,0:T(8,128)(2,1)S(1)}, bf16[4,1,32,4096]{3,2,1,0:T(8,128)(2,1)}, u32[]{:S(2)}, u32[]{:S(2)}) collective-permute-start(bf16[4,1,32,4096]{3,2,1,0:T(8,128)(2,1)S(1)} %get-tuple-element.307), channel_id=1, source_target_pairs={{0,2},{1,3},{2,0},{3,1},{4,6},{5,7},{6,4},{7,5},{8,10},{9,11},{10,... | collective-permute-start | bytes 3145736 | tf_op jit(solution)/shard_map/ppermute | solution.py:239
  312.6 46.0 %collective-permute-start.16 = (bf16[4,2,32,4096]{3,2,1,0:T(8,128)(2,1)}, bf16[4,2,32,4096]{3,2,1,0:T(8,128)(2,1)S(1)}, u32[]{:S(2)}, u32[]{:S(2)}) collective-permute-start(bf16[4,2,32,4096]{3,2,1,0:T(8,128)(2,1)} %pad_maximum_fusion.10), channel_id=1, source_target_pairs={{0,1},{1,0},{2,3},{3,2},{4,5},{5,4},{6,7},{7,6},{8,9},{9,8},{10,11... | collective-permute-start | bytes 6291464 | tf_op jit(solution)/shard_map/ppermute | solution.py:229
  340.9 32.1 %collective-permute-start.18 = (bf16[32,4096]{1,0:T(8,128)(2,1)}, bf16[32,4096]{1,0:T(8,128)(2,1)}, u32[]{:S(2)}, u32[]{:S(2)}) collective-permute-start(bf16[32,4096]{1,0:T(8,128)(2,1)} %get-tuple-element.327), channel_id=1, source_target_pairs={{0,4},{1,5},{2,6},{3,7},{4,0},{5,1},{6,2},{7,3},{8,12},{9,13},{10,... | collective-permute-start | bytes 786440 | tf_op jit(solution)/shard_map/ppermute | solution.py:254
  348.6 24.5 %collective-permute-start.19 = (bf16[32,4096]{1,0:T(8,128)(2,1)}, bf16[32,4096]{1,0:T(8,128)(2,1)}, u32[]{:S(2)}, u32[]{:S(2)}) collective-permute-start(bf16[32,4096]{1,0:T(8,128)(2,1)} %get-tuple-element.326), channel_id=1, source_target_pairs={{0,8},{1,9},{2,10},{3,11},{4,12},{5,13},{6,14},{7,15},{8,0},{9,1},... | collective-permute-start | bytes 786440 | tf_op jit(solution)/shard_map/ppermute | solution.py:254
  348.6 24.5 %collective-permute-start.20 = (bf16[32,4096]{1,0:T(8,128)(2,1)}, bf16[32,4096]{1,0:T(8,128)(2,1)}, u32[]{:S(2)}, u32[]{:S(2)}) collective-permute-start(bf16[32,4096]{1,0:T(8,128)(2,1)} %get-tuple-element.325), channel_id=1, source_target_pairs={{0,12},{1,13},{2,14},{3,15},{4,8},{5,9},{6,10},{7,11},{8,4},{9,5},... | collective-permute-start | bytes 786440 | tf_op jit(solution)/shard_map/ppermute | solution.py:254
  358.7 25.9 %collective-permute-start.17 = (bf16[512,4096]{1,0:T(8,128)(2,1)}, bf16[512,4096]{1,0:T(8,128)(2,1)}, u32[]{:S(2)}, u32[]{:S(2)}) collective-permute-start(bf16[512,4096]{1,0:T(8,128)(2,1)} %pad_maximum_fusion.1), channel_id=1, source_target_pairs={{0,16},{16,0},{1,17},{17,1},{2,18},{18,2},{3,19},{19,3},{4,20},{20... | collective-permute-start | bytes 12582920 | tf_op jit(solution)/shard_map/ppermute | solution.py:208
  360.6 21.5 %collective-permute-start.21 = (bf16[4,1,32,4096]{3,2,1,0:T(8,128)(2,1)}, bf16[4,1,32,4096]{3,2,1,0:T(8,128)(2,1)}, u32[]{:S(2)}, u32[]{:S(2)}) collective-permute-start(bf16[4,1,32,4096]{3,2,1,0:T(8,128)(2,1)} %get-tuple-element.305), channel_id=1, source_target_pairs={{0,2},{1,3},{2,0},{3,1},{4,6},{5,7},{6,4},{7,5},{8,10},{9,11},{10,... | collective-permute-start | bytes 3145736 | tf_op jit(solution)/shard_map/ppermute | solution.py:239
  394.7 13.2 %collective-permute-start.22 = (bf16[512,1408]{1,0:T(8,128)(2,1)S(1)}, bf16[512,1408]{1,0:T(8,128)(2,1)S(1)}, u32[]{:S(2)}, u32[]{:S(2)}) collective-permute-start(bf16[512,1408]{1,0:T(8,128)(2,1)S(1)} %pad_maximum_fusion.14), channel_id=1, source_target_pairs={{0,16},{16,0},{1,17},{17,1},{2,18},{18,2},{3,19},{19,3},{4,20},{20... | collective-permute-start | bytes 4325384 | tf_op jit(solution)/shard_map/ppermute | solution.py:208
  399.5 15.2 %collective-permute-start.23 = (bf16[32,4096]{1,0:T(8,128)(2,1)}, bf16[32,4096]{1,0:T(8,128)(2,1)}, u32[]{:S(2)}, u32[]{:S(2)}) collective-permute-start(bf16[32,4096]{1,0:T(8,128)(2,1)} %get-tuple-element.323), channel_id=1, source_target_pairs={{0,4},{1,5},{2,6},{3,7},{4,0},{5,1},{6,2},{7,3},{8,12},{9,13},{10,... | collective-permute-start | bytes 786440 | tf_op jit(solution)/shard_map/ppermute | solution.py:254
  400.7 21.6 %collective-permute-start.24 = (bf16[32,4096]{1,0:T(8,128)(2,1)}, bf16[32,4096]{1,0:T(8,128)(2,1)}, u32[]{:S(2)}, u32[]{:S(2)}) collective-permute-start(bf16[32,4096]{1,0:T(8,128)(2,1)} %get-tuple-element.322), channel_id=1, source_target_pairs={{0,8},{1,9},{2,10},{3,11},{4,12},{5,13},{6,14},{7,15},{8,0},{9,1},... | collective-permute-start | bytes 786440 | tf_op jit(solution)/shard_map/ppermute | solution.py:254
  401.6 20.7 %collective-permute-start.25 = (bf16[32,4096]{1,0:T(8,128)(2,1)}, bf16[32,4096]{1,0:T(8,128)(2,1)}, u32[]{:S(2)}, u32[]{:S(2)}) collective-permute-start(bf16[32,4096]{1,0:T(8,128)(2,1)} %get-tuple-element.321), channel_id=1, source_target_pairs={{0,12},{1,13},{2,14},{3,15},{4,8},{5,9},{6,10},{7,11},{8,4},{9,5},... | collective-permute-start | bytes 786440 | tf_op jit(solution)/shard_map/ppermute | solution.py:254
  405.4 26.4 %collective-permute-start.26 = (bf16[4,2,32,4096]{3,2,1,0:T(8,128)(2,1)}, bf16[4,2,32,4096]{3,2,1,0:T(8,128)(2,1)}, u32[]{:S(2)}, u32[]{:S(2)}) collective-permute-start(bf16[4,2,32,4096]{3,2,1,0:T(8,128)(2,1)} %pad_maximum_fusion.12), channel_id=1, source_target_pairs={{0,1},{1,0},{2,3},{3,2},{4,5},{5,4},{6,7},{7,6},{8,9},{9,8},{10,11... | collective-permute-start | bytes 6291464 | tf_op jit(solution)/shard_map/ppermute | solution.py:229
  409.4 30.1 %collective-permute-start.27 = (bf16[4,2,32,1408]{3,2,1,0:T(8,128)(2,1)}, bf16[4,2,32,1408]{3,2,1,0:T(8,128)(2,1)}, u32[]{:S(2)}, u32[]{:S(2)}) collective-permute-start(bf16[4,2,32,1408]{3,2,1,0:T(8,128)(2,1)} %pad_maximum_fusion.18), channel_id=1, source_target_pairs={{0,1},{1,0},{2,3},{3,2},{4,5},{5,4},{6,7},{7,6},{8,9},{9,8},{10,11... | collective-permute-start | bytes 2162696 | tf_op jit(solution)/shard_map/ppermute | solution.py:229
  444.2 24.8 %collective-permute-start.28 = (bf16[4,1,32,5504]{3,2,1,0:T(8,128)(2,1)}, bf16[4,1,32,5504]{3,2,1,0:T(8,128)(2,1)}, u32[]{:S(2)}, u32[]{:S(2)}) collective-permute-start(bf16[4,1,32,5504]{3,2,1,0:T(8,128)(2,1)} %get-tuple-element.304), channel_id=1, source_target_pairs={{0,2},{1,3},{2,0},{3,1},{4,6},{5,7},{6,4},{7,5},{8,10},{9,11},{10,... | collective-permute-start | bytes 4227080 | tf_op jit(solution)/shard_map/ppermute | solution.py:239
  453.1 25.8 %all-to-all-start.2 = ((bf16[16,49,512]{2,1,0:T(8,128)(2,1)}), bf16[16,49,512]{2,1,0:T(8,128)(2,1)}, u32[]{:S(2)}, u32[]{:S(2)}) async-start(bf16[16,49,512]{2,1,0:T(8,128)(2,1)} %reshape.757), calls=%async_computation.2 | async-start | bytes 1835008 | tf_op jit(solution)/shard_map/all_to_all | solution.py:811
  471.7 14.9 %collective-permute-start.29 = (bf16[32,5504]{1,0:T(8,128)(2,1)}, bf16[32,5504]{1,0:T(8,128)(2,1)S(1)}, u32[]{:S(2)}, u32[]{:S(2)}) collective-permute-start(bf16[32,5504]{1,0:T(8,128)(2,1)} %get-tuple-element.318), channel_id=1, source_target_pairs={{0,4},{1,5},{2,6},{3,7},{4,0},{5,1},{6,2},{7,3},{8,12},{9,13},{10,... | collective-permute-start | bytes 1056776 | tf_op jit(solution)/shard_map/ppermute | solution.py:254
  471.7 31.2 %collective-permute-start.30 = (bf16[32,5504]{1,0:T(8,128)(2,1)}, bf16[32,5504]{1,0:T(8,128)(2,1)S(1)}, u32[]{:S(2)}, u32[]{:S(2)}) collective-permute-start(bf16[32,5504]{1,0:T(8,128)(2,1)} %get-tuple-element.320), channel_id=1, source_target_pairs={{0,8},{1,9},{2,10},{3,11},{4,12},{5,13},{6,14},{7,15},{8,0},{9,1},... | collective-permute-start | bytes 1056776 | tf_op jit(solution)/shard_map/ppermute | solution.py:254
  473.8 29.8 %collective-permute-start.31 = (bf16[32,5504]{1,0:T(8,128)(2,1)S(1)}, bf16[32,5504]{1,0:T(8,128)(2,1)}, u32[]{:S(2)}, u32[]{:S(2)}) collective-permute-start(bf16[32,5504]{1,0:T(8,128)(2,1)S(1)} %get-tuple-element.319), channel_id=1, source_target_pairs={{0,12},{1,13},{2,14},{3,15},{4,8},{5,9},{6,10},{7,11},{8,4},{9,5},... | collective-permute-start | bytes 1056776 | tf_op jit(solution)/shard_map/ppermute | solution.py:254
  (96 other events, 1173.9 us)
Sparse Core Ops, SparseCore 0:
  12.4 170.7 all-gather.1

commit v3 on v2

v3 whole, which is shorter than its diff:
```python
import functools

import jax
import jax.numpy as jnp
import ml_dtypes
import numpy as np
from jax import lax
from jax.experimental import pallas as pl
from jax.experimental.pallas import tpu as pltpu
from jax.sharding import PartitionSpec as P

D = 1024
FF = 4096
HEADS = 16
HDIM = 64
DDEC = 512
PATCH = 16
SIDE = 14
BANDS = 3
STEP = 10
PIX = 768
GRID = 196
VIS = 49
QUART = 49
NSCALE = 4
AXES = ("grp", "dp")
HALF = D // 2
BF = jnp.bfloat16
F32 = jnp.float32

EPS_NORM = 1e-05
BETA_ONE = 0.9
BETA_TWO = 0.95
ADAM_EPS = 1e-08
LR_MATRIX = 0.08
LR_VECTOR = 0.3
DECAY_MATRIX = 0.05
CLIP_LEVEL = 1.0


def forward_product(left, right):
    return jnp.dot(left, right, preferred_element_type=F32)


def back_product(left, right):
    return lax.dot_general(left, right, (((1,), (1,)), ((), ())), preferred_element_type=F32)


def weight_product(left, right):
    return lax.dot_general(left, right, (((0,), (0,)), ((), ())), preferred_element_type=F32)


def angle_pieces(channels, pieces):
    quarter = channels // 4
    step = np.float32(-np.log(np.float32(10000.0))) / np.float32(quarter)
    frequency = np.exp(np.arange(quarter, dtype=np.float32) * step)
    ratio = np.float32(2.0) ** (np.arange(NSCALE, dtype=np.float32) - 1)
    spot = np.arange(SIDE, dtype=np.float32)
    angle = (ratio[:, None] * spot[None, :]).reshape(-1, 1) * frequency[None, :]
    half = np.concatenate([np.sin(angle.astype(np.float64)), np.cos(angle.astype(np.float64))], 1)
    zeros = np.zeros_like(half)
    rest = np.concatenate(
        [np.concatenate([half, zeros], 1), np.concatenate([zeros, half], 1)], 0
    ).astype(np.float32)
    cut = []
    for _ in range(pieces):
        part = rest.astype(ml_dtypes.bfloat16)
        cut.append(part)
        rest = rest - part.astype(np.float32)
    return jnp.asarray(np.concatenate(cut, 0))


def angle_hot(spots, scale_rows, pieces):
    row_at = scale_rows * SIDE + spots // SIDE
    col_at = (NSCALE + scale_rows) * SIDE + spots % SIDE
    slot = jnp.arange(2 * NSCALE * SIDE)[None, :]
    hot = ((slot == row_at[:, None]) | (slot == col_at[:, None])).astype(BF)
    return jnp.concatenate([hot] * pieces, axis=1)


def split_vectors(vector_all):
    pieces = tuple((vector_all[number * D : (number + 1) * D] for number in range(10)))
    return (pieces, vector_all[10 * D : 10 * D + FF], vector_all[10 * D + FF :])


def halves(array):
    return (array[..., :HALF], array[..., HALF:])


def row_mean(pair):
    return sum(jnp.sum(part, axis=-1, keepdims=True) for part in pair) * (1.0 / D)


def norm_forward(hidden_in, norm_gain, norm_shift):
    mean = row_mean(hidden_in)
    center = [part - mean for part in hidden_in]
    inv_std = lax.rsqrt(row_mean([part * part for part in center]) + EPS_NORM)
    normed = [part * inv_std for part in center]
    low = [
        (part * gain + shift).astype(BF) for part, gain, shift in zip(normed, norm_gain, norm_shift)
    ]
    return (low, normed, inv_std)


def norm_backward(grad_out, normed, inv_std, norm_gain):
    scaled = [part * gain for part, gain in zip(grad_out, norm_gain)]
    mean = row_mean(scaled)
    along = row_mean([part * unit for part, unit in zip(scaled, normed)])
    inner = [(part - mean - unit * along) * inv_std for part, unit in zip(scaled, normed)]
    gain_grad = [jnp.sum(part * unit, axis=0) for part, unit in zip(grad_out, normed)]
    return (inner, gain_grad, [jnp.sum(part, axis=0) for part in grad_out])


def inward(pair, weights, first, count):
    return sum(
        forward_product(part, weight[:, first : first + count]) for part, weight in zip(pair, weights)
    )


def outward(left, weights, first, count):
    return [back_product(left, weight[:, first : first + count]) for weight in weights]


def adamw_update(weight, moment_one, moment_two, gradient, step_rate, decay_rate):
    new_one = BETA_ONE * moment_one + (1.0 - BETA_ONE) * gradient
    new_two = BETA_TWO * moment_two + (1.0 - BETA_TWO) * gradient * gradient
    fixed_one = new_one / (1.0 - BETA_ONE**STEP)
    fixed_two = new_two / (1.0 - BETA_TWO**STEP)
    new_weight = weight - step_rate * (
        fixed_one / (jnp.sqrt(fixed_two) + ADAM_EPS) + decay_rate * weight
    )
    return (new_one, new_two, new_weight)


def core_pairs():
    return [(0, 1), (1, 0)]


def dp_pairs(bits):
    return [(i, i ^ bits) for i in range(16)]


def turn_pairs(core_zero, core_one):
    return [(g * 16 + i, g * 16 + (i ^ (core_one if g else core_zero))) for g in range(2) for i in range(16)]


def tiny_sum(value, routed):
    if not routed:
        return lax.psum(value, AXES)
    for unit in (1, 4):
        one, two, three = [lax.ppermute(value, "dp", dp_pairs(unit * k)) for k in (1, 2, 3)]
        value = (value + one) + (two + three)
    return value + lax.ppermute(value, "grp", core_pairs())


class Order:
    def __init__(self, token):
        self.token = token

    def __call__(self, *values):
        *values, self.token = lax.optimization_barrier((*values, self.token))
        return values[0] if len(values) == 1 else values


def spot_of_chip():
    chip = lax.axis_index("dp")
    return lax.axis_index("grp"), chip % 2, (chip // 2) % 2, chip // 4


def block_order():
    core, x, y, z = spot_of_chip()
    place = jnp.arange(32)
    far, turn_one, turn_two, step = place // 16, (place // 8) % 2, (place // 4) % 2, place % 4
    at_core = core ^ far
    at_x = x ^ jnp.where(at_core == 0, turn_one, turn_two)
    at_y = y ^ jnp.where(at_core == 0, turn_two, turn_one)
    owner = at_core * 16 + (z ^ step) * 4 + at_y * 2 + at_x
    return (owner[:, None] == jnp.arange(32)[None, :]).astype(BF)


class Gathering:
    def __init__(self, shard, direct, order):
        self.order = order
        self.held = order(shard)
        steps = (1, 2, 3) if direct else (1,)
        self.near = [lax.ppermute(self.held, "dp", dp_pairs(4 * k)) for k in steps]

    def grow(self):
        held = self.order(self.held)
        self.held = self.order(jnp.concatenate([held] + self.near))
        return self.held

    def middle(self):
        self.near = [lax.ppermute(self.grow(), "dp", dp_pairs(8))]

    def first_turn(self):
        self.near = [lax.ppermute(self.grow(), AXES, turn_pairs(2, 1))]

    def second_turn(self):
        self.near = [lax.ppermute(self.grow(), AXES, turn_pairs(1, 2))]

    def cores(self):
        self.near = [lax.ppermute(self.grow(), "grp", core_pairs())]

    def total(self):
        return (self.held, self.near[0])


class Reduction:
    def __init__(self, product, routed, order):
        self.product, self.routed, self.order = product, routed, order

    def cores(self):
        if self.routed:
            away = self.order(self.product(1, None))
            self.came = lax.ppermute(away, "grp", core_pairs())

    def first_turn(self):
        if self.routed:
            self.kept, away = self.order(*self.product(0, self.came))
            self.came = lax.ppermute(away, AXES, turn_pairs(1, 2))

    def sum_of(self, first, count):
        part = self.kept[first : first + count].astype(F32)
        return (part + self.came[first : first + count].astype(F32)).astype(BF)

    def second_turn(self):
        if self.routed:
            self.kept = self.order(self.kept)
            half = HALF // 4
            away, self.kept = self.order(self.sum_of(half, half), self.sum_of(0, half))
            self.came = lax.ppermute(away, AXES, turn_pairs(2, 1))

    def along_z(self):
        if self.routed:
            self.kept = self.order(self.kept)
            parts = self.order(*[self.sum_of(32 * k, 32) for k in range(4)])
            self.kept = parts[0]
            self.came = [lax.ppermute(parts[k], "dp", dp_pairs(4 * k)) for k in (1, 2, 3)]

    def join(self, other):
        if self.routed:
            self.came = jnp.concatenate([self.came, other.came], axis=-1)
            self.kept = jnp.concatenate([self.kept, other.kept], axis=-1)
        else:
            mine, theirs = self.product, other.product
            self.product = lambda *at: jnp.concatenate([mine(*at), theirs(*at)], axis=1)

    def total(self):
        if not self.routed:
            full = jnp.concatenate([self.product(half, None) for half in range(2)])
            half = lax.psum_scatter(full, "grp", scatter_dimension=0, tiled=True)
            return lax.psum_scatter(half, "dp", scatter_dimension=0, tiled=True).astype(F32)
        total = self.order(self.kept).astype(F32)
        for part in self.came:
            total = total + part.astype(F32)
        return self.order(total)


WEIGHT_TILE = 1024


def weight_kernel(edges, added, *refs):
    tile = pl.program_id(0)
    sides = refs[: 2 * len(edges)]
    outs = refs[2 * len(edges) + added :]
    first = 0
    for number, last in enumerate(edges):

        @pl.when((tile >= first) & (tile < last))
        def _(left=sides[2 * number], right=sides[2 * number + 1]):
            value = tn(left[...], right[...])
            if added:
                value = value + refs[2 * len(edges)][...].astype(F32)
                outs[0][...] = value[: HALF // 2].astype(BF)
                outs[1][...] = value[HALF // 2 :].astype(BF)
            else:
                outs[0][...] = value.astype(BF)

        first = last


def weight_call(pairs, came):
    edges, specs, count = [], [], 0
    for left, right in pairs:
        start, tiles = count, right.shape[1] // WEIGHT_TILE
        count += tiles

        def at(i, start=start, tiles=tiles):
            return (0, jnp.clip(i - start, 0, tiles - 1))

        specs.append(pl.BlockSpec(left.shape, lambda i: (0, 0)))
        specs.append(pl.BlockSpec((right.shape[0], WEIGHT_TILE), at))
        edges.append(count)
    columns = count * WEIGHT_TILE
    sides = [side for pair in pairs for side in pair]
    if came is None:
        shapes = [(HALF, columns)]
    else:
        shapes = [(HALF // 2, columns)] * 2
        sides.append(came)
        specs.append(pl.BlockSpec((HALF, WEIGHT_TILE), lambda i: (0, i)))
    outs = pl.pallas_call(
        functools.partial(weight_kernel, tuple(edges), int(came is not None)),
        grid=(count,),
        in_specs=specs,
        out_specs=[pl.BlockSpec((shape[0], WEIGHT_TILE), lambda i: (0, i)) for shape in shapes],
        out_shape=[jax.ShapeDtypeStruct(shape, BF) for shape in shapes],
        compiler_params=pltpu.CompilerParams(vmem_limit_bytes=40 * 2**20),
        cost_estimate=SMALL,
        name="weight_product",
    )(*sides)
    return outs if came is not None else outs[0]


def product_of(order, *pairs):
    def product(half, came):
        lefts = order(*[left[half] for left, _ in pairs])
        lefts = lefts if len(pairs) > 1 else [lefts]
        return weight_call([(left, right) for left, (_, right) in zip(lefts, pairs)], came)

    return product


def last_kernel(added, in_ref, pixel_ref, vec_ref, stream_ref, dy_ref, token_ref, vacant_ref, *refs):
    outs = refs[added:]
    parts = (
        (0, PIX, tn(in_ref[...], pixel_ref[...])),
        (PIX, SPAN, vec_ref[...]),
        (PIX + SPAN, DDEC, tn(stream_ref[...], dy_ref[...]) + token_ref[...] * vacant_ref[...]),
    )
    for first, count, value in parts:
        cols = pl.ds(first, count)
        if added:
            value = value + refs[0][:, cols].astype(F32)
            outs[0][:, cols] = value[: HALF // 2].astype(BF)
            outs[1][:, cols] = value[HALF // 2 :].astype(BF)
        else:
            outs[0][:, cols] = value.astype(BF)


def last_call(operands, came):
    columns = PIX + SPAN + DDEC
    shapes = [(HALF, columns)] if came is None else [(HALF // 2, columns)] * 2
    extra = [] if came is None else [came]
    outs = pl.pallas_call(
        functools.partial(last_kernel, len(extra)),
        out_shape=[jax.ShapeDtypeStruct(shape, BF) for shape in shapes],
        compiler_params=pltpu.CompilerParams(vmem_limit_bytes=40 * 2**20),
        cost_estimate=SMALL,
        name="last_product",
    )(*operands, *extra)
    return outs if came is not None else outs[0]


SPAN = 128
SMALL = pl.CostEstimate(flops=10**6, bytes_accessed=10**5, transcendentals=0)


def windows(rows):
    for pair in range(rows // (2 * VIS)):
        start = min(2 * VIS * pair // 16 * 16, rows - SPAN)
        yield start, 2 * VIS * pair - start


def same_image(offset):
    key = lax.broadcasted_iota(jnp.int32, (SPAN, SPAN), 0) - offset
    query = lax.broadcasted_iota(jnp.int32, (SPAN, SPAN), 1) - offset
    inside = (key >= 0) & (key < 2 * VIS)
    match = inside & (query >= 0) & (query < 2 * VIS) & ((key >= VIS) == (query >= VIS))
    weight = match.astype(F32)
    return jnp.concatenate([weight, weight], axis=1) > 0.5, inside


def head_lanes():
    lane = lax.broadcasted_iota(jnp.int32, (SPAN, SPAN), 1)
    low = (lane < HDIM).astype(F32)
    return low.astype(BF), (1.0 - low).astype(BF), lane < HDIM


def nt(left, right):
    return lax.dot_general(left, right, (((1,), (1,)), ((), ())), preferred_element_type=F32)


def tn(left, right):
    return lax.dot_general(left, right, (((0,), (0,)), ((), ())), preferred_element_type=F32)


SCALE = HDIM ** (-0.5)


def attend_kernel(q_ref, k_ref, v_ref, mix_ref, peak_ref):
    low, high, is_low = head_lanes()
    low, high = low * SCALE, high * SCALE
    for number, (start, offset) in enumerate(windows(mix_ref.shape[0])):
        rows = pl.ds(start, SPAN)
        match, inside = same_image(offset)
        q_win = q_ref[rows, :]
        q_two = jnp.concatenate([q_win * low, q_win * high], axis=0)
        scores = jnp.where(match, nt(k_ref[rows, :], q_two), -1e30)
        peak = jnp.max(scores, axis=0, keepdims=True)
        grown = jnp.exp(scores - peak)
        total = jnp.sum(grown, axis=0, keepdims=True)
        probs = (grown * (1.0 / total)).astype(BF)
        peak_ref[0, number : number + 1, :] = peak + jnp.log(total)
        both = tn(probs, v_ref[rows, :])
        mixed = jnp.where(is_low, both[:SPAN], both[SPAN:])
        held = mix_ref[rows, :].astype(F32)
        mix_ref[rows, :] = jnp.where(inside, mixed, held).astype(BF)


def attend(projected):
    rows = projected.shape[0]
    pairs = HEADS // 2
    count = rows // (2 * VIS)
    block = lambda shift: pl.BlockSpec((rows, SPAN), lambda i: (0, i + shift))
    return pl.pallas_call(
        attend_kernel,
        grid=(pairs,),
        in_specs=[block(0), block(pairs), block(2 * pairs)],
        out_specs=[block(0), pl.BlockSpec((1, count, 2 * SPAN), lambda i: (i, 0, 0))],
        out_shape=[
            jax.ShapeDtypeStruct((rows, D), BF),
            jax.ShapeDtypeStruct((pairs, count, 2 * SPAN), F32),
        ],
        compiler_params=pltpu.CompilerParams(vmem_limit_bytes=32 * 2**20),
        cost_estimate=SMALL,
        name="attend",
    )(projected, projected, projected)


def attend_back_kernel(q_ref, k_ref, v_ref, mix_ref, peak_ref, grad_ref, sums_ref):
    at = pl.program_id(0) * SPAN
    low, high, is_low = head_lanes()
    q_sum = jnp.zeros((1, SPAN), F32)
    v_sum = jnp.zeros((1, SPAN), F32)

    def put(rows, shift, value, inside):
        cols = pl.ds(pl.multiple_of(at + shift * D, SPAN), SPAN)
        held = grad_ref[rows, cols].astype(F32)
        grad_ref[rows, cols] = jnp.where(inside, value, held).astype(BF)

    for number, (start, offset) in enumerate(windows(q_ref.shape[0])):
        rows = pl.ds(start, SPAN)
        match, inside = same_image(offset)
        q_win, k_win, v_win, mix_win = q_ref[rows, :], k_ref[rows, :], v_ref[rows, :], mix_ref[rows, :]
        q_win = q_win * SCALE
        q_two = jnp.concatenate([q_win * low, q_win * high], axis=0)
        mix_two = jnp.concatenate([mix_win * low, mix_win * high], axis=0)
        scores = nt(k_win, q_two) - peak_ref[0, number : number + 1, :]
        probs = jnp.exp(jnp.where(match, scores, -1e30))
        probs_low = probs.astype(BF)
        v_grad = jnp.dot(probs_low, mix_two, preferred_element_type=F32)
        probs_grad = nt(v_win, mix_two)
        inner = jnp.sum(probs_grad * probs, axis=0, keepdims=True)
        score = (probs * (probs_grad - inner)).astype(BF)
        k_grad = jnp.dot(score, q_two, preferred_element_type=F32)
        q_both = tn(score, k_win * SCALE)
        q_grad = jnp.where(is_low, q_both[:SPAN], q_both[SPAN:])
        put(rows, 0, q_grad, inside)
        put(rows, 1, k_grad, inside)
        put(rows, 2, v_grad, inside)
        q_sum += jnp.sum(jnp.where(inside, q_grad, 0.0), axis=0, keepdims=True)
        v_sum += jnp.sum(jnp.where(inside, v_grad, 0.0), axis=0, keepdims=True)
    sums_ref[...] = jnp.concatenate([q_sum, v_sum, jnp.zeros((6, SPAN), F32)], axis=0)


def attend_back(projected, mixture_grad, peaks):
    rows = projected.shape[0]
    pairs = HEADS // 2
    count = rows // (2 * VIS)
    block = lambda shift: pl.BlockSpec((rows, SPAN), lambda i: (0, i + shift))
    return pl.pallas_call(
        attend_back_kernel,
        grid=(pairs,),
        in_specs=[
            block(0),
            block(pairs),
            block(2 * pairs),
            block(0),
            pl.BlockSpec((1, count, 2 * SPAN), lambda i: (i, 0, 0)),
        ],
        out_specs=[
            pl.BlockSpec((rows, 3 * D), lambda i: (0, 0)),
            pl.BlockSpec((8, SPAN), lambda i: (0, i)),
        ],
        out_shape=[
            jax.ShapeDtypeStruct((rows, 3 * D), BF),
            jax.ShapeDtypeStruct((8, D), F32),
        ],
        compiler_params=pltpu.CompilerParams(vmem_limit_bytes=40 * 2**20),
        cost_estimate=SMALL,
        name="attend_back",
    )(projected, projected, projected, mixture_grad, peaks)


TAIL_STEP = 0.33
TAIL = (
    0.18636611813641438,
    0.1828371164957563,
    0.20192458123233548,
    0.04500824941716716,
    0.41254593072161144,
    -0.3554434272669394,
    0.46269071975152953,
    -0.1359293701595944,
)


def gelu_and_slope(x):
    t = 1.0 / (1.0 + (TAIL_STEP * 0.7071067811865476) * jnp.abs(x))
    bell = jnp.exp(-0.5 * x * x)
    tail = jnp.full_like(x, 0.5 * TAIL[-1])
    for factor in TAIL[-2::-1]:
        tail = tail * t + 0.5 * factor
    tail = tail * t * bell
    normal = jnp.where(x >= 0.0, 1.0 - tail, tail)
    return x * normal, normal + x * bell * 0.3989422804014327


UP_TILE = 512


def both(near_ref, far_ref, near_w_ref, far_w_ref):
    product = jnp.dot(near_ref[...], near_w_ref[...], preferred_element_type=F32)
    return product + jnp.dot(far_ref[...], far_w_ref[...], preferred_element_type=F32)


def expand_kernel(near_ref, far_ref, near_w_ref, far_w_ref, bias_ref, act_ref, slope_ref):
    preact = both(near_ref, far_ref, near_w_ref, far_w_ref) + bias_ref[...]
    activated, slope = gelu_and_slope(preact)
    act_ref[...] = activated.astype(BF)
    slope_ref[...] = slope.astype(BF)


def shift_kernel(near_ref, far_ref, near_w_ref, far_w_ref, bias_ref, out_ref):
    out_ref[...] = (both(near_ref, far_ref, near_w_ref, far_w_ref) + bias_ref[...]).astype(BF)


def scale_kernel(near_ref, far_ref, near_w_ref, far_w_ref, scale_ref, out_ref):
    out_ref[...] = both(near_ref, far_ref, near_w_ref, far_w_ref) * scale_ref[...]


def slope_kernel(near_ref, far_ref, near_w_ref, far_w_ref, slope_ref, out_ref, sums_ref):
    grad = both(near_ref, far_ref, near_w_ref, far_w_ref) * slope_ref[...].astype(F32)
    out_ref[...] = grad.astype(BF)
    sums_ref[...] = jnp.sum(grad, axis=0, keepdims=True)


def inward_call(kernel, pair, weights, first_column, columns, extra, outs, width=UP_TILE):
    rows = pair[0].shape[0]
    shift = first_column // width
    whole = pl.BlockSpec((rows, HALF), lambda i: (0, 0))
    weight = pl.BlockSpec((HALF, width), lambda i: (0, i + shift))
    tile = lambda array: pl.BlockSpec((array.shape[0], width), lambda i: (0, i))
    return pl.pallas_call(
        kernel,
        grid=(columns // width,),
        in_specs=[whole, whole, weight, weight, tile(extra)],
        out_specs=[tile(out) for out in outs],
        out_shape=outs,
        compiler_params=pltpu.CompilerParams(vmem_limit_bytes=40 * 2**20),
        cost_estimate=SMALL,
        name=kernel.__name__,
    )(*pair, *weights, extra)


def expand(pair, weights, first_column, bias):
    out = jax.ShapeDtypeStruct((pair[0].shape[0], FF), BF)
    return inward_call(expand_kernel, pair, weights, first_column, FF, bias.reshape(1, FF), [out, out])


def sums_kernel(pixel_ref, out_ref):
    sums = [jnp.zeros((1, PIX), F32)] * 2
    for image in range(pixel_ref.shape[0]):
        values = pixel_ref[image].astype(F32)
        sums[0] = sums[0] + jnp.sum(values, axis=0, keepdims=True)
        sums[1] = sums[1] + jnp.sum(values * values, axis=0, keepdims=True)
    out_ref[...] = jnp.concatenate(sums, axis=0)


def column_sums(pixels):
    return pl.pallas_call(
        sums_kernel,
        out_shape=jax.ShapeDtypeStruct((2, PIX), F32),
        compiler_params=pltpu.CompilerParams(vmem_limit_bytes=20 * 2**20),
        cost_estimate=SMALL,
        name="column_sums",
    )(pixels)


def grid_spec():
    return pl.BlockSpec((1, 4, 1, QUART, DDEC), lambda i: (0, 0, i, 0, 0))


def pick_kernel(spot_ref, dy_ref, rows_ref, sums_ref, pieces_ref):
    spot = spot_ref[0]
    rows = jnp.zeros((VIS, DDEC), F32)
    sums = jnp.zeros((8, DDEC), F32)
    for quarter in range(4):
        place = lax.broadcasted_iota(jnp.int32, (VIS, QUART), 1) + quarter * QUART
        hot = (spot == place).astype(F32)
        values = dy_ref[0, quarter, 0]
        rows = rows + jnp.dot(hot.astype(BF), values, preferred_element_type=F32)
        vacant = 1.0 - jnp.sum(hot, axis=0, keepdims=True)
        weights = jnp.concatenate([jnp.ones_like(vacant), vacant, jnp.zeros((6, QUART), F32)], axis=0)
        sums = sums + jnp.dot(weights.astype(BF), values, preferred_element_type=F32)
    rows_ref[0] = rows.astype(BF)

    @pl.when(pl.program_id(0) == 0)
    def _():
        sums_ref[...] = jnp.zeros_like(sums_ref)

    sums_ref[...] += sums

    @pl.when(pl.program_id(0) == pl.num_programs(0) - 1)
    def _():
        rest = sums_ref[1:2]
        pieces = []
        for _ in range(3):
            pieces.append(rest.astype(BF))
            rest = rest - pieces[-1].astype(F32)
        zeros = jnp.zeros((5, DDEC), BF)
        pieces_ref[...] = jnp.concatenate(pieces + [zeros], axis=0)


def pick_rows(visible_in, grids):
    images = visible_in.shape[0]
    return pl.pallas_call(
        pick_kernel,
        grid=(images,),
        in_specs=[pl.BlockSpec((1, VIS, 1), lambda i: (i, 0, 0)), grid_spec()],
        out_specs=[
            pl.BlockSpec((1, VIS, DDEC), lambda i: (i, 0, 0)),
            pl.BlockSpec((8, DDEC), lambda i: (0, 0)),
            pl.BlockSpec((8, DDEC), lambda i: (0, 0)),
        ],
        out_shape=[
            jax.ShapeDtypeStruct((images, VIS, DDEC), BF),
            jax.ShapeDtypeStruct((8, DDEC), F32),
            jax.ShapeDtypeStruct((8, DDEC), BF),
        ],
        compiler_params=pltpu.CompilerParams(vmem_limit_bytes=20 * 2**20),
        cost_estimate=SMALL,
        name="pick_rows",
    )(visible_in[:, :, None], grids)


def place_kernel(scale_ref, spot_ref, rows_ref, table_ref, base_ref, out_ref):
    scale = scale_ref[pl.program_id(0)]
    spot = spot_ref[0]
    for quarter in range(4):
        place = lax.broadcasted_iota(jnp.int32, (QUART, VIS), 0) + quarter * QUART
        hot = (spot == place).astype(F32)
        vacant = jnp.sum(hot, axis=1, keepdims=True) < 0.5
        placed = jnp.dot(hot.astype(BF), rows_ref[0], preferred_element_type=F32)
        slot = lax.broadcasted_iota(jnp.int32, (QUART, 2 * NSCALE * SIDE), 1)
        place = lax.broadcasted_iota(jnp.int32, slot.shape, 0) + quarter * QUART
        line = lax.shift_right_logical(place * 1171, 14)
        row_at = scale * SIDE + line
        col_at = (NSCALE + scale) * SIDE + place - line * SIDE
        angle_at = ((slot == row_at) | (slot == col_at)).astype(F32).astype(BF)
        angle_at = jnp.concatenate([angle_at, angle_at], axis=1)
        empty = jnp.dot(angle_at, table_ref[...], preferred_element_type=F32) + base_ref[...]
        out_ref[0, quarter, 0] = jnp.where(vacant, empty, placed).astype(BF)


def place_rows(visible_in, scale_in, rows, table, base):
    images = visible_in.shape[0]
    return pl.pallas_call(
        place_kernel,
        grid_spec=pltpu.PrefetchScalarGridSpec(
            num_scalar_prefetch=1,
            grid=(images,),
            in_specs=[
                pl.BlockSpec((1, 1, VIS), lambda i, scale: (i, 0, 0)),
                pl.BlockSpec((1, VIS, DDEC), lambda i, scale: (i, 0, 0)),
                pl.BlockSpec(table.shape, lambda i, scale: (0, 0)),
                pl.BlockSpec((1, DDEC), lambda i, scale: (0, 0)),
            ],
            out_specs=pl.BlockSpec((1, 4, 1, QUART, DDEC), lambda i, scale: (0, 0, i, 0, 0)),
        ),
        out_shape=jax.ShapeDtypeStruct((1, 4, images, QUART, DDEC), BF),
        compiler_params=pltpu.CompilerParams(vmem_limit_bytes=20 * 2**20),
        cost_estimate=SMALL,
        name="place_rows",
    )(scale_in, visible_in[:, None, :], rows, table, base)


def local(
    pixels,
    visible,
    scale_index,
    cotangent,
    pe_weight,
    pe_first,
    pe_second,
    qkv_weight,
    qkv_first,
    qkv_second,
    out_weight,
    out_first,
    out_second,
    up_weight,
    up_first,
    up_second,
    down_weight,
    down_first,
    down_second,
    dec_weight,
    dec_first,
    dec_second,
    vectors,
    vec_first,
    vec_second,
):
    image_count = pixels.shape[0]
    row_count = image_count * VIS
    device_count = lax.axis_size(AXES)
    dp_count = lax.axis_size("dp")
    shard_rows = D // device_count
    routed = dp_count == 16 and device_count == 32
    item_count = 4 * image_count // dp_count
    whole_images = item_count == 4

    order = Order(vec_first)
    vec_length = vectors.shape[0]
    pe_rows = pe_weight.T.astype(BF)
    middle_rows = jnp.concatenate([out_weight.T, up_weight, dec_weight], axis=1).astype(BF)
    if routed:
        vec_low = jnp.pad(vectors.astype(BF), (0, 4 * SPAN - vec_length)).reshape(4, SPAN)
        vec_low = jnp.pad(vec_low, ((0, shard_rows - 4), (0, 0)))
        pe_gather = Gathering(jnp.concatenate([pe_rows, vec_low], axis=1), True, order)
        middle_gather = Gathering(middle_rows, False, order)
        qkv_gather = Gathering(qkv_weight.astype(BF), False, order)
        owners = block_order()
    stats = column_sums(order(pixels)).reshape(2, BANDS, PATCH * PATCH)
    stats = order(jnp.sum(stats, axis=2).reshape(2 * BANDS))
    if routed:
        pe_gather.first_turn()
        qkv_gather.middle()
        middle_gather.middle()
    if whole_images:
        marks = jnp.concatenate([visible, scale_index[:, None]], axis=1).astype(F32)
        marks = jnp.concatenate(
            [marks, jnp.broadcast_to(stats[None], (dp_count, 2 * BANDS))], axis=1
        )
        marks_in = lax.all_to_all(order(marks), "dp", split_axis=0, concat_axis=0, tiled=True)
        stats = jnp.sum(marks_in[:, -2 * BANDS :], axis=0)
        marks_in, stats = order(marks_in, stats + lax.ppermute(stats, "grp", core_pairs()))
    else:
        stats = lax.psum(stats, AXES)
    down_rows = order(down_weight).T.astype(BF)
    if routed:
        pe_gather.second_turn()
        down_gather = Gathering(down_rows, False, order)

    dp_index = lax.axis_index("dp")
    cotangent_rows = order(cotangent)
    if whole_images:
        image_order = marks_in[:, : -2 * BANDS].astype(jnp.int32)
        visible_in, scale_in = image_order[:, :VIS], image_order[:, VIS]
        dy_sent, dy_sums, vacant_low = order(*pick_rows(visible_in, cotangent_rows))
        dec_bias_grad, dy_vacant = dy_sums[0], dy_sums[1]
        dy_rows = lax.all_to_all(dy_sent, "dp", split_axis=0, concat_axis=0, tiled=True)
    spots, scale_rows = order(visible.reshape(row_count), jnp.repeat(scale_index, VIS))
    table = angle_pieces(D, 3)
    if routed:
        pe_gather.cores()
        table = table.reshape(-1, 32, shard_rows)
        table = jnp.einsum("pb,kbr->kpr", owners, table, preferred_element_type=F32).astype(BF)
        table = table.reshape(-1, D)
    hot = angle_hot(spots, scale_rows, 3)
    enc_table = order(*[forward_product(hot, part) for part in halves(table)])
    if routed:
        qkv_gather.first_turn()
    if routed:
        pe_pair = pe_gather.total()
        vector_all = jnp.concatenate([part[:, PIX:] for part in pe_pair])
        vector_all = vector_all.reshape(device_count, shard_rows, SPAN)[:, :4].reshape(device_count, -1)
        vector_all = jnp.einsum("pb,pv->bv", owners, vector_all, preferred_element_type=F32)
        vector_all = vector_all[:, :vec_length].reshape(-1)
    else:
        early = jnp.concatenate([pe_rows, qkv_weight.astype(BF)], axis=1)
        early_full = lax.all_gather(early, AXES, axis=0, tiled=True)
        middle_full = lax.all_gather(middle_rows, AXES, axis=0, tiled=True)
        down_full = lax.all_gather(down_rows, AXES, axis=0, tiled=True)
        vector_all = lax.all_gather(vectors.astype(BF), AXES, axis=0, tiled=True).astype(F32)
        pe_pair = (early_full[:HALF, :PIX], early_full[HALF:, :PIX])
        qkv_pair = (early_full[:HALF, PIX:], early_full[HALF:, PIX:])
        middle_pair = (middle_full[:HALF], middle_full[HALF:])
        down_pair = (down_full[:HALF], down_full[HALF:])

    entry_count = row_count * device_count * PATCH * PATCH
    band_mean = stats[:BANDS] / entry_count
    band_scale = lax.rsqrt(stats[BANDS:] / entry_count - band_mean * band_mean + EPS_NORM)
    scale_row = jnp.repeat(band_scale, PATCH * PATCH)[None]
    pixel_norm = pixels.reshape(row_count, PIX).astype(F32) - jnp.repeat(band_mean, PATCH * PATCH)[None]
    pixel_low = order((pixel_norm * scale_row).astype(BF))
    pieces, up_bias, dec_bias = split_vectors(vector_all)
    query_bias, value_bias = pieces[5], pieces[6]
    wide = jnp.stack(pieces[:5] + pieces[7:])
    if routed:
        wide = wide.astype(BF).reshape(8, 32, shard_rows)
        wide = jnp.einsum("pb,nbr->npr", owners, wide, preferred_element_type=F32).reshape(8, D)
    gain_one, shift_one, gain_two, shift_two, pe_bias, out_bias, down_bias, mask_token = [
        halves(wide[number]) for number in range(8)
    ]

    stream_in = outward(pixel_low, pe_pair, 0, PIX)
    stream_in = [part + bias + angle for part, bias, angle in zip(stream_in, pe_bias, enc_table)]
    norm_one, normed_one, inv_std_one = norm_forward(stream_in, gain_one, shift_one)
    norm_one = order(*norm_one)
    if routed:
        middle_gather.first_turn()
        down_gather.middle()
        qkv_gather.second_turn()
    if whole_images:
        dy_rows = order(dy_rows).reshape(row_count, DDEC)
    if routed:
        middle_gather.second_turn()
        qkv_gather.cores()
        qkv_pair = qkv_gather.total()
    norm_one = order(*norm_one)
    low_rows = jax.ShapeDtypeStruct((row_count, 3 * D), BF)
    qkv_bias = jnp.concatenate([query_bias, jnp.zeros_like(query_bias), value_bias])
    (projected,) = inward_call(
        shift_kernel, norm_one, qkv_pair, 0, 3 * D, qkv_bias.reshape(1, 3 * D), [low_rows]
    )
    projected = order(projected)
    mixture_low, peaks = order(*attend(projected))
    if routed:
        down_gather.first_turn()
        middle_gather.cores()
        middle_pair = middle_gather.total()
        down_gather.second_turn()
    mixture_low = order(mixture_low)
    UP, DEC = D, D + FF
    stream_mid = outward(mixture_low, middle_pair, 0, D)
    stream_mid = [part + more + bias for part, more, bias in zip(stream_in, stream_mid, out_bias)]
    norm_two, normed_two, inv_std_two = norm_forward(stream_mid, gain_two, shift_two)

    if whole_images:
        out_low = [part.astype(BF) for part in outward(dy_rows, middle_pair, DEC, DDEC)]
    else:
        placement = visible[:, :, None] == jnp.arange(GRID)[None, None, :]
        placement_low = placement.astype(BF)
        vacant = 1.0 - jnp.sum(placement.astype(F32), axis=1)
        grad_rows = cotangent_rows[0].reshape(-1, DDEC)
        dec_bias_grad = jnp.sum(grad_rows.astype(F32), axis=0)
        grid_grad = jnp.concatenate(outward(grad_rows, middle_pair, DEC, DDEC), axis=1)
        grid_grad = grid_grad.astype(BF).reshape(item_count, dp_count, QUART, D)
        returned = lax.all_to_all(
            grid_grad, "dp", split_axis=1, concat_axis=0, tiled=True
        ).reshape(image_count, GRID, D)
        out_low = jnp.einsum(
            "nvg,ngd->nvd", placement_low, returned, preferred_element_type=F32
        )
        out_low = halves(out_low.reshape(row_count, D).astype(BF))
        mask_grad = halves(
            jnp.einsum("ng,ngd->d", vacant.astype(BF), returned, preferred_element_type=F32)
        )
    out_grad_rows = [part.astype(F32) for part in out_low]

    out_low = order(*out_low)
    norm_two = order(*norm_two)
    activated, slope = order(*expand(norm_two, middle_pair, UP, up_bias))
    if routed:
        down_gather.cores()
        down_pair = down_gather.total()
    down_part = Reduction(product_of(order, (out_low, activated)), routed, order)
    down_part.cores()
    out_low = order(*out_low)
    hidden = jax.ShapeDtypeStruct((row_count, FF), BF)
    preact_low, up_bias_grad = order(
        *inward_call(
            slope_kernel,
            out_low,
            down_pair,
            0,
            FF,
            slope,
            [hidden, jax.ShapeDtypeStruct((1, FF), F32)],
        )
    )
    up_bias_grad = up_bias_grad[0]
    down_part.first_turn()
    activated = order(activated)
    stream_out = outward(activated, down_pair, 0, FF)
    stream_low = order(
        *[
            (part + more + bias).astype(BF)
            for part, more, bias in zip(stream_mid, stream_out, down_bias)
        ]
    )

    if not whole_images:
        full_grid = jnp.einsum(
            "nvg,nvd->ngd",
            placement_low,
            jnp.concatenate(stream_low, axis=1).reshape(image_count, VIS, D),
            preferred_element_type=F32,
        )
        full_grid = full_grid + vacant[:, :, None] * jnp.concatenate(mask_token)
        quarters = full_grid.astype(BF).reshape(4 * image_count, 1, QUART, D)
        ratio_image = jnp.power(2.0, scale_index.astype(F32) - 1.0)
        ratio_quarter = jnp.repeat(ratio_image, 4).reshape(4 * image_count, 1).astype(BF)
        received = lax.all_to_all(quarters, "dp", split_axis=0, concat_axis=1, tiled=True)
        received_ratio = lax.all_to_all(
            ratio_quarter, "dp", split_axis=0, concat_axis=1, tiled=True
        )
        quarter_id = dp_index * item_count + jnp.arange(item_count)
        position = (quarter_id % 4)[:, None] * QUART + jnp.arange(QUART)[None, :]
        scale_at = jnp.round(jnp.log2(received_ratio.astype(F32))).astype(jnp.int32) + 1
        full = (item_count, dp_count, QUART)
        dec_table = forward_product(
            angle_hot(
                jnp.broadcast_to(position[:, None, :], full).reshape(-1),
                jnp.broadcast_to(scale_at[:, :, None], full).reshape(-1),
                2,
            ),
            angle_pieces(DDEC, 2),
        )
        received = halves(received.reshape(-1, D))
        decoded = inward(received, middle_pair, DEC, DDEC) + dec_bias + dec_table
        decoded = decoded.astype(BF).reshape((1,) + full + (DDEC,))

    down_bias_grad = [jnp.sum(part, axis=0) for part in out_grad_rows]
    up_part = Reduction(product_of(order, (norm_two, preact_low)), routed, order)
    up_part.cores()
    down_part.second_turn()
    two_grad = outward(order(preact_low), middle_pair, UP, FF)
    mid_grad, gain_two_grad, shift_two_grad = norm_backward(
        two_grad, normed_two, inv_std_two, gain_two
    )
    mid_grad = [part + more for part, more in zip(mid_grad, out_grad_rows)]
    out_bias_grad = [jnp.sum(part, axis=0) for part in mid_grad]
    mid_low = order(*[part.astype(BF) for part in mid_grad])
    up_part.first_turn()
    down_part.along_z()
    mid_low = order(*mid_low)
    mixture_grad = order(inward(mid_low, middle_pair, 0, D).astype(BF))
    projected_low, attend_sums = order(*attend_back(projected, mixture_grad, peaks))
    query_bias_grad, value_bias_grad = attend_sums[0], attend_sums[1]
    down_shard = down_part.total()
    up_part.second_turn()
    qkv_part = Reduction(
        product_of(order, (mid_low, mixture_low), (norm_one, projected_low)), routed, order
    )
    qkv_part.cores()
    one_grad = outward(order(projected_low), qkv_pair, 0, 3 * D)
    in_grad, gain_one_grad, shift_one_grad = norm_backward(
        one_grad, normed_one, inv_std_one, gain_one
    )
    in_grad = [part + more for part, more in zip(in_grad, mid_grad)]
    pe_bias_grad = [jnp.sum(part, axis=0) for part in in_grad]
    in_low = order(*[part.astype(BF) for part in in_grad])
    qkv_part.first_turn()
    up_part.along_z()
    if whole_images:
        mask_grad = [
            jnp.sum(part, axis=0) for part in outward(order(vacant_low), middle_pair, DEC, DDEC)
        ]
    wide_grad = jnp.stack(
        [
            jnp.concatenate(pair)
            for pair in (
                gain_one_grad,
                shift_one_grad,
                gain_two_grad,
                shift_two_grad,
                pe_bias_grad,
                out_bias_grad,
                down_bias_grad,
                mask_grad,
            )
        ]
    )
    if routed:
        wide_grad = wide_grad.astype(BF).reshape(8, 32, shard_rows)
        wide_grad = jnp.einsum("pb,npr->nbr", owners, wide_grad, preferred_element_type=F32)
        wide_grad = wide_grad.reshape(8, D)
    vec_grad = jnp.concatenate(
        [
            wide_grad[:5].reshape(-1),
            query_bias_grad,
            value_bias_grad,
            wide_grad[5:].reshape(-1),
            up_bias_grad,
            dec_bias_grad,
        ]
    )
    if routed:
        vec_rows = jnp.pad(
            vec_grad.reshape(device_count, vec_length), ((0, 0), (0, 4 * SPAN - vec_length))
        )
        vec_rows = jnp.einsum("pb,bv->pv", owners, vec_rows.astype(BF), preferred_element_type=F32)
        vec_rows = vec_rows.reshape(device_count, 4, SPAN)
        vec_rows = jnp.pad(vec_rows, ((0, 0), (0, shard_rows - 4), (0, 0))).reshape(2, HALF, SPAN)

        def last_product(half, came):
            left, stream = order(in_low[half], stream_low[half])
            token = mask_token[half].reshape(HALF, 1)
            operands = (left, pixel_low, vec_rows[half], stream, dy_rows, token, dy_vacant[None])
            return last_call(operands, came)

    else:

        def last_product(half, came):
            return jnp.concatenate(
                [
                    weight_product(in_low[half], pixel_low),
                    weight_product(received[half], grad_rows),
                ],
                axis=1,
            ).astype(BF)

    pe_part = Reduction(last_product, routed, order)
    pe_part.cores()
    (norm_grad,) = inward_call(
        scale_kernel,
        order(*in_low),
        pe_pair,
        0,
        PIX,
        scale_row,
        [jax.ShapeDtypeStruct((row_count, PIX), F32)],
        256,
    )
    norm_grad = order(norm_grad)
    pe_part.first_turn()
    qkv_part.join(pe_part)
    qkv_part.second_turn()
    if whole_images:
        dec_pieces = angle_pieces(DDEC, 2)
        vis_table = forward_product(angle_hot(spots, scale_rows, 2), dec_pieces)
        vis_rows = inward(order(*stream_low), middle_pair, DEC, DDEC) + dec_bias + vis_table
        vis_rows = order(vis_rows.astype(BF).reshape(image_count, VIS, DDEC))
        vis_in = lax.all_to_all(vis_rows, "dp", split_axis=0, concat_axis=0, tiled=True)
        tokens = [jnp.broadcast_to(part.astype(BF), (8, HALF)) for part in mask_token]
        mask_rows = inward(tokens, middle_pair, DEC, DDEC)[:1] + dec_bias
    up_shard = up_part.total()
    qkv_part.along_z()
    pixel_grad = order(norm_grad).reshape(image_count, VIS, PIX)
    if whole_images:
        decoded = order(place_rows(visible_in, scale_in, order(vis_in), dec_pieces, mask_rows))
    last_total = qkv_part.total()
    out_shard, qkv_shard = last_total[:, :D], last_total[:, D : 4 * D]
    pe_shard, dec_shard = last_total[:, 4 * D : 4 * D + PIX], last_total[:, -DDEC:]
    if routed:
        vec_shard = last_total[:4, 4 * D + PIX : 4 * D + PIX + SPAN].reshape(-1)[:vec_length]
    else:
        vec_shard = lax.psum_scatter(vec_grad, AXES, scatter_dimension=0, tiled=True)
    shards = (pe_shard, qkv_shard, out_shard, up_shard, down_shard, dec_shard, vec_shard)
    parts = (last_total, up_shard, down_shard) if routed else shards
    local_squares = sum((jnp.sum(gradient * gradient) for gradient in parts))
    squares = tiny_sum(local_squares.reshape(1), routed)[0]
    grad_norm = jnp.sqrt(squares)
    vec_first = order.token
    clip_factor = jnp.minimum(1.0, CLIP_LEVEL / grad_norm)
    params = (pe_weight, qkv_weight, out_weight, up_weight, down_weight, dec_weight, vectors)
    firsts = (pe_first, qkv_first, out_first, up_first, down_first, dec_first, vec_first)
    seconds = (pe_second, qkv_second, out_second, up_second, down_second, dec_second, vec_second)
    results = []
    for number in range(7):
        step_rate = LR_VECTOR if number == 6 else LR_MATRIX
        decay_rate = 0.0 if number == 6 else DECAY_MATRIX
        gradient = shards[number].T if number in (0, 2, 4) else shards[number]
        results.extend(
            adamw_update(
                params[number],
                firsts[number],
                seconds[number],
                gradient * clip_factor,
                step_rate,
                decay_rate,
            )
        )
    return (decoded, pixel_grad, *results, grad_norm)


def solution(mesh):
    rows = P(AXES, None)
    cols = P(None, AXES)
    vecs = P(AXES)
    images = P(AXES, None, None)
    grids = P("grp", "dp", None, None, None)
    states = (cols,) * 3 + (rows,) * 3 + (cols,) * 3 + (rows,) * 3 + (cols,) * 3 + (rows,) * 3
    states = states + (vecs,) * 3
    return jax.shard_map(
        local,
        mesh=mesh,
        in_specs=(images, rows, vecs, grids) + states,
        out_specs=(grids, images) + states + (P(),),
        check_vma=False,
    )
```

time: 565 us -> 554 us (0.981)
  Pallas kernels: 52 us -> 141 us
  matrix products: 133 us -> 71.2 us
  waiting for transfers between devices: 132 us -> 108 us
  local copies, waits for them, and re-layouts: 38.4 us -> 55.2 us
  between operations: 25 us -> 10.3 us
  other arithmetic: 81.5 us -> 69.3 us
    pallas_call x1 -> x15, Pallas kernels: 22.9 us -> 112 us  [the longest x6 45.3 us: weight_call(): pl.pallas_call(functools.partial(weight_kernel, tuple(edges), int(came is...]
    dot_general x16 -> x5, matrix products: 57.4 us -> 1.28 us  [the longest x1 0.41 us: local(): jnp.einsum('pb,kbr->kpr', owners, table, preferred_element_type=F32)]
    all_to_all x3, waiting for transfers between devices: 33.3 us -> 1.12 us  [the longest x1 1.11 us: local(): lax.all_to_all(dy_sent, 'dp', split_axis=0, concat_axis=0, tiled=True)]
    dot_general x11 -> x10, matrix products: 31.4 us -> 17.1 us  [forward_product(): return jnp.dot(left, right, preferred_element_type=F32)]
    concatenate x16 -> x26, other arithmetic: 11.3 us -> 24.7 us  [the longest x15 23.6 us: grow(): self.held = self.order(jnp.concatenate([held] + self.near))]
    unnamed x188 -> x305, local copies, waits for them, and re-layouts: 18.9 us -> 28.6 us
    reduce_sum x16 -> x8, other arithmetic: 17 us -> 7.51 us  [the longest x3 2.25 us: local(): local_squares = sum((jnp.sum(gradient * gradient) for gradient in parts))]
    dot_general x7 -> x14, matrix products: 44.3 us -> 52.8 us  [back_product(): lax.dot_general(left, right, (((1,), (1,)), ((), ())), preferred_element_...]
  transfers between devices with their start and end apart: 41 -> 52, of which waited for: 19 -> 19; matrix products, arithmetic and copies ran while one was open for 33% -> 27% of each run, Pallas kernels for 5% -> 23%
where the time goes in v3:
time: 554 us; the launch traced here: 546 us
  Pallas kernels  141 us (25%)
  waiting for transfers between devices  108 us (19%)
  starting transfers between devices  90.3 us (16%)
  matrix products  71.2 us (13%)
  other arithmetic  69.3 us (13%)
  local copies, waits for them, and re-layouts  55.2 us (10%)
  between operations  10.3 us (2%)
    dot_general x14, matrix products, back_product(): lax.dot_general(left, right, (((1,), (1,)), ((), ())), preferred_element_...  52.8 us
    pallas_call x6, Pallas kernels, weight_call(): pl.pallas_call(functools.partial(weight_kernel, tuple(edges), int(came is...  45.3 us
    pallas_call x4, Pallas kernels, inward_call(): pl.pallas_call(kernel, grid=(columns // width,), in_specs=[whole, whole,...  45 us
    ppermute x4, waiting for transfers between devices, first_turn(): self.near = [lax.ppermute(self.grow(), AXES, turn_pairs(2, 1))]  37.6 us
    unnamed x305, local copies, waits for them, and re-layouts  28.6 us
    concatenate x15, other arithmetic, grow(): self.held = self.order(jnp.concatenate([held] + self.near))  23.6 us
    ppermute x6, starting transfers between devices, tiny_sum(): lax.ppermute(value, 'dp', dp_pairs(unit * k))  20.8 us
    pallas_call x1, Pallas kernels, attend_back(): pl.pallas_call(attend_back_kernel, grid=(pairs,), in_specs=[block(0), blo...  20.3 us
  transfers between devices with their start and end apart: 52, of which 19 were waited for; matrix products, arithmetic and copies ran while one was open for 27% of the time, Pallas kernels for 23%

profile of v3, /device:TPU:0, one launch (start us, length us, event | category | flops | bytes accessed | tf_op | source)
XLA Modules:
  0.0 545.6 jit_solution(15625260613163934887)
XLA Ops:
  19.7 5.8 %collective-permute-done.4 = bf16[32,5632]{1,0:T(8,128)(2,1)S(1)} collective-permute-done((bf16[32,5632]{1,0:T(8,128)(2,1)S(1)}, bf16[32,5632]{1,0:T(8,128)(2,1)S(1)}, u32[]{:S(2)}, u32[]{:S(2)}) %collective-permute-start.4) | collective-permute-done | bytes 360480 | tf_op jit(solution)/shard_map/ppermute | solution.py:186
  26.4 6.2 %all-to-all-start = ((f32[16,1,56]{2,1,0:T(1,128)}), f32[16,1,56]{2,1,0:T(1,128)S(1)}, u32[]{:S(2)}, u32[]{:S(2)}) async-start(f32[16,1,56]{2,1,0:T(1,128)} %bitcast.4), calls=%async_computation | async-start | bytes 16384 | tf_op jit(solution)/shard_map/all_to_all | solution.py:748
  44.9 5.6 %copy.82.dy_ref = bf16[1,4,16,49,512]{4,3,2,1,0:T(8,128)(2,1)} copy(bf16[1,4,16,49,512]{4,2,3,1,0:T(8,128)(2,1)} %param.30) | data formatting | bytes 6422528 | tf_op jit(solution)/shard_map/optimization_barrier | solution.py:161
  52.8 8.0 %pick_rows.1 = (bf16[16,49,512]{2,1,0:T(8,128)(2,1)}, f32[8,512]{1,0:T(8,128)S(1)}, bf16[8,512]{1,0:T(8,128)(2,1)S(1)}) custom-call(s32[16,49,1]{2,1,0:T(8,128)S(1)} %copy.81.spot_ref, bf16[1,4,16,49,512]{4,3,2,1,0:T(8,128)(2,1)S(1)} %copy-done.3), custom_call_target="tpu_custom_call" | custom-call | flops 1000000 | bytes 100000 | tf_op jit(solution)/shard_map/pick_rows/pallas_call | solution.py:629
  73.9 6.1 %all-to-all-start.1 = ((bf16[16,49,512]{2,1,0:T(8,128)(2,1)}), bf16[16,49,512]{2,1,0:T(8,128)(2,1)}, u32[]{:S(2)}, u32[]{:S(2)}) async-start(bf16[16,49,512]{2,1,0:T(8,128)(2,1)} %get-tuple-element.365), calls=%async_computation.1 | async-start | bytes 1835008 | tf_op jit(solution)/shard_map/all_to_all | solution.py:765
  109.5 28.5 %collective-permute-done.13 = bf16[128,5632]{1,0:T(8,128)(2,1)} collective-permute-done((bf16[128,5632]{1,0:T(8,128)(2,1)}, bf16[128,5632]{1,0:T(8,128)(2,1)}, u32[]{:S(2)}, u32[]{:S(2)}) %collective-permute-start.13) | collective-permute-done | bytes 1441824 | tf_op jit(solution)/shard_map/ppermute | solution.py:197
  147.4 6.8 %shift_kernel.1.q_ref.k_ref.v_ref = bf16[784,3072]{1,0:T(8,128)(2,1)S(1)} custom-call(bf16[784,512]{1,0:T(8,128)(2,1)S(1)} %get-tuple-element.491.near_ref.refs_2_, bf16[784,512]{1,0:T(8,128)(2,1)S(1)} %get-tuple-element.484.far_ref.refs_2_, bf16[512,3072]{1,0:T(8,128)(2,1)S(1)} %pad_maximum_fusion.2.near_w_ref, ...), custom_call_target="tpu_custom_call" | custom-call | flops 1000000 | bytes 100000 | tf_op jit(solution)/shard_map/shift_kernel/pallas_call | solution.py:556
  154.3 9.2 %attend.1 = (bf16[784,1024]{1,0:T(8,128)(2,1)S(1)}, f32[8,8,256]{2,1,0:T(8,128)S(1)}) custom-call(bf16[784,3072]{1,0:T(8,128)(2,1)S(1)} %shift_kernel.1.q_ref.k_ref.v_ref, bf16[784,3072]{1,0:T(8,128)(2,1)S(1)} %shift_kernel.1.q_ref.k_ref.v_ref, bf16[784,3072]{1,0:T(8,128)(2,1)S(1)} %shift_kernel.1.q_ref.k_ref.v_ref), custom_call_target="tpu_custom_call" | custom-call | flops 1000000 | bytes 100000 | tf_op jit(solution)/shard_map/attend/pallas_call | solution.py:417
  163.5 5.7 %collective-permute-done.16 = bf16[64,4096]{1,0:T(8,128)(2,1)S(1)} collective-permute-done((bf16[64,4096]{1,0:T(8,128)(2,1)S(1)}, bf16[64,4096]{1,0:T(8,128)(2,1)S(1)}, u32[]{:S(2)}, u32[]{:S(2)}) %collective-permute-start.16) | collective-permute-done | bytes 524320 | tf_op jit(solution)/shard_map/ppermute | solution.py:194
  170.3 6.0 %collective-permute-done.17 = bf16[256,5632]{1,0:T(8,128)(2,1)S(1)} collective-permute-done((bf16[256,5632]{1,0:T(8,128)(2,1)S(1)}, bf16[256,5632]{1,0:T(8,128)(2,1)S(1)}, u32[]{:S(2)}, u32[]{:S(2)}) %collective-permute-start.17) | collective-permute-done | bytes 2883616 | tf_op jit(solution)/shard_map/ppermute | solution.py:200
  185.2 9.1 %collective-permute-done.18 = bf16[128,4096]{1,0:T(8,128)(2,1)} collective-permute-done((bf16[128,4096]{1,0:T(8,128)(2,1)}, bf16[128,4096]{1,0:T(8,128)(2,1)}, u32[]{:S(2)}, u32[]{:S(2)}) %collective-permute-start.18) | collective-permute-done | bytes 1048608 | tf_op jit(solution)/shard_map/ppermute | solution.py:197
  206.3 22.9 %expand_kernel.1 = (bf16[784,4096]{1,0:T(8,128)(2,1)}, bf16[784,4096]{1,0:T(8,128)(2,1)}) custom-call(bf16[784,512]{1,0:T(8,128)(2,1)S(1)} %get-tuple-element.451.near_ref.refs_0_, bf16[784,512]{1,0:T(8,128)(2,1)S(1)} %get-tuple-element.438.far_ref.refs_0_, bf16[512,5632]{1,0:T(8,128)(2,1)} %pad_maximum_fusion.near_w_ref, ...), custom_call_target="tpu_custom_call" | custom-call | flops 1000000 | bytes 100000 | tf_op jit(solution)/shard_map/expand_kernel/pallas_call | solution.py:556
  233.6 6.8 %weight_product.6 = bf16[512,4096]{1,0:T(8,128)(2,1)} custom-call(bf16[784,512]{1,0:T(8,128)(2,1)S(1)} %get-tuple-element.418.refs_0_.far_ref, bf16[784,4096]{1,0:T(8,128)(2,1)S(1)} %copy-done.1), custom_call_target="tpu_custom_call" | custom-call | flops 1000000 | bytes 100000 | tf_op jit(solution)/shard_map/weight_product/pallas_call | solution.py:303
  243.2 13.1 %slope_kernel.1 = (bf16[784,4096]{1,0:T(8,128)(2,1)}, f32[1,4096]{1,0:T(1,128)S(1)}) custom-call(bf16[784,512]{1,0:T(8,128)(2,1)S(1)} %copy-done.22, bf16[784,512]{1,0:T(8,128)(2,1)S(1)} %copy-done.25, bf16[512,4096]{1,0:T(8,128)(2,1)} %pad_maximum_fusion.1.near_w_ref, bf16[512,4096]{1,0:T(8,128)(2,1)} %collective-permute-done.21.far_w_ref, ...), custom_call_target="tpu_custom_call" | custom-call | flops 1000000 | bytes 100000 | tf_op jit(solution)/shard_map/slope_kernel/pallas_call | solution.py:556
  256.3 8.7 %weight_product.7 = (bf16[256,4096]{1,0:T(8,128)(2,1)S(1)}, bf16[256,4096]{1,0:T(8,128)(2,1)}) custom-call(bf16[784,512]{1,0:T(8,128)(2,1)S(1)} %copy-done.22, bf16[784,4096]{1,0:T(8,128)(2,1)} %get-tuple-element.431.refs_1_, bf16[512,4096]{1,0:T(8,128)(2,1)} %collective-permute-done.22.refs_2_), custom_call_target="tpu_custom_call" | custom-call | flops 1000000 | bytes 100000 | tf_op jit(solution)/shard_map/weight_product/pallas_call | solution.py:303
  267.4 6.8 %add_convert_fusion.8.stream_ref = bf16[784,512]{1,0:T(8,128)(2,1)} fusion(f32[784,512]{1,0:T(8,128)S(1)} %copy-done.51, bf16[784,4096]{1,0:T(8,128)(2,1)S(1)} %bitcast.99, bf16[512,4096]{1,0:T(8,128)(2,1)} %pad_maximum_fusion.1.near_w_ref, f32[512]{0:T(512)S(1)} %add.605), kind=kOutput, calls=%fused_computation.33 | convolution fusion | flops 3289538560 | bytes 13027328 | tf_op jit(solution)/shard_map/dot_general | solution.py:46
  274.1 6.7 %add_convert_fusion.7.stream_ref = bf16[784,512]{1,0:T(8,128)(2,1)} fusion(f32[784,512]{1,0:T(8,128)S(1)} %copy-done.54, bf16[784,4096]{1,0:T(8,128)(2,1)S(1)} %bitcast.99, bf16[512,4096]{1,0:T(8,128)(2,1)} %collective-permute-done.21.far_w_ref, f32[512]{0:T(512)S(1)} %add.609), kind=kOutput, calls=%fused_computation.32 | convolution fusion | flops 3289538560 | bytes 13027328 | tf_op jit(solution)/shard_map/dot_general | solution.py:46
  280.9 6.8 %weight_product.8 = bf16[512,4096]{1,0:T(8,128)(2,1)} custom-call(bf16[784,512]{1,0:T(8,128)(2,1)S(1)} %copy-done.17, bf16[784,4096]{1,0:T(8,128)(2,1)S(1)} %bitcast.95), custom_call_target="tpu_custom_call" | custom-call | flops 1000000 | bytes 100000 | tf_op jit(solution)/shard_map/weight_product/pallas_call | solution.py:303
  296.7 7.7 %fusion.2 = f32[784,512]{1,0:T(8,128)S(1)} fusion(bf16[784,4096]{1,0:T(8,128)(2,1)} %get-tuple-element.445.refs_1_, bf16[512,5632]{1,0:T(8,128)(2,1)} %pad_maximum_fusion.near_w_ref), kind=kOutput, calls=%fused_computation.4 | convolution fusion | flops 3288334336 | bytes 12222464 | tf_op jit(solution)/shard_map/dot_general | solution.py:46
  304.5 7.0 %multiply_reduce_fusion = (bf16[512]{0:T(512)(128)(2,1)}, f32[784]{0:T(1024)S(1)}, f32[784]{0:T(1024)S(1)}, bf16[512]{0:T(512)(128)(2,1)}, bf16[512]{0:T(512)(12...) fusion(f32[784,512]{1,0:T(8,128)S(1)} %copy-done.55, ...), kind=kOutput, calls=%fused_computation.20 | convolution fusion | flops 3295554560 | bytes 17066368 | tf_op jit(solution)/shard_map/dot_general | solution.py:46
  315.3 7.6 %weight_product.9 = (bf16[256,4096]{1,0:T(8,128)(2,1)S(1)}, bf16[256,4096]{1,0:T(8,128)(2,1)S(1)}) custom-call(bf16[784,512]{1,0:T(8,128)(2,1)S(1)} %get-tuple-element.451.near_ref.refs_0_, bf16[784,4096]{1,0:T(8,128)(2,1)} %get-tuple-element.445.refs_1_, bf16[512,4096]{1,0:T(8,128)(2,1)} %collective-permute-done.24.refs_2_), custom_call_target="tpu_custom_call" | custom-call | flops 1000000 | bytes 100000 | tf_op jit(solution)/shard_map/weight_product/pallas_call | solution.py:303
  323.6 5.5 collective-permute-start.27
  333.5 20.3 %attend_back.1 = (bf16[784,3072]{1,0:T(8,128)(2,1)S(1)}, f32[8,1024]{1,0:T(8,128)S(1)}) custom-call(bf16[784,3072]{1,0:T(8,128)(2,1)S(1)} %bitcast.93, bf16[784,3072]{1,0:T(8,128)(2,1)S(1)} %bitcast.93, bf16[784,3072]{1,0:T(8,128)(2,1)S(1)} %bitcast.93, bf16[784,1024]{1,0:T(8,128)(2,1)S(1)} %add_convert_fusion.mix_ref, ...), custom_call_target="tpu_custom_call" | custom-call | flops 1000000 | bytes 100000 | tf_op jit(solution)/shard_map/attend_back/pallas_call | solution.py:473
  359.4 6.6 %weight_product.10 = bf16[512,4096]{1,0:T(8,128)(2,1)} custom-call(bf16[784,512]{1,0:T(8,128)(2,1)S(1)} %convert_element_type.347.refs_0_, bf16[784,1024]{1,0:T(8,128)(2,1)S(1)} %copy-done.28, bf16[784,512]{1,0:T(8,128)(2,1)S(1)} %copy-done.15, bf16[784,3072]{1,0:T(8,128)(2,1)S(1)} %get-tuple-element.487.refs_3_), custom_call_target="tpu_custom_call" | custom-call | flops 1000000 | bytes 100000 | tf_op jit(solution)/shard_map/weight_product/pallas_call | solution.py:303
  383.4 8.8 %weight_product.11 = (bf16[256,4096]{1,0:T(8,128)(2,1)S(1)}, bf16[256,4096]{1,0:T(8,128)(2,1)}) custom-call(bf16[784,512]{1,0:T(8,128)(2,1)S(1)} %copy-done.9, bf16[784,1024]{1,0:T(8,128)(2,1)S(1)} %copy-done.29, bf16[784,512]{1,0:T(8,128)(2,1)S(1)} %copy-done.13, bf16[784,3072]{1,0:T(8,128)(2,1)} %copy-done.2, bf16[512,4096]{1,0:T(8,128)(2,1)} %collective-permute-done.30.refs_4_), custom_call_target="tpu_custom_call" | custom-call | flops 1000000 | bytes 100000 | tf_op jit(solution)/shard_map/weight_product/pallas_call | solution.py:303
  433.7 5.9 %collective-permute-done.34 = bf16[256,1408]{1,0:T(8,128)(2,1)S(1)} collective-permute-done((bf16[256,1408]{1,0:T(8,128)(2,1)S(1)}, bf16[256,1408]{1,0:T(8,128)(2,1)S(1)}, u32[]{:S(2)}, u32[]{:S(2)}) %collective-permute-start.34) | collective-permute-done | bytes 720928 | tf_op jit(solution)/shard_map/ppermute | solution.py:221
  449.8 6.6 %all-to-all-start.2 = ((bf16[16,49,512]{2,1,0:T(8,128)(2,1)}), bf16[16,49,512]{2,1,0:T(8,128)(2,1)S(1)}, u32[]{:S(2)}, u32[]{:S(2)}) async-start(bf16[16,49,512]{2,1,0:T(8,128)(2,1)} %reshape.419), calls=%async_computation.2 | async-start | bytes 1835008 | tf_op jit(solution)/shard_map/all_to_all | solution.py:1039
  456.5 9.8 %collective-permute-done.38 = bf16[128,5504]{1,0:T(8,128)(2,1)} collective-permute-done((bf16[128,5504]{1,0:T(8,128)(2,1)}, bf16[128,5504]{1,0:T(8,128)(2,1)}, u32[]{:S(2)}, u32[]{:S(2)}) %collective-permute-start.38) | collective-permute-done | bytes 1409056 | tf_op jit(solution)/shard_map/ppermute | solution.py:232
  469.3 5.9 %collective-permute-start.40 = (bf16[32,5504]{1,0:T(8,128)(2,1)}, bf16[32,5504]{1,0:T(8,128)(2,1)}, u32[]{:S(2)}, u32[]{:S(2)}) collective-permute-start(bf16[32,5504]{1,0:T(8,128)(2,1)} %get-tuple-element.559), channel_id=1, source_target_pairs={{0,8},{1,9},{2,10},{3,11},{4,12},{5,13},{6,14},{7,15},{8,0},{9,1},... | collective-permute-start | bytes 1056776 | tf_op jit(solution)/shard_map/ppermute | solution.py:239
  482.3 7.2 %place_rows.1 = bf16[1,4,16,49,512]{4,3,2,1,0:T(8,128)(2,1)S(1)} custom-call(s32[16]{0:T(128)S(1)} %slice_reduce_fusion.scale_ref, s32[16,1,49]{2,1,0:T(1,128)S(1)} %bitcast.106, bf16[16,49,512]{2,1,0:T(8,128)(2,1)S(1)} %all-to-all-done.2.rows_ref, bf16[224,512]{1,0:T(8,128)(2,1)S(1)} %copy-done.43, f32[1,512]{1,0:T(1,128)S(1)} %fusion.65.base_ref), custom_call_target="tpu_custom_call" | custom-call | flops 1000000 | bytes 100000 | tf_op jit(solution)/shard_map/place_rows/pallas_call | solution.py:670
  492.5 9.6 %collective-permute-done.40 = bf16[32,5504]{1,0:T(8,128)(2,1)} collective-permute-done((bf16[32,5504]{1,0:T(8,128)(2,1)}, bf16[32,5504]{1,0:T(8,128)(2,1)}, u32[]{:S(2)}, u32[]{:S(2)}) %collective-permute-start.40) | collective-permute-done | bytes 352288 | tf_op jit(solution)/shard_map/ppermute | solution.py:239
  517.1 8.3 %collective-permute-start.46 = (f32[1]{0:T(128)}, f32[1]{0:T(128)}, u32[]{:S(2)}, u32[]{:S(2)}) collective-permute-start(f32[1]{0:T(128)} %add.658), channel_id=1, source_target_pairs={{0,8},{1,9},{2,10},{3,11},{4,12},{5,13},{6,14},{7,15},{8,0},{9,1},... | collective-permute-start | bytes 20 | tf_op jit(solution)/shard_map/ppermute | solution.py:151
  (604 shorter events, 249.7 us)
Async XLA Ops:
  15.7 27.3 %collective-permute-start.6 = (bf16[128,896]{1,0:T(8,128)(2,1)}, bf16[128,896]{1,0:T(8,128)(2,1)}, u32[]{:S(2)}, u32[]{:S(2)}) collective-permute-start(bf16[128,896]{1,0:T(8,128)(2,1)} %pad_maximum_fusion.20), channel_id=1, source_target_pairs={{0,2},{1,3},{2,0},{3,1},{4,6},{5,7},{6,4},{7,5},{8,10},{9,11},{10,... | collective-permute-start | bytes 688136 | tf_op jit(solution)/shard_map/ppermute | solution.py:197
  38.9 43.2 %collective-permute-start.8 = (bf16[64,3072]{1,0:T(8,128)(2,1)}, bf16[64,3072]{1,0:T(8,128)(2,1)}, u32[]{:S(2)}, u32[]{:S(2)}) collective-permute-start(bf16[64,3072]{1,0:T(8,128)(2,1)} %pad_maximum_fusion.17), channel_id=1, source_target_pairs={{0,8},{1,9},{2,10},{3,11},{4,12},{5,13},{6,14},{7,15},{8,0},{9,1},... | collective-permute-start | bytes 1179656 | tf_op jit(solution)/shard_map/ppermute | solution.py:194
  41.7 57.8 %collective-permute-start.10 = (bf16[64,5632]{1,0:T(8,128)(2,1)}, bf16[64,5632]{1,0:T(8,128)(2,1)}, u32[]{:S(2)}, u32[]{:S(2)}) collective-permute-start(bf16[64,5632]{1,0:T(8,128)(2,1)} %pad_maximum_fusion.11), channel_id=1, source_target_pairs={{0,8},{1,9},{2,10},{3,11},{4,12},{5,13},{6,14},{7,15},{8,0},{9,1},... | collective-permute-start | bytes 2162696 | tf_op jit(solution)/shard_map/ppermute | solution.py:194
  69.4 17.0 %collective-permute-start.9 = (bf16[512,896]{1,0:T(8,128)(2,1)S(1)}, bf16[512,896]{1,0:T(8,128)(2,1)S(1)}, u32[]{:S(2)}, u32[]{:S(2)}) collective-permute-start(bf16[512,896]{1,0:T(8,128)(2,1)S(1)} %pad_maximum_fusion.9.near_w_ref), channel_id=1, source_target_pairs={{0,16},{16,0},{1,17},{17,1},{2,18},{18,2},{3,19},{19,3},{4,20},{20... | collective-permute-start | bytes 2752520 | tf_op jit(solution)/shard_map/ppermute | solution.py:203
  72.0 31.5 %collective-permute-start.11 = (bf16[32,4096]{1,0:T(8,128)(2,1)}, bf16[32,4096]{1,0:T(8,128)(2,1)}, u32[]{:S(2)}, u32[]{:S(2)}) collective-permute-start(bf16[32,4096]{1,0:T(8,128)(2,1)} %convert_bitcast_fusion), channel_id=1, source_target_pairs={{0,4},{1,5},{2,6},{3,7},{4,0},{5,1},{6,2},{7,3},{8,12},{9,13},{10,... | collective-permute-start | bytes 786440 | tf_op jit(solution)/shard_map/ppermute | solution.py:186
  73.9 35.5 %all-to-all-start.1 = ((bf16[16,49,512]{2,1,0:T(8,128)(2,1)}), bf16[16,49,512]{2,1,0:T(8,128)(2,1)}, u32[]{:S(2)}, u32[]{:S(2)}) async-start(bf16[16,49,512]{2,1,0:T(8,128)(2,1)} %get-tuple-element.365), calls=%async_computation.1 | async-start | bytes 1835008 | tf_op jit(solution)/shard_map/all_to_all | solution.py:765
  84.4 21.0 %collective-permute-start.12 = (bf16[128,3072]{1,0:T(8,128)(2,1)}, bf16[128,3072]{1,0:T(8,128)(2,1)}, u32[]{:S(2)}, u32[]{:S(2)}) collective-permute-start(bf16[128,3072]{1,0:T(8,128)(2,1)} %pad_maximum_fusion.10), channel_id=1, source_target_pairs={{0,2},{1,3},{2,0},{3,1},{4,6},{5,7},{6,4},{7,5},{8,10},{9,11},{10,... | collective-permute-start | bytes 2359304 | tf_op jit(solution)/shard_map/ppermute | solution.py:197
  102.0 36.0 %collective-permute-start.13 = (bf16[128,5632]{1,0:T(8,128)(2,1)}, bf16[128,5632]{1,0:T(8,128)(2,1)}, u32[]{:S(2)}, u32[]{:S(2)}) collective-permute-start(bf16[128,5632]{1,0:T(8,128)(2,1)} %pad_maximum_fusion.7), channel_id=1, source_target_pairs={{0,2},{1,3},{2,0},{3,1},{4,6},{5,7},{6,4},{7,5},{8,10},{9,11},{10,... | collective-permute-start | bytes 4325384 | tf_op jit(solution)/shard_map/ppermute | solution.py:197
  106.8 33.2 %collective-permute-start.14 = (bf16[256,3072]{1,0:T(8,128)(2,1)S(1)}, bf16[256,3072]{1,0:T(8,128)(2,1)}, u32[]{:S(2)}, u32[]{:S(2)}) collective-permute-start(bf16[256,3072]{1,0:T(8,128)(2,1)S(1)} %pad_maximum_fusion.6), channel_id=1, source_target_pairs={{0,1},{1,0},{2,3},{3,2},{4,5},{5,4},{6,7},{7,6},{8,9},{9,8},{10,11... | collective-permute-start | bytes 4718600 | tf_op jit(solution)/shard_map/ppermute | solution.py:200
  141.8 34.5 %collective-permute-start.17 = (bf16[256,5632]{1,0:T(8,128)(2,1)S(1)}, bf16[256,5632]{1,0:T(8,128)(2,1)S(1)}, u32[]{:S(2)}, u32[]{:S(2)}) collective-permute-start(bf16[256,5632]{1,0:T(8,128)(2,1)S(1)} %pad_maximum_fusion.3), channel_id=1, source_target_pairs={{0,1},{1,0},{2,3},{3,2},{4,5},{5,4},{6,7},{7,6},{8,9},{9,8},{10,11... | collective-permute-start | bytes 8650760 | tf_op jit(solution)/shard_map/ppermute | solution.py:200
  142.9 26.3 %collective-permute-start.16 = (bf16[64,4096]{1,0:T(8,128)(2,1)S(1)}, bf16[64,4096]{1,0:T(8,128)(2,1)S(1)}, u32[]{:S(2)}, u32[]{:S(2)}) collective-permute-start(bf16[64,4096]{1,0:T(8,128)(2,1)S(1)} %copy-done.71), channel_id=1, source_target_pairs={{0,8},{1,9},{2,10},{3,11},{4,12},{5,13},{6,14},{7,15},{8,0},{9,1},... | collective-permute-start | bytes 1572872 | tf_op jit(solution)/shard_map/ppermute | solution.py:194
  179.2 20.4 %collective-permute-start.19 = (bf16[512,5632]{1,0:T(8,128)(2,1)}, bf16[512,5632]{1,0:T(8,128)(2,1)}, u32[]{:S(2)}, u32[]{:S(2)}) collective-permute-start(bf16[512,5632]{1,0:T(8,128)(2,1)} %pad_maximum_fusion.near_w_ref), channel_id=1, source_target_pairs={{0,16},{16,0},{1,17},{17,1},{2,18},{18,2},{3,19},{19,3},{4,20},{20... | collective-permute-start | bytes 17301512 | tf_op jit(solution)/shard_map/ppermute | solution.py:203
  196.1 33.2 %collective-permute-start.20 = (bf16[256,4096]{1,0:T(8,128)(2,1)S(1)}, bf16[256,4096]{1,0:T(8,128)(2,1)S(1)}, u32[]{:S(2)}, u32[]{:S(2)}) collective-permute-start(bf16[256,4096]{1,0:T(8,128)(2,1)S(1)} %pad_maximum_fusion.5), channel_id=1, source_target_pairs={{0,1},{1,0},{2,3},{3,2},{4,5},{5,4},{6,7},{7,6},{8,9},{9,8},{10,11... | collective-permute-start | bytes 6291464 | tf_op jit(solution)/shard_map/ppermute | solution.py:200
  266.3 26.4 %collective-permute-start.23 = (bf16[256,4096]{1,0:T(8,128)(2,1)}, bf16[256,4096]{1,0:T(8,128)(2,1)}, u32[]{:S(2)}, u32[]{:S(2)}) collective-permute-start(bf16[256,4096]{1,0:T(8,128)(2,1)} %get-tuple-element.442), channel_id=1, source_target_pairs={{0,1},{1,0},{2,3},{3,2},{4,5},{5,4},{6,7},{7,6},{8,9},{9,8},{10,11... | collective-permute-start | bytes 6291464 | tf_op jit(solution)/shard_map/ppermute | solution.py:221
  287.7 27.5 %collective-permute-start.24 = (bf16[512,4096]{1,0:T(8,128)(2,1)}, bf16[512,4096]{1,0:T(8,128)(2,1)}, u32[]{:S(2)}, u32[]{:S(2)}) collective-permute-start(bf16[512,4096]{1,0:T(8,128)(2,1)} %weight_product.8), channel_id=1, source_target_pairs={{0,16},{16,0},{1,17},{17,1},{2,18},{18,2},{3,19},{19,3},{4,20},{20... | collective-permute-start | bytes 12582920 | tf_op jit(solution)/shard_map/ppermute | solution.py:216
  295.0 28.3 %collective-permute-start.25 = (bf16[128,4096]{1,0:T(8,128)(2,1)S(1)}, bf16[128,4096]{1,0:T(8,128)(2,1)S(1)}, u32[]{:S(2)}, u32[]{:S(2)}) collective-permute-start(bf16[128,4096]{1,0:T(8,128)(2,1)S(1)} %get-tuple-element.458), channel_id=1, source_target_pairs={{0,2},{1,3},{2,0},{3,1},{4,6},{5,7},{6,4},{7,5},{8,10},{9,11},{10,... | collective-permute-start | bytes 3145736 | tf_op jit(solution)/shard_map/ppermute | solution.py:232
  322.9 32.1 %collective-permute-start.29 = (bf16[256,4096]{1,0:T(8,128)(2,1)S(1)}, bf16[256,4096]{1,0:T(8,128)(2,1)}, u32[]{:S(2)}, u32[]{:S(2)}) collective-permute-start(bf16[256,4096]{1,0:T(8,128)(2,1)S(1)} %get-tuple-element.480), channel_id=1, source_target_pairs={{0,1},{1,0},{2,3},{3,2},{4,5},{5,4},{6,7},{7,6},{8,9},{9,8},{10,11... | collective-permute-start | bytes 6291464 | tf_op jit(solution)/shard_map/ppermute | solution.py:221
  323.5 30.4 %collective-permute-start.26 = (bf16[32,4096]{1,0:T(8,128)(2,1)S(1)}, bf16[32,4096]{1,0:T(8,128)(2,1)S(1)}, u32[]{:S(2)}, u32[]{:S(2)}) collective-permute-start(bf16[32,4096]{1,0:T(8,128)(2,1)S(1)} %get-tuple-element.474), channel_id=1, source_target_pairs={{0,4},{1,5},{2,6},{3,7},{4,0},{5,1},{6,2},{7,3},{8,12},{9,13},{10,... | collective-permute-start | bytes 786440 | tf_op jit(solution)/shard_map/ppermute | solution.py:239
  323.6 30.3 %collective-permute-start.27 = (bf16[32,4096]{1,0:T(8,128)(2,1)S(1)}, bf16[32,4096]{1,0:T(8,128)(2,1)S(1)}, u32[]{:S(2)}, u32[]{:S(2)}) collective-permute-start(bf16[32,4096]{1,0:T(8,128)(2,1)S(1)} %get-tuple-element.475), channel_id=1, source_target_pairs={{0,8},{1,9},{2,10},{3,11},{4,12},{5,13},{6,14},{7,15},{8,0},{9,1},... | collective-permute-start | bytes 786440 | tf_op jit(solution)/shard_map/ppermute | solution.py:239
  329.1 24.9 %collective-permute-start.28 = (bf16[32,4096]{1,0:T(8,128)(2,1)S(1)}, bf16[32,4096]{1,0:T(8,128)(2,1)S(1)}, u32[]{:S(2)}, u32[]{:S(2)}) collective-permute-start(bf16[32,4096]{1,0:T(8,128)(2,1)S(1)} %get-tuple-element.476), channel_id=1, source_target_pairs={{0,12},{1,13},{2,14},{3,15},{4,8},{5,9},{6,10},{7,11},{8,4},{9,5},... | collective-permute-start | bytes 786440 | tf_op jit(solution)/shard_map/ppermute | solution.py:239
  370.4 21.9 %collective-permute-start.31 = (bf16[128,4096]{1,0:T(8,128)(2,1)}, bf16[128,4096]{1,0:T(8,128)(2,1)}, u32[]{:S(2)}, u32[]{:S(2)}) collective-permute-start(bf16[128,4096]{1,0:T(8,128)(2,1)} %get-tuple-element.503), channel_id=1, source_target_pairs={{0,2},{1,3},{2,0},{3,1},{4,6},{5,7},{6,4},{7,5},{8,10},{9,11},{10,... | collective-permute-start | bytes 3145736 | tf_op jit(solution)/shard_map/ppermute | solution.py:232
  404.5 20.2 %collective-permute-start.32 = (bf16[512,1408]{1,0:T(8,128)(2,1)}, bf16[512,1408]{1,0:T(8,128)(2,1)}, u32[]{:S(2)}, u32[]{:S(2)}) collective-permute-start(bf16[512,1408]{1,0:T(8,128)(2,1)} %last_product.2), channel_id=1, source_target_pairs={{0,16},{16,0},{1,17},{17,1},{2,18},{18,2},{3,19},{19,3},{4,20},{20... | collective-permute-start | bytes 4325384 | tf_op jit(solution)/shard_map/ppermute | solution.py:216
  405.6 26.4 %collective-permute-start.33 = (bf16[256,4096]{1,0:T(8,128)(2,1)}, bf16[256,4096]{1,0:T(8,128)(2,1)}, u32[]{:S(2)}, u32[]{:S(2)}) collective-permute-start(bf16[256,4096]{1,0:T(8,128)(2,1)} %get-tuple-element.528), channel_id=1, source_target_pairs={{0,1},{1,0},{2,3},{3,2},{4,5},{5,4},{6,7},{7,6},{8,9},{9,8},{10,11... | collective-permute-start | bytes 6291464 | tf_op jit(solution)/shard_map/ppermute | solution.py:221
  420.3 27.5 %collective-permute-start.35 = (bf16[32,4096]{1,0:T(8,128)(2,1)}, bf16[32,4096]{1,0:T(8,128)(2,1)}, u32[]{:S(2)}, u32[]{:S(2)}) collective-permute-start(bf16[32,4096]{1,0:T(8,128)(2,1)} %get-tuple-element.541), channel_id=1, source_target_pairs={{0,4},{1,5},{2,6},{3,7},{4,0},{5,1},{6,2},{7,3},{8,12},{9,13},{10,... | collective-permute-start | bytes 786440 | tf_op jit(solution)/shard_map/ppermute | solution.py:239
  420.8 26.9 %collective-permute-start.36 = (bf16[32,4096]{1,0:T(8,128)(2,1)}, bf16[32,4096]{1,0:T(8,128)(2,1)}, u32[]{:S(2)}, u32[]{:S(2)}) collective-permute-start(bf16[32,4096]{1,0:T(8,128)(2,1)} %get-tuple-element.542), channel_id=1, source_target_pairs={{0,8},{1,9},{2,10},{3,11},{4,12},{5,13},{6,14},{7,15},{8,0},{9,1},... | collective-permute-start | bytes 786440 | tf_op jit(solution)/shard_map/ppermute | solution.py:239
  424.7 23.1 %collective-permute-start.37 = (bf16[32,4096]{1,0:T(8,128)(2,1)}, bf16[32,4096]{1,0:T(8,128)(2,1)}, u32[]{:S(2)}, u32[]{:S(2)}) collective-permute-start(bf16[32,4096]{1,0:T(8,128)(2,1)} %get-tuple-element.543), channel_id=1, source_target_pairs={{0,12},{1,13},{2,14},{3,15},{4,8},{5,9},{6,10},{7,11},{8,4},{9,5},... | collective-permute-start | bytes 786440 | tf_op jit(solution)/shard_map/ppermute | solution.py:239
  441.9 24.4 %collective-permute-start.38 = (bf16[128,5504]{1,0:T(8,128)(2,1)}, bf16[128,5504]{1,0:T(8,128)(2,1)}, u32[]{:S(2)}, u32[]{:S(2)}) collective-permute-start(bf16[128,5504]{1,0:T(8,128)(2,1)} %get-tuple-element.547), channel_id=1, source_target_pairs={{0,2},{1,3},{2,0},{3,1},{4,6},{5,7},{6,4},{7,5},{8,10},{9,11},{10,... | collective-permute-start | bytes 4227080 | tf_op jit(solution)/shard_map/ppermute | solution.py:232
  449.8 32.5 %all-to-all-start.2 = ((bf16[16,49,512]{2,1,0:T(8,128)(2,1)}), bf16[16,49,512]{2,1,0:T(8,128)(2,1)S(1)}, u32[]{:S(2)}, u32[]{:S(2)}) async-start(bf16[16,49,512]{2,1,0:T(8,128)(2,1)} %reshape.419), calls=%async_computation.2 | async-start | bytes 1835008 | tf_op jit(solution)/shard_map/all_to_all | solution.py:1039
  469.3 23.2 %collective-permute-start.39 = (bf16[32,5504]{1,0:T(8,128)(2,1)}, bf16[32,5504]{1,0:T(8,128)(2,1)}, u32[]{:S(2)}, u32[]{:S(2)}) collective-permute-start(bf16[32,5504]{1,0:T(8,128)(2,1)} %get-tuple-element.558), channel_id=1, source_target_pairs={{0,4},{1,5},{2,6},{3,7},{4,0},{5,1},{6,2},{7,3},{8,12},{9,13},{10,... | collective-permute-start | bytes 1056776 | tf_op jit(solution)/shard_map/ppermute | solution.py:239
  469.3 32.8 %collective-permute-start.40 = (bf16[32,5504]{1,0:T(8,128)(2,1)}, bf16[32,5504]{1,0:T(8,128)(2,1)}, u32[]{:S(2)}, u32[]{:S(2)}) collective-permute-start(bf16[32,5504]{1,0:T(8,128)(2,1)} %get-tuple-element.559), channel_id=1, source_target_pairs={{0,8},{1,9},{2,10},{3,11},{4,12},{5,13},{6,14},{7,15},{8,0},{9,1},... | collective-permute-start | bytes 1056776 | tf_op jit(solution)/shard_map/ppermute | solution.py:239
  475.1 27.0 %collective-permute-start.41 = (bf16[32,5504]{1,0:T(8,128)(2,1)}, bf16[32,5504]{1,0:T(8,128)(2,1)}, u32[]{:S(2)}, u32[]{:S(2)}) collective-permute-start(bf16[32,5504]{1,0:T(8,128)(2,1)} %get-tuple-element.560), channel_id=1, source_target_pairs={{0,12},{1,13},{2,14},{3,15},{4,8},{5,9},{6,10},{7,11},{8,4},{9,5},... | collective-permute-start | bytes 1056776 | tf_op jit(solution)/shard_map/ppermute | solution.py:239
  517.1 16.2 %collective-permute-start.46 = (f32[1]{0:T(128)}, f32[1]{0:T(128)}, u32[]{:S(2)}, u32[]{:S(2)}) collective-permute-start(f32[1]{0:T(128)} %add.658), channel_id=1, source_target_pairs={{0,8},{1,9},{2,10},{3,11},{4,12},{5,13},{6,14},{7,15},{8,0},{9,1},... | collective-permute-start | bytes 20 | tf_op jit(solution)/shard_map/ppermute | solution.py:151
  (160 other events, 1463.7 us)

commit v4 on v3

--- a/solution.py
+++ b/solution.py
@@ -570,51 +570,57 @@
     return inward_call(expand_kernel, pair, weights, first_column, FF, bias.reshape(1, FF), [out, out])
 
 
-def sums_kernel(pixel_ref, out_ref):
+def sums_kernel(first, pixel_ref, vec_ref, out_ref):
     sums = [jnp.zeros((1, PIX), F32)] * 2
     for image in range(pixel_ref.shape[0]):
         values = pixel_ref[image].astype(F32)
         sums[0] = sums[0] + jnp.sum(values, axis=0, keepdims=True)
         sums[1] = sums[1] + jnp.sum(values * values, axis=0, keepdims=True)
-    out_ref[...] = jnp.concatenate(sums, axis=0)
-
-
-def column_sums(pixels):
+    place = lax.broadcasted_iota(jnp.int32, vec_ref.shape, 0) * SPAN
+    place = place + lax.broadcasted_iota(jnp.int32, vec_ref.shape, 1)
+    values = vec_ref[...]
+    for number in range(2 * BANDS):
+        band = number % BANDS
+        rest = sums[number // BANDS][:, band * PATCH * PATCH : (band + 1) * PATCH * PATCH]
+        rest = jnp.sum(rest, axis=1, keepdims=True)
+        for piece in range(3):
+            part = rest.astype(BF).astype(F32)
+            rest = rest - part
+            values = jnp.where(place == first + 3 * number + piece, part, values)
+    out_ref[...] = values.astype(BF)
+
+
+def vectors_and_sums(pixels, vec_rows, first):
     return pl.pallas_call(
-        sums_kernel,
-        out_shape=jax.ShapeDtypeStruct((2, PIX), F32),
+        functools.partial(sums_kernel, first),
+        out_shape=jax.ShapeDtypeStruct(vec_rows.shape, BF),
         compiler_params=pltpu.CompilerParams(vmem_limit_bytes=20 * 2**20),
         cost_estimate=SMALL,
-        name="column_sums",
-    )(pixels)
-
-
-def grid_spec():
-    return pl.BlockSpec((1, 4, 1, QUART, DDEC), lambda i: (0, 0, i, 0, 0))
-
-
-def pick_kernel(spot_ref, dy_ref, rows_ref, sums_ref, pieces_ref):
-    spot = spot_ref[0]
-    rows = jnp.zeros((VIS, DDEC), F32)
-    sums = jnp.zeros((8, DDEC), F32)
-    for quarter in range(4):
-        place = lax.broadcasted_iota(jnp.int32, (VIS, QUART), 1) + quarter * QUART
-        hot = (spot == place).astype(F32)
-        values = dy_ref[0, quarter, 0]
-        rows = rows + jnp.dot(hot.astype(BF), values, preferred_element_type=F32)
-        vacant = 1.0 - jnp.sum(hot, axis=0, keepdims=True)
-        weights = jnp.concatenate([jnp.ones_like(vacant), vacant, jnp.zeros((6, QUART), F32)], axis=0)
-        sums = sums + jnp.dot(weights.astype(BF), values, preferred_element_type=F32)
-    rows_ref[0] = rows.astype(BF)
-
-    @pl.when(pl.program_id(0) == 0)
+        name="vectors_and_sums",
+    )(pixels, vec_rows)
+
+
+def pick_kernel(spot_ref, source_ref, dy_ref, rows_ref, sums_ref, pieces_ref, total_ref):
+    quarter = pl.program_id(0)
+
+    @pl.when(quarter == 0)
     def _():
         sums_ref[...] = jnp.zeros_like(sums_ref)
-
-    sums_ref[...] += sums
-
-    @pl.when(pl.program_id(0) == pl.num_programs(0) - 1)
+        total_ref[...] = jnp.zeros_like(total_ref)
+
+    count = dy_ref.shape[1]
+    place = spot_ref[...] - quarter * QUART
+    target = jnp.where((place >= 0) & (place < QUART), place * (count // QUART) + source_ref[...], -1)
+    hot = (lax.broadcasted_iota(jnp.int32, (count, count), 1) == target).astype(F32)
+    values = dy_ref[0]
+    total_ref[...] += jnp.dot(hot.astype(BF), values, preferred_element_type=F32)
+    vacant = 1.0 - jnp.sum(hot, axis=0, keepdims=True)
+    weights = jnp.concatenate([jnp.ones_like(vacant), vacant, jnp.zeros((6, count), F32)], axis=0)
+    sums_ref[...] += jnp.dot(weights.astype(BF), values, preferred_element_type=F32)
+
+    @pl.when(quarter == pl.num_programs(0) - 1)
     def _():
+        rows_ref[...] = total_ref[...].astype(BF)
         rest = sums_ref[1:2]
         pieces = []
         for _ in range(3):
@@ -626,24 +632,26 @@
 
 def pick_rows(visible_in, grids):
     images = visible_in.shape[0]
+    count = images * QUART
+    grids = grids[0].transpose(0, 2, 1, 3).reshape(4, count, DDEC)
+    source = jnp.asarray(np.repeat(np.arange(images, dtype=np.int32), VIS)[:, None])
+    column = pl.BlockSpec((count, 1), lambda i: (0, 0))
+    small = pl.BlockSpec((8, DDEC), lambda i: (0, 0))
     return pl.pallas_call(
         pick_kernel,
-        grid=(images,),
-        in_specs=[pl.BlockSpec((1, VIS, 1), lambda i: (i, 0, 0)), grid_spec()],
-        out_specs=[
-            pl.BlockSpec((1, VIS, DDEC), lambda i: (i, 0, 0)),
-            pl.BlockSpec((8, DDEC), lambda i: (0, 0)),
-            pl.BlockSpec((8, DDEC), lambda i: (0, 0)),
-        ],
+        grid=(4,),
+        in_specs=[column, column, pl.BlockSpec((1, count, DDEC), lambda i: (i, 0, 0))],
+        out_specs=[pl.BlockSpec((count, DDEC), lambda i: (0, 0)), small, small],
         out_shape=[
-            jax.ShapeDtypeStruct((images, VIS, DDEC), BF),
+            jax.ShapeDtypeStruct((count, DDEC), BF),
             jax.ShapeDtypeStruct((8, DDEC), F32),
             jax.ShapeDtypeStruct((8, DDEC), BF),
         ],
-        compiler_params=pltpu.CompilerParams(vmem_limit_bytes=20 * 2**20),
+        scratch_shapes=[pltpu.VMEM((count, DDEC), F32)],
+        compiler_params=pltpu.CompilerParams(vmem_limit_bytes=40 * 2**20),
         cost_estimate=SMALL,
         name="pick_rows",
-    )(visible_in[:, :, None], grids)
+    )(visible_in.reshape(count, 1), source, grids)
 
 
 def place_kernel(scale_ref, spot_ref, rows_ref, table_ref, base_ref, out_ref):
@@ -724,61 +732,61 @@
     whole_images = item_count == 4
 
     order = Order(vec_first)
+    dp_index = lax.axis_index("dp")
     vec_length = vectors.shape[0]
+    if whole_images:
+        marks = jnp.concatenate([visible, scale_index[:, None]], axis=1)
+        marks_in = lax.all_to_all(marks, "dp", split_axis=0, concat_axis=0, tiled=True)
     pe_rows = pe_weight.T.astype(BF)
     middle_rows = jnp.concatenate([out_weight.T, up_weight, dec_weight], axis=1).astype(BF)
     if routed:
-        vec_low = jnp.pad(vectors.astype(BF), (0, 4 * SPAN - vec_length)).reshape(4, SPAN)
-        vec_low = jnp.pad(vec_low, ((0, shard_rows - 4), (0, 0)))
+        qkv_gather = Gathering(qkv_weight.astype(BF), False, order)
+        middle_gather = Gathering(middle_rows, False, order)
+        owners = block_order()
+        vec_low = jnp.pad(vectors.astype(BF).astype(F32), (0, shard_rows * SPAN - vec_length))
+        vec_low = vec_low.reshape(shard_rows, SPAN)
+        table = order(angle_pieces(D, 3)).reshape(-1, 32, shard_rows)
+        table = jnp.einsum("pb,kbr->kpr", owners, table, preferred_element_type=F32).astype(BF)
+        table, pixel_flat = order(table.reshape(-1, D), pixels.reshape(row_count, PIX))
+        vec_low = vectors_and_sums(order(pixels), vec_low, vec_length)
         pe_gather = Gathering(jnp.concatenate([pe_rows, vec_low], axis=1), True, order)
-        middle_gather = Gathering(middle_rows, False, order)
-        qkv_gather = Gathering(qkv_weight.astype(BF), False, order)
-        owners = block_order()
-    stats = column_sums(order(pixels)).reshape(2, BANDS, PATCH * PATCH)
-    stats = order(jnp.sum(stats, axis=2).reshape(2 * BANDS))
-    if routed:
-        pe_gather.first_turn()
         qkv_gather.middle()
         middle_gather.middle()
-    if whole_images:
-        marks = jnp.concatenate([visible, scale_index[:, None]], axis=1).astype(F32)
-        marks = jnp.concatenate(
-            [marks, jnp.broadcast_to(stats[None], (dp_count, 2 * BANDS))], axis=1
-        )
-        marks_in = lax.all_to_all(order(marks), "dp", split_axis=0, concat_axis=0, tiled=True)
-        stats = jnp.sum(marks_in[:, -2 * BANDS :], axis=0)
-        marks_in, stats = order(marks_in, stats + lax.ppermute(stats, "grp", core_pairs()))
     else:
-        stats = lax.psum(stats, AXES)
+        pixel_rows = pixels.astype(F32).reshape(row_count, BANDS, PATCH * PATCH)
+        band_sum = jnp.sum(pixel_rows, axis=(0, 2))
+        band_square = jnp.sum(pixel_rows * pixel_rows, axis=(0, 2))
+        stats = lax.psum(jnp.concatenate([band_sum, band_square]), AXES)
     down_rows = order(down_weight).T.astype(BF)
     if routed:
-        pe_gather.second_turn()
+        pe_gather.first_turn()
         down_gather = Gathering(down_rows, False, order)
 
-    dp_index = lax.axis_index("dp")
     cotangent_rows = order(cotangent)
     if whole_images:
-        image_order = marks_in[:, : -2 * BANDS].astype(jnp.int32)
-        visible_in, scale_in = image_order[:, :VIS], image_order[:, VIS]
+        marks_in = order(marks_in)
+        visible_in, scale_in = marks_in[:, :VIS], marks_in[:, VIS]
         dy_sent, dy_sums, vacant_low = order(*pick_rows(visible_in, cotangent_rows))
         dec_bias_grad, dy_vacant = dy_sums[0], dy_sums[1]
+        dy_sent = dy_sent.reshape(image_count, VIS, DDEC)
         dy_rows = lax.all_to_all(dy_sent, "dp", split_axis=0, concat_axis=0, tiled=True)
+    if routed:
+        pe_gather.second_turn()
+        qkv_gather.first_turn()
     spots, scale_rows = order(visible.reshape(row_count), jnp.repeat(scale_index, VIS))
-    table = angle_pieces(D, 3)
     if routed:
         pe_gather.cores()
-        table = table.reshape(-1, 32, shard_rows)
-        table = jnp.einsum("pb,kbr->kpr", owners, table, preferred_element_type=F32).astype(BF)
-        table = table.reshape(-1, D)
+    else:
+        table, pixel_flat = angle_pieces(D, 3), pixels.reshape(row_count, PIX)
     hot = angle_hot(spots, scale_rows, 3)
     enc_table = order(*[forward_product(hot, part) for part in halves(table)])
-    if routed:
-        qkv_gather.first_turn()
     if routed:
         pe_pair = pe_gather.total()
         vector_all = jnp.concatenate([part[:, PIX:] for part in pe_pair])
         vector_all = vector_all.reshape(device_count, shard_rows, SPAN)[:, :4].reshape(device_count, -1)
         vector_all = jnp.einsum("pb,pv->bv", owners, vector_all, preferred_element_type=F32)
+        stats = vector_all[:, vec_length : vec_length + 6 * BANDS].reshape(-1, 2 * BANDS, 3)
+        stats = jnp.sum(stats, axis=(0, 2))
         vector_all = vector_all[:, :vec_length].reshape(-1)
     else:
         early = jnp.concatenate([pe_rows, qkv_weight.astype(BF)], axis=1)
@@ -795,7 +803,7 @@
     band_mean = stats[:BANDS] / entry_count
     band_scale = lax.rsqrt(stats[BANDS:] / entry_count - band_mean * band_mean + EPS_NORM)
     scale_row = jnp.repeat(band_scale, PATCH * PATCH)[None]
-    pixel_norm = pixels.reshape(row_count, PIX).astype(F32) - jnp.repeat(band_mean, PATCH * PATCH)[None]
+    pixel_norm = pixel_flat.astype(F32) - jnp.repeat(band_mean, PATCH * PATCH)[None]
     pixel_low = order((pixel_norm * scale_row).astype(BF))
     pieces, up_bias, dec_bias = split_vectors(vector_all)
     query_bias, value_bias = pieces[5], pieces[6]
@@ -818,6 +826,7 @@
     if whole_images:
         dy_rows = order(dy_rows).reshape(row_count, DDEC)
     if routed:
+        down_gather.first_turn()
         middle_gather.second_turn()
         qkv_gather.cores()
         qkv_pair = qkv_gather.total()
@@ -830,10 +839,9 @@
     projected = order(projected)
     mixture_low, peaks = order(*attend(projected))
     if routed:
-        down_gather.first_turn()
+        down_gather.second_turn()
         middle_gather.cores()
         middle_pair = middle_gather.total()
-        down_gather.second_turn()
     mixture_low = order(mixture_low)
     UP, DEC = D, D + FF
     stream_mid = outward(mixture_low, middle_pair, 0, D)

time: 554 us -> 540 us (0.975)
  starting transfers between devices: 90.3 us -> 79.9 us
    ppermute x4, waiting for transfers between devices: 37.6 us -> 8.78 us  [first_turn(): self.near = [lax.ppermute(self.grow(), AXES, turn_pairs(2, 1))]]
    ppermute x3, waiting for transfers between devices: 11 us -> 39.7 us  [middle(): self.near = [lax.ppermute(self.grow(), 'dp', dp_pairs(8))]]
    ppermute x6, waiting for transfers between devices: 7.23 us -> 0.02 us  [__init__(): self.near = [lax.ppermute(self.held, 'dp', dp_pairs(4 * k)) for k in steps]]
    ppermute x4, waiting for transfers between devices: 10.5 us -> 17.5 us  [second_turn(): self.near = [lax.ppermute(self.grow(), AXES, turn_pairs(1, 2))]]
    optimization_barrier x2 -> x1, local copies, waits for them, and re-layouts: 5.97 us -> 0.36 us  [__call__(): *values, self.token = lax.optimization_barrier((*values, self.token))]
    unnamed x305 -> x303, local copies, waits for them, and re-layouts: 28.6 us -> 30.1 us
  transfers between devices with their start and end apart: 52 -> 51, of which waited for: 19 -> 15; matrix products, arithmetic and copies ran while one was open for 27% -> 27% of each run, Pallas kernels for 23% -> 23%
where the time goes in v4:
time: 540 us; the launch traced here: 533 us
  Pallas kernels  139 us (26%)
  waiting for transfers between devices  110 us (20%)
  starting transfers between devices  79.9 us (15%)
  other arithmetic  71.7 us (13%)
  matrix products  70.9 us (13%)
  local copies, waits for them, and re-layouts  50.7 us (9%)
  between operations  10.8 us (2%)
    dot_general x14, matrix products, back_product(): lax.dot_general(left, right, (((1,), (1,)), ((), ())), preferred_element_...  52.4 us
    pallas_call x6, Pallas kernels, weight_call(): pl.pallas_call(functools.partial(weight_kernel, tuple(edges), int(came is...  45.8 us
    pallas_call x4, Pallas kernels, inward_call(): pl.pallas_call(kernel, grid=(columns // width,), in_specs=[whole, whole,...  45 us
    ppermute x3, waiting for transfers between devices, middle(): self.near = [lax.ppermute(self.grow(), 'dp', dp_pairs(8))]  39.7 us
    unnamed x303, local copies, waits for them, and re-layouts  30.1 us
    concatenate x15, other arithmetic, grow(): self.held = self.order(jnp.concatenate([held] + self.near))  26.1 us
    ppermute x6, starting transfers between devices, tiny_sum(): lax.ppermute(value, 'dp', dp_pairs(unit * k))  20.8 us
    pallas_call x1, Pallas kernels, attend_back(): pl.pallas_call(attend_back_kernel, grid=(pairs,), in_specs=[block(0), blo...  19.9 us
  transfers between devices with their start and end apart: 51, of which 15 were waited for; matrix products, arithmetic and copies ran while one was open for 27% of the time, Pallas kernels for 23%

profile of v4, /device:TPU:0, one launch (start us, length us, event | category | flops | bytes accessed | tf_op | source)
XLA Modules:
  0.0 533.1 jit_solution(16471619081494832738)
XLA Ops:
  17.8 6.2 %all-to-all-start = ((s32[16,1,50]{2,1,0:T(1,128)}), s32[16,1,50]{2,1,0:T(1,128)S(1)}, u32[]{:S(2)}, u32[]{:S(2)}) async-start(s32[16,1,50]{2,1,0:T(1,128)} %bitcast.1), calls=%async_computation | async-start | bytes 16384 | tf_op jit(solution)/shard_map/all_to_all | solution.py:739
  38.5 5.5 %pick_rows.1 = (bf16[784,512]{1,0:T(8,128)(2,1)S(1)}, f32[8,512]{1,0:T(8,128)S(1)}, bf16[8,512]{1,0:T(8,128)(2,1)S(1)}) custom-call(s32[784,1]{1,0:T(8,128)S(1)} %copy-done.41, s32[784,1]{1,0:T(8,128)S(1)} %copy-done.45, bf16[4,784,512]{2,1,0:T(8,128)(2,1)S(1)} %bitcast.108), custom_call_target="tpu_custom_call" | custom-call | flops 1000000 | bytes 100000 | tf_op jit(solution)/shard_map/pick_rows/pallas_call | solution.py:640
  52.2 4.5 all-to-all-start.1
  75.4 15.1 %collective-permute-done.9 = bf16[64,5632]{1,0:T(8,128)(2,1)} collective-permute-done((bf16[64,5632]{1,0:T(8,128)(2,1)}, bf16[64,5632]{1,0:T(8,128)(2,1)}, u32[]{:S(2)}, u32[]{:S(2)}) %collective-permute-start.9) | collective-permute-done | bytes 720928 | tf_op jit(solution)/shard_map/ppermute | solution.py:194
  97.2 24.6 %collective-permute-done.12 = bf16[64,4096]{1,0:T(8,128)(2,1)} collective-permute-done((bf16[64,4096]{1,0:T(8,128)(2,1)}, bf16[64,4096]{1,0:T(8,128)(2,1)}, u32[]{:S(2)}, u32[]{:S(2)}) %collective-permute-start.12) | collective-permute-done | bytes 524320 | tf_op jit(solution)/shard_map/ppermute | solution.py:194
  123.1 4.0 collective-permute-done.13
  136.4 6.8 %shift_kernel.1.q_ref.k_ref.v_ref = bf16[784,3072]{1,0:T(8,128)(2,1)S(1)} custom-call(bf16[784,512]{1,0:T(8,128)(2,1)S(1)} %get-tuple-element.491.near_ref.refs_2_, bf16[784,512]{1,0:T(8,128)(2,1)S(1)} %get-tuple-element.484.far_ref.refs_2_, bf16[512,3072]{1,0:T(8,128)(2,1)S(1)} %pad_maximum_fusion.2.near_w_ref, ...), custom_call_target="tpu_custom_call" | custom-call | flops 1000000 | bytes 100000 | tf_op jit(solution)/shard_map/shift_kernel/pallas_call | solution.py:556
  143.3 9.5 %attend.1 = (bf16[784,1024]{1,0:T(8,128)(2,1)S(1)}, f32[8,8,256]{2,1,0:T(8,128)S(1)}) custom-call(bf16[784,3072]{1,0:T(8,128)(2,1)S(1)} %shift_kernel.1.q_ref.k_ref.v_ref, bf16[784,3072]{1,0:T(8,128)(2,1)S(1)} %shift_kernel.1.q_ref.k_ref.v_ref, bf16[784,3072]{1,0:T(8,128)(2,1)S(1)} %shift_kernel.1.q_ref.k_ref.v_ref), custom_call_target="tpu_custom_call" | custom-call | flops 1000000 | bytes 100000 | tf_op jit(solution)/shard_map/attend/pallas_call | solution.py:417
  152.8 4.8 collective-permute-done.16
  159.0 17.5 %collective-permute-done.17 = bf16[256,5632]{1,0:T(8,128)(2,1)S(1)} collective-permute-done((bf16[256,5632]{1,0:T(8,128)(2,1)S(1)}, bf16[256,5632]{1,0:T(8,128)(2,1)S(1)}, u32[]{:S(2)}, u32[]{:S(2)}) %collective-permute-start.17) | collective-permute-done | bytes 2883616 | tf_op jit(solution)/shard_map/ppermute | solution.py:200
  195.3 23.0 %expand_kernel.1 = (bf16[784,4096]{1,0:T(8,128)(2,1)}, bf16[784,4096]{1,0:T(8,128)(2,1)}) custom-call(bf16[784,512]{1,0:T(8,128)(2,1)S(1)} %get-tuple-element.451.near_ref.refs_0_, bf16[784,512]{1,0:T(8,128)(2,1)S(1)} %get-tuple-element.438.far_ref.refs_0_, bf16[512,5632]{1,0:T(8,128)(2,1)} %pad_maximum_fusion.near_w_ref, ...), custom_call_target="tpu_custom_call" | custom-call | flops 1000000 | bytes 100000 | tf_op jit(solution)/shard_map/expand_kernel/pallas_call | solution.py:556
  222.6 6.7 %weight_product.6 = bf16[512,4096]{1,0:T(8,128)(2,1)} custom-call(bf16[784,512]{1,0:T(8,128)(2,1)S(1)} %get-tuple-element.418.refs_0_.far_ref, bf16[784,4096]{1,0:T(8,128)(2,1)S(1)} %copy-done.1), custom_call_target="tpu_custom_call" | custom-call | flops 1000000 | bytes 100000 | tf_op jit(solution)/shard_map/weight_product/pallas_call | solution.py:303
  232.3 13.1 %slope_kernel.1 = (bf16[784,4096]{1,0:T(8,128)(2,1)}, f32[1,4096]{1,0:T(1,128)S(1)}) custom-call(bf16[784,512]{1,0:T(8,128)(2,1)S(1)} %copy-done.21, bf16[784,512]{1,0:T(8,128)(2,1)S(1)} %copy-done.24, bf16[512,4096]{1,0:T(8,128)(2,1)} %pad_maximum_fusion.1.near_w_ref, bf16[512,4096]{1,0:T(8,128)(2,1)} %collective-permute-done.20.far_w_ref, ...), custom_call_target="tpu_custom_call" | custom-call | flops 1000000 | bytes 100000 | tf_op jit(solution)/shard_map/slope_kernel/pallas_call | solution.py:556
  245.4 9.1 %weight_product.7 = (bf16[256,4096]{1,0:T(8,128)(2,1)S(1)}, bf16[256,4096]{1,0:T(8,128)(2,1)}) custom-call(bf16[784,512]{1,0:T(8,128)(2,1)S(1)} %copy-done.21, bf16[784,4096]{1,0:T(8,128)(2,1)} %get-tuple-element.431.refs_1_, bf16[512,4096]{1,0:T(8,128)(2,1)} %collective-permute-done.21.refs_2_), custom_call_target="tpu_custom_call" | custom-call | flops 1000000 | bytes 100000 | tf_op jit(solution)/shard_map/weight_product/pallas_call | solution.py:303
  256.5 6.7 %add_convert_fusion.8.stream_ref = bf16[784,512]{1,0:T(8,128)(2,1)} fusion(f32[784,512]{1,0:T(8,128)S(1)} %copy-done.54, bf16[784,4096]{1,0:T(8,128)(2,1)S(1)} %bitcast.105, bf16[512,4096]{1,0:T(8,128)(2,1)} %pad_maximum_fusion.1.near_w_ref, f32[512]{0:T(512)S(1)} %add.599), kind=kOutput, calls=%fused_computation.33 | convolution fusion | flops 3289538560 | bytes 13027328 | tf_op jit(solution)/shard_map/dot_general | solution.py:46
  263.3 6.8 %add_convert_fusion.7.stream_ref = bf16[784,512]{1,0:T(8,128)(2,1)} fusion(f32[784,512]{1,0:T(8,128)S(1)} %copy-done.57, bf16[784,4096]{1,0:T(8,128)(2,1)S(1)} %bitcast.105, bf16[512,4096]{1,0:T(8,128)(2,1)} %collective-permute-done.20.far_w_ref, f32[512]{0:T(512)S(1)} %add.603), kind=kOutput, calls=%fused_computation.32 | convolution fusion | flops 3289538560 | bytes 13027328 | tf_op jit(solution)/shard_map/dot_general | solution.py:46
  270.1 6.6 %weight_product.8 = bf16[512,4096]{1,0:T(8,128)(2,1)} custom-call(bf16[784,512]{1,0:T(8,128)(2,1)S(1)} %copy-done.16, bf16[784,4096]{1,0:T(8,128)(2,1)S(1)} %bitcast.101), custom_call_target="tpu_custom_call" | custom-call | flops 1000000 | bytes 100000 | tf_op jit(solution)/shard_map/weight_product/pallas_call | solution.py:303
  285.8 7.7 %fusion.2 = f32[784,512]{1,0:T(8,128)S(1)} fusion(bf16[784,4096]{1,0:T(8,128)(2,1)} %get-tuple-element.445.refs_1_, bf16[512,5632]{1,0:T(8,128)(2,1)} %pad_maximum_fusion.near_w_ref), kind=kOutput, calls=%fused_computation.4 | convolution fusion | flops 3288334336 | bytes 12222464 | tf_op jit(solution)/shard_map/dot_general | solution.py:46
  293.6 7.0 %multiply_reduce_fusion = (bf16[512]{0:T(512)(128)(2,1)}, f32[784]{0:T(1024)S(1)}, f32[784]{0:T(1024)S(1)}, bf16[512]{0:T(512)(128)(2,1)}, bf16[512]{0:T(512)(12...) fusion(f32[784,512]{1,0:T(8,128)S(1)} %copy-done.58, ...), kind=kOutput, calls=%fused_computation.20 | convolution fusion | flops 3295554560 | bytes 17066368 | tf_op jit(solution)/shard_map/dot_general | solution.py:46
  304.4 7.6 %weight_product.9 = (bf16[256,4096]{1,0:T(8,128)(2,1)S(1)}, bf16[256,4096]{1,0:T(8,128)(2,1)S(1)}) custom-call(bf16[784,512]{1,0:T(8,128)(2,1)S(1)} %get-tuple-element.451.near_ref.refs_0_, bf16[784,4096]{1,0:T(8,128)(2,1)} %get-tuple-element.445.refs_1_, bf16[512,4096]{1,0:T(8,128)(2,1)} %collective-permute-done.23.refs_2_), custom_call_target="tpu_custom_call" | custom-call | flops 1000000 | bytes 100000 | tf_op jit(solution)/shard_map/weight_product/pallas_call | solution.py:303
  321.6 19.9 %attend_back.1 = (bf16[784,3072]{1,0:T(8,128)(2,1)S(1)}, f32[8,1024]{1,0:T(8,128)S(1)}) custom-call(bf16[784,3072]{1,0:T(8,128)(2,1)S(1)} %bitcast.99, bf16[784,3072]{1,0:T(8,128)(2,1)S(1)} %bitcast.99, bf16[784,3072]{1,0:T(8,128)(2,1)S(1)} %bitcast.99, bf16[784,1024]{1,0:T(8,128)(2,1)S(1)} %add_convert_fusion.mix_ref, ...), custom_call_target="tpu_custom_call" | custom-call | flops 1000000 | bytes 100000 | tf_op jit(solution)/shard_map/attend_back/pallas_call | solution.py:473
  342.7 4.4 add_convert_fusion.3
  347.1 6.8 %weight_product.10 = bf16[512,4096]{1,0:T(8,128)(2,1)} custom-call(bf16[784,512]{1,0:T(8,128)(2,1)S(1)} %convert_element_type.334.refs_0_, bf16[784,1024]{1,0:T(8,128)(2,1)S(1)} %copy-done.27, bf16[784,512]{1,0:T(8,128)(2,1)S(1)} %copy-done.14, bf16[784,3072]{1,0:T(8,128)(2,1)S(1)} %get-tuple-element.487.refs_3_), custom_call_target="tpu_custom_call" | custom-call | flops 1000000 | bytes 100000 | tf_op jit(solution)/shard_map/weight_product/pallas_call | solution.py:303
  359.5 5.4 %fusion.105 = f32[784,512]{1,0:T(8,128)S(1)} fusion(bf16[784,3072]{1,0:T(8,128)(2,1)} %copy-done.2, bf16[512,3072]{1,0:T(8,128)(2,1)S(1)} %copy-done.4), kind=kOutput, calls=%fused_computation.290 | convolution fusion | flops 2466250752 | bytes 9568256 | tf_op jit(solution)/shard_map/dot_general | solution.py:46
  372.8 8.9 %weight_product.11 = (bf16[256,4096]{1,0:T(8,128)(2,1)S(1)}, bf16[256,4096]{1,0:T(8,128)(2,1)}) custom-call(bf16[784,512]{1,0:T(8,128)(2,1)S(1)} %copy-done.8, bf16[784,1024]{1,0:T(8,128)(2,1)S(1)} %copy-done.28, bf16[784,512]{1,0:T(8,128)(2,1)S(1)} %copy-done.12, bf16[784,3072]{1,0:T(8,128)(2,1)} %copy-done.2, bf16[512,4096]{1,0:T(8,128)(2,1)} %collective-permute-done.29.refs_4_), custom_call_target="tpu_custom_call" | custom-call | flops 1000000 | bytes 100000 | tf_op jit(solution)/shard_map/weight_product/pallas_call | solution.py:303
  422.9 5.9 %collective-permute-done.33 = bf16[256,1408]{1,0:T(8,128)(2,1)S(1)} collective-permute-done((bf16[256,1408]{1,0:T(8,128)(2,1)S(1)}, bf16[256,1408]{1,0:T(8,128)(2,1)S(1)}, u32[]{:S(2)}, u32[]{:S(2)}) %collective-permute-start.33) | collective-permute-done | bytes 720928 | tf_op jit(solution)/shard_map/ppermute | solution.py:221
  438.4 4.7 all-to-all-start.2
  443.1 13.1 %collective-permute-done.37 = bf16[128,5504]{1,0:T(8,128)(2,1)} collective-permute-done((bf16[128,5504]{1,0:T(8,128)(2,1)}, bf16[128,5504]{1,0:T(8,128)(2,1)}, u32[]{:S(2)}, u32[]{:S(2)}) %collective-permute-start.37) | collective-permute-done | bytes 1409056 | tf_op jit(solution)/shard_map/ppermute | solution.py:232
  466.8 4.0 copy.97
  470.8 7.2 %place_rows.1 = bf16[1,4,16,49,512]{4,3,2,1,0:T(8,128)(2,1)S(1)} custom-call(s32[16]{0:T(128)S(1)} %slice_reduce_fusion.1.scale_ref, s32[16,1,49]{2,1,0:T(1,128)S(1)} %bitcast.113, bf16[16,49,512]{2,1,0:T(8,128)(2,1)S(1)} %all-to-all-done.2.rows_ref, bf16[224,512]{1,0:T(8,128)(2,1)S(1)} %copy-done.46, f32[1,512]{1,0:T(1,128)S(1)} %fusion.65.base_ref), custom_call_target="tpu_custom_call" | custom-call | flops 1000000 | bytes 100000 | tf_op jit(solution)/shard_map/place_rows/pallas_call | solution.py:678
  480.9 8.2 %collective-permute-done.39 = bf16[32,5504]{1,0:T(8,128)(2,1)} collective-permute-done((bf16[32,5504]{1,0:T(8,128)(2,1)}, bf16[32,5504]{1,0:T(8,128)(2,1)}, u32[]{:S(2)}, u32[]{:S(2)}) %collective-permute-start.39) | collective-permute-done | bytes 352288 | tf_op jit(solution)/shard_map/ppermute | solution.py:239
  504.3 8.3 %collective-permute-start.45 = (f32[1]{0:T(128)}, f32[1]{0:T(128)}, u32[]{:S(2)}, u32[]{:S(2)}) collective-permute-start(f32[1]{0:T(128)} %add.652), channel_id=1, source_target_pairs={{0,8},{1,9},{2,10},{3,11},{4,12},{5,13},{6,14},{7,15},{8,0},{9,1},... | collective-permute-start | bytes 20 | tf_op jit(solution)/shard_map/ppermute | solution.py:151
  (593 shorter events, 232.6 us)
Async XLA Ops:
  1.8 22.2 %collective-permute-start = (bf16[32,3072]{1,0:T(8,128)(2,1)S(1)}, bf16[32,3072]{1,0:T(8,128)(2,1)}, u32[]{:S(2)}, u32[]{:S(2)}) collective-permute-start(bf16[32,3072]{1,0:T(8,128)(2,1)S(1)} %convert_element_type.306), channel_id=1, source_target_pairs={{0,4},{1,5},{2,6},{3,7},{4,0},{5,1},{6,2},{7,3},{8,12},{9,13},{10,... | collective-permute-start | bytes 589832 | tf_op jit(solution)/shard_map/ppermute | solution.py:186
  12.4 18.4 %collective-permute-start.2 = (bf16[32,896]{1,0:T(8,128)(2,1)S(1)}, bf16[32,896]{1,0:T(8,128)(2,1)S(1)}, u32[]{:S(2)}, u32[]{:S(2)}) collective-permute-start(bf16[32,896]{1,0:T(8,128)(2,1)S(1)} %pad_maximum_fusion.21), channel_id=1, source_target_pairs={{0,4},{1,5},{2,6},{3,7},{4,0},{5,1},{6,2},{7,3},{8,12},{9,13},{10,... | collective-permute-start | bytes 172040 | tf_op jit(solution)/shard_map/ppermute | solution.py:186
  12.5 18.2 %collective-permute-start.3 = (bf16[32,896]{1,0:T(8,128)(2,1)S(1)}, bf16[32,896]{1,0:T(8,128)(2,1)}, u32[]{:S(2)}, u32[]{:S(2)}) collective-permute-start(bf16[32,896]{1,0:T(8,128)(2,1)S(1)} %pad_maximum_fusion.21), channel_id=1, source_target_pairs={{0,8},{1,9},{2,10},{3,11},{4,12},{5,13},{6,14},{7,15},{8,0},{9,1},... | collective-permute-start | bytes 172040 | tf_op jit(solution)/shard_map/ppermute | solution.py:186
  25.9 30.9 %collective-permute-start.6 = (bf16[64,3072]{1,0:T(8,128)(2,1)}, bf16[64,3072]{1,0:T(8,128)(2,1)}, u32[]{:S(2)}, u32[]{:S(2)}) collective-permute-start(bf16[64,3072]{1,0:T(8,128)(2,1)} %pad_maximum_fusion.17), channel_id=1, source_target_pairs={{0,8},{1,9},{2,10},{3,11},{4,12},{5,13},{6,14},{7,15},{8,0},{9,1},... | collective-permute-start | bytes 1179656 | tf_op jit(solution)/shard_map/ppermute | solution.py:194
  47.8 42.7 %collective-permute-start.9 = (bf16[64,5632]{1,0:T(8,128)(2,1)}, bf16[64,5632]{1,0:T(8,128)(2,1)}, u32[]{:S(2)}, u32[]{:S(2)}) collective-permute-start(bf16[64,5632]{1,0:T(8,128)(2,1)} %pad_maximum_fusion.11), channel_id=1, source_target_pairs={{0,8},{1,9},{2,10},{3,11},{4,12},{5,13},{6,14},{7,15},{8,0},{9,1},... | collective-permute-start | bytes 2162696 | tf_op jit(solution)/shard_map/ppermute | solution.py:194
  48.4 44.9 %collective-permute-start.10 = (bf16[32,4096]{1,0:T(8,128)(2,1)}, bf16[32,4096]{1,0:T(8,128)(2,1)}, u32[]{:S(2)}, u32[]{:S(2)}) collective-permute-start(bf16[32,4096]{1,0:T(8,128)(2,1)} %convert_bitcast_fusion), channel_id=1, source_target_pairs={{0,4},{1,5},{2,6},{3,7},{4,0},{5,1},{6,2},{7,3},{8,12},{9,13},{10,... | collective-permute-start | bytes 786440 | tf_op jit(solution)/shard_map/ppermute | solution.py:186
  52.2 45.0 %all-to-all-start.1 = ((bf16[16,49,512]{2,1,0:T(8,128)(2,1)}), bf16[16,49,512]{2,1,0:T(8,128)(2,1)}, u32[]{:S(2)}, u32[]{:S(2)}) async-start(bf16[16,49,512]{2,1,0:T(8,128)(2,1)} %reshape.418), calls=%async_computation.1 | async-start | bytes 1835008 | tf_op jit(solution)/shard_map/all_to_all | solution.py:772
  58.9 36.2 %collective-permute-start.11 = (bf16[128,3072]{1,0:T(8,128)(2,1)}, bf16[128,3072]{1,0:T(8,128)(2,1)}, u32[]{:S(2)}, u32[]{:S(2)}) collective-permute-start(bf16[128,3072]{1,0:T(8,128)(2,1)} %pad_maximum_fusion.10), channel_id=1, source_target_pairs={{0,2},{1,3},{2,0},{3,1},{4,6},{5,7},{6,4},{7,5},{8,10},{9,11},{10,... | collective-permute-start | bytes 2359304 | tf_op jit(solution)/shard_map/ppermute | solution.py:197
  92.8 34.3 %collective-permute-start.13 = (bf16[128,5632]{1,0:T(8,128)(2,1)}, bf16[128,5632]{1,0:T(8,128)(2,1)}, u32[]{:S(2)}, u32[]{:S(2)}) collective-permute-start(bf16[128,5632]{1,0:T(8,128)(2,1)} %pad_maximum_fusion.7), channel_id=1, source_target_pairs={{0,2},{1,3},{2,0},{3,1},{4,6},{5,7},{6,4},{7,5},{8,10},{9,11},{10,... | collective-permute-start | bytes 4325384 | tf_op jit(solution)/shard_map/ppermute | solution.py:197
  95.1 26.7 %collective-permute-start.12 = (bf16[64,4096]{1,0:T(8,128)(2,1)}, bf16[64,4096]{1,0:T(8,128)(2,1)}, u32[]{:S(2)}, u32[]{:S(2)}) collective-permute-start(bf16[64,4096]{1,0:T(8,128)(2,1)} %pad_maximum_fusion.13), channel_id=1, source_target_pairs={{0,8},{1,9},{2,10},{3,11},{4,12},{5,13},{6,14},{7,15},{8,0},{9,1},... | collective-permute-start | bytes 1572872 | tf_op jit(solution)/shard_map/ppermute | solution.py:194
  96.6 32.5 %collective-permute-start.14 = (bf16[256,3072]{1,0:T(8,128)(2,1)S(1)}, bf16[256,3072]{1,0:T(8,128)(2,1)}, u32[]{:S(2)}, u32[]{:S(2)}) collective-permute-start(bf16[256,3072]{1,0:T(8,128)(2,1)S(1)} %pad_maximum_fusion.6), channel_id=1, source_target_pairs={{0,1},{1,0},{2,3},{3,2},{4,5},{5,4},{6,7},{7,6},{8,9},{9,8},{10,11... | collective-permute-start | bytes 4718600 | tf_op jit(solution)/shard_map/ppermute | solution.py:200
  130.8 45.8 %collective-permute-start.17 = (bf16[256,5632]{1,0:T(8,128)(2,1)S(1)}, bf16[256,5632]{1,0:T(8,128)(2,1)S(1)}, u32[]{:S(2)}, u32[]{:S(2)}) collective-permute-start(bf16[256,5632]{1,0:T(8,128)(2,1)S(1)} %pad_maximum_fusion.3), channel_id=1, source_target_pairs={{0,1},{1,0},{2,3},{3,2},{4,5},{5,4},{6,7},{7,6},{8,9},{9,8},{10,11... | collective-permute-start | bytes 8650760 | tf_op jit(solution)/shard_map/ppermute | solution.py:200
  131.5 26.1 %collective-permute-start.16 = (bf16[128,4096]{1,0:T(8,128)(2,1)S(1)}, bf16[128,4096]{1,0:T(8,128)(2,1)S(1)}, u32[]{:S(2)}, u32[]{:S(2)}) collective-permute-start(bf16[128,4096]{1,0:T(8,128)(2,1)S(1)} %pad_maximum_fusion.8), channel_id=1, source_target_pairs={{0,2},{1,3},{2,0},{3,1},{4,6},{5,7},{6,4},{7,5},{8,10},{9,11},{10,... | collective-permute-start | bytes 3145736 | tf_op jit(solution)/shard_map/ppermute | solution.py:197
  181.3 36.9 %collective-permute-start.19 = (bf16[256,4096]{1,0:T(8,128)(2,1)}, bf16[256,4096]{1,0:T(8,128)(2,1)S(1)}, u32[]{:S(2)}, u32[]{:S(2)}) collective-permute-start(bf16[256,4096]{1,0:T(8,128)(2,1)} %pad_maximum_fusion.5), channel_id=1, source_target_pairs={{0,1},{1,0},{2,3},{3,2},{4,5},{5,4},{6,7},{7,6},{8,9},{9,8},{10,11... | collective-permute-start | bytes 6291464 | tf_op jit(solution)/shard_map/ppermute | solution.py:200
  255.8 26.4 %collective-permute-start.22 = (bf16[256,4096]{1,0:T(8,128)(2,1)}, bf16[256,4096]{1,0:T(8,128)(2,1)}, u32[]{:S(2)}, u32[]{:S(2)}) collective-permute-start(bf16[256,4096]{1,0:T(8,128)(2,1)} %get-tuple-element.442), channel_id=1, source_target_pairs={{0,1},{1,0},{2,3},{3,2},{4,5},{5,4},{6,7},{7,6},{8,9},{9,8},{10,11... | collective-permute-start | bytes 6291464 | tf_op jit(solution)/shard_map/ppermute | solution.py:221
  276.7 27.6 %collective-permute-start.23 = (bf16[512,4096]{1,0:T(8,128)(2,1)}, bf16[512,4096]{1,0:T(8,128)(2,1)}, u32[]{:S(2)}, u32[]{:S(2)}) collective-permute-start(bf16[512,4096]{1,0:T(8,128)(2,1)} %weight_product.8), channel_id=1, source_target_pairs={{0,16},{16,0},{1,17},{17,1},{2,18},{18,2},{3,19},{19,3},{4,20},{20... | collective-permute-start | bytes 12582920 | tf_op jit(solution)/shard_map/ppermute | solution.py:216
  284.6 27.9 %collective-permute-start.24 = (bf16[128,4096]{1,0:T(8,128)(2,1)S(1)}, bf16[128,4096]{1,0:T(8,128)(2,1)S(1)}, u32[]{:S(2)}, u32[]{:S(2)}) collective-permute-start(bf16[128,4096]{1,0:T(8,128)(2,1)S(1)} %get-tuple-element.458), channel_id=1, source_target_pairs={{0,2},{1,3},{2,0},{3,1},{4,6},{5,7},{6,4},{7,5},{8,10},{9,11},{10,... | collective-permute-start | bytes 3145736 | tf_op jit(solution)/shard_map/ppermute | solution.py:232
  312.0 30.6 %collective-permute-start.28 = (bf16[256,4096]{1,0:T(8,128)(2,1)S(1)}, bf16[256,4096]{1,0:T(8,128)(2,1)}, u32[]{:S(2)}, u32[]{:S(2)}) collective-permute-start(bf16[256,4096]{1,0:T(8,128)(2,1)S(1)} %get-tuple-element.480), channel_id=1, source_target_pairs={{0,1},{1,0},{2,3},{3,2},{4,5},{5,4},{6,7},{7,6},{8,9},{9,8},{10,11... | collective-permute-start | bytes 6291464 | tf_op jit(solution)/shard_map/ppermute | solution.py:221
  312.7 28.9 %collective-permute-start.25 = (bf16[32,4096]{1,0:T(8,128)(2,1)S(1)}, bf16[32,4096]{1,0:T(8,128)(2,1)S(1)}, u32[]{:S(2)}, u32[]{:S(2)}) collective-permute-start(bf16[32,4096]{1,0:T(8,128)(2,1)S(1)} %get-tuple-element.474), channel_id=1, source_target_pairs={{0,4},{1,5},{2,6},{3,7},{4,0},{5,1},{6,2},{7,3},{8,12},{9,13},{10,... | collective-permute-start | bytes 786440 | tf_op jit(solution)/shard_map/ppermute | solution.py:239
  312.8 28.8 %collective-permute-start.26 = (bf16[32,4096]{1,0:T(8,128)(2,1)S(1)}, bf16[32,4096]{1,0:T(8,128)(2,1)S(1)}, u32[]{:S(2)}, u32[]{:S(2)}) collective-permute-start(bf16[32,4096]{1,0:T(8,128)(2,1)S(1)} %get-tuple-element.475), channel_id=1, source_target_pairs={{0,8},{1,9},{2,10},{3,11},{4,12},{5,13},{6,14},{7,15},{8,0},{9,1},... | collective-permute-start | bytes 786440 | tf_op jit(solution)/shard_map/ppermute | solution.py:239
  315.1 26.5 %collective-permute-start.27 = (bf16[32,4096]{1,0:T(8,128)(2,1)S(1)}, bf16[32,4096]{1,0:T(8,128)(2,1)S(1)}, u32[]{:S(2)}, u32[]{:S(2)}) collective-permute-start(bf16[32,4096]{1,0:T(8,128)(2,1)S(1)} %get-tuple-element.476), channel_id=1, source_target_pairs={{0,12},{1,13},{2,14},{3,15},{4,8},{5,9},{6,10},{7,11},{8,4},{9,5},... | collective-permute-start | bytes 786440 | tf_op jit(solution)/shard_map/ppermute | solution.py:239
  358.3 23.4 %collective-permute-start.30 = (bf16[128,4096]{1,0:T(8,128)(2,1)}, bf16[128,4096]{1,0:T(8,128)(2,1)}, u32[]{:S(2)}, u32[]{:S(2)}) collective-permute-start(bf16[128,4096]{1,0:T(8,128)(2,1)} %get-tuple-element.503), channel_id=1, source_target_pairs={{0,2},{1,3},{2,0},{3,1},{4,6},{5,7},{6,4},{7,5},{8,10},{9,11},{10,... | collective-permute-start | bytes 3145736 | tf_op jit(solution)/shard_map/ppermute | solution.py:232
  394.0 18.6 %collective-permute-start.31 = (bf16[512,1408]{1,0:T(8,128)(2,1)}, bf16[512,1408]{1,0:T(8,128)(2,1)}, u32[]{:S(2)}, u32[]{:S(2)}) collective-permute-start(bf16[512,1408]{1,0:T(8,128)(2,1)} %last_product.2), channel_id=1, source_target_pairs={{0,16},{16,0},{1,17},{17,1},{2,18},{18,2},{3,19},{19,3},{4,20},{20... | collective-permute-start | bytes 4325384 | tf_op jit(solution)/shard_map/ppermute | solution.py:216
  394.8 26.4 %collective-permute-start.32 = (bf16[256,4096]{1,0:T(8,128)(2,1)}, bf16[256,4096]{1,0:T(8,128)(2,1)}, u32[]{:S(2)}, u32[]{:S(2)}) collective-permute-start(bf16[256,4096]{1,0:T(8,128)(2,1)} %get-tuple-element.528), channel_id=1, source_target_pairs={{0,1},{1,0},{2,3},{3,2},{4,5},{5,4},{6,7},{7,6},{8,9},{9,8},{10,11... | collective-permute-start | bytes 6291464 | tf_op jit(solution)/shard_map/ppermute | solution.py:221
  408.2 28.2 %collective-permute-start.34 = (bf16[32,4096]{1,0:T(8,128)(2,1)}, bf16[32,4096]{1,0:T(8,128)(2,1)}, u32[]{:S(2)}, u32[]{:S(2)}) collective-permute-start(bf16[32,4096]{1,0:T(8,128)(2,1)} %get-tuple-element.541), channel_id=1, source_target_pairs={{0,4},{1,5},{2,6},{3,7},{4,0},{5,1},{6,2},{7,3},{8,12},{9,13},{10,... | collective-permute-start | bytes 786440 | tf_op jit(solution)/shard_map/ppermute | solution.py:239
  408.2 28.2 %collective-permute-start.35 = (bf16[32,4096]{1,0:T(8,128)(2,1)}, bf16[32,4096]{1,0:T(8,128)(2,1)}, u32[]{:S(2)}, u32[]{:S(2)}) collective-permute-start(bf16[32,4096]{1,0:T(8,128)(2,1)} %get-tuple-element.542), channel_id=1, source_target_pairs={{0,8},{1,9},{2,10},{3,11},{4,12},{5,13},{6,14},{7,15},{8,0},{9,1},... | collective-permute-start | bytes 786440 | tf_op jit(solution)/shard_map/ppermute | solution.py:239
  411.2 25.2 %collective-permute-start.36 = (bf16[32,4096]{1,0:T(8,128)(2,1)}, bf16[32,4096]{1,0:T(8,128)(2,1)}, u32[]{:S(2)}, u32[]{:S(2)}) collective-permute-start(bf16[32,4096]{1,0:T(8,128)(2,1)} %get-tuple-element.543), channel_id=1, source_target_pairs={{0,12},{1,13},{2,14},{3,15},{4,8},{5,9},{6,10},{7,11},{8,4},{9,5},... | collective-permute-start | bytes 786440 | tf_op jit(solution)/shard_map/ppermute | solution.py:239
  431.1 25.1 %collective-permute-start.37 = (bf16[128,5504]{1,0:T(8,128)(2,1)}, bf16[128,5504]{1,0:T(8,128)(2,1)}, u32[]{:S(2)}, u32[]{:S(2)}) collective-permute-start(bf16[128,5504]{1,0:T(8,128)(2,1)} %get-tuple-element.547), channel_id=1, source_target_pairs={{0,2},{1,3},{2,0},{3,1},{4,6},{5,7},{6,4},{7,5},{8,10},{9,11},{10,... | collective-permute-start | bytes 4227080 | tf_op jit(solution)/shard_map/ppermute | solution.py:232
  438.4 32.4 %all-to-all-start.2 = ((bf16[16,49,512]{2,1,0:T(8,128)(2,1)}), bf16[16,49,512]{2,1,0:T(8,128)(2,1)S(1)}, u32[]{:S(2)}, u32[]{:S(2)}) async-start(bf16[16,49,512]{2,1,0:T(8,128)(2,1)} %reshape.428), calls=%async_computation.2 | async-start | bytes 1835008 | tf_op jit(solution)/shard_map/all_to_all | solution.py:1047
  459.2 21.7 %collective-permute-start.38 = (bf16[32,5504]{1,0:T(8,128)(2,1)}, bf16[32,5504]{1,0:T(8,128)(2,1)}, u32[]{:S(2)}, u32[]{:S(2)}) collective-permute-start(bf16[32,5504]{1,0:T(8,128)(2,1)} %get-tuple-element.558), channel_id=1, source_target_pairs={{0,4},{1,5},{2,6},{3,7},{4,0},{5,1},{6,2},{7,3},{8,12},{9,13},{10,... | collective-permute-start | bytes 1056776 | tf_op jit(solution)/shard_map/ppermute | solution.py:239
  459.2 29.9 %collective-permute-start.39 = (bf16[32,5504]{1,0:T(8,128)(2,1)}, bf16[32,5504]{1,0:T(8,128)(2,1)}, u32[]{:S(2)}, u32[]{:S(2)}) collective-permute-start(bf16[32,5504]{1,0:T(8,128)(2,1)} %get-tuple-element.559), channel_id=1, source_target_pairs={{0,8},{1,9},{2,10},{3,11},{4,12},{5,13},{6,14},{7,15},{8,0},{9,1},... | collective-permute-start | bytes 1056776 | tf_op jit(solution)/shard_map/ppermute | solution.py:239
  462.4 26.8 %collective-permute-start.40 = (bf16[32,5504]{1,0:T(8,128)(2,1)}, bf16[32,5504]{1,0:T(8,128)(2,1)}, u32[]{:S(2)}, u32[]{:S(2)}) collective-permute-start(bf16[32,5504]{1,0:T(8,128)(2,1)} %get-tuple-element.560), channel_id=1, source_target_pairs={{0,12},{1,13},{2,14},{3,15},{4,8},{5,9},{6,10},{7,11},{8,4},{9,5},... | collective-permute-start | bytes 1056776 | tf_op jit(solution)/shard_map/ppermute | solution.py:239
  (158 other events, 1512.7 us)

commit v5 on v4

--- a/solution.py
+++ b/solution.py
@@ -826,7 +826,7 @@
     if whole_images:
         dy_rows = order(dy_rows).reshape(row_count, DDEC)
     if routed:
-        down_gather.first_turn()
+        down_gather.grow()
         middle_gather.second_turn()
         qkv_gather.cores()
         qkv_pair = qkv_gather.total()
@@ -839,7 +839,7 @@
     projected = order(projected)
     mixture_low, peaks = order(*attend(projected))
     if routed:
-        down_gather.second_turn()
+        down_gather.near = [lax.ppermute(order(down_gather.held), AXES, turn_pairs(2, 1))]
         middle_gather.cores()
         middle_pair = middle_gather.total()
     mixture_low = order(mixture_low)
@@ -872,6 +872,8 @@
 
     out_low = order(*out_low)
     norm_two = order(*norm_two)
+    if routed:
+        down_gather.second_turn()
     activated, slope = order(*expand(norm_two, middle_pair, UP, up_bias))
     if routed:
         down_gather.cores()

time: 540 us -> 534 us (0.989)
  waiting for transfers between devices: 110 us -> 103 us
    ppermute x4 -> x3, waiting for transfers between devices: 8.78 us -> 2.97 us  [first_turn(): self.near = [lax.ppermute(self.grow(), AXES, turn_pairs(2, 1))]]
  transfers between devices with their start and end apart: 51 -> 51, of which waited for: 15 -> 16; matrix products, arithmetic and copies ran while one was open for 27% -> 27% of each run, Pallas kernels for 23% -> 23%
where the time goes in v5:
time: 534 us; the launch traced here: 527 us
  Pallas kernels  139 us (26%)
  waiting for transfers between devices  103 us (19%)
  starting transfers between devices  80.5 us (15%)
  other arithmetic  71.5 us (13%)
  matrix products  71.1 us (13%)
  local copies, waits for them, and re-layouts  50.2 us (9%)
  between operations  10.8 us (2%)
    dot_general x14, matrix products, back_product(): lax.dot_general(left, right, (((1,), (1,)), ((), ())), preferred_element_...  52.6 us
    pallas_call x6, Pallas kernels, weight_call(): pl.pallas_call(functools.partial(weight_kernel, tuple(edges), int(came is...  45.8 us
    pallas_call x4, Pallas kernels, inward_call(): pl.pallas_call(kernel, grid=(columns // width,), in_specs=[whole, whole,...  44.7 us
    ppermute x3, waiting for transfers between devices, middle(): self.near = [lax.ppermute(self.grow(), 'dp', dp_pairs(8))]  39.7 us
    unnamed x303, local copies, waits for them, and re-layouts  29.6 us
    concatenate x15, other arithmetic, grow(): self.held = self.order(jnp.concatenate([held] + self.near))  25.9 us
    ppermute x6, starting transfers between devices, tiny_sum(): lax.ppermute(value, 'dp', dp_pairs(unit * k))  20.8 us
    pallas_call x1, Pallas kernels, attend_back(): pl.pallas_call(attend_back_kernel, grid=(pairs,), in_specs=[block(0), blo...  19.9 us
  transfers between devices with their start and end apart: 51, of which 16 were waited for; matrix products, arithmetic and copies ran while one was open for 27% of the time, Pallas kernels for 23%

profile of v5, /device:TPU:0, one launch (start us, length us, event | category | flops | bytes accessed | tf_op | source)
XLA Modules:
  0.0 526.5 jit_solution(2343920072413669303)
XLA Ops:
  17.8 6.2 %all-to-all-start = ((s32[16,1,50]{2,1,0:T(1,128)}), s32[16,1,50]{2,1,0:T(1,128)S(1)}, u32[]{:S(2)}, u32[]{:S(2)}) async-start(s32[16,1,50]{2,1,0:T(1,128)} %bitcast.1), calls=%async_computation | async-start | bytes 16384 | tf_op jit(solution)/shard_map/all_to_all | solution.py:739
  38.5 5.5 %pick_rows.1 = (bf16[784,512]{1,0:T(8,128)(2,1)S(1)}, f32[8,512]{1,0:T(8,128)S(1)}, bf16[8,512]{1,0:T(8,128)(2,1)S(1)}) custom-call(s32[784,1]{1,0:T(8,128)S(1)} %copy-done.41, s32[784,1]{1,0:T(8,128)S(1)} %copy-done.45, bf16[4,784,512]{2,1,0:T(8,128)(2,1)S(1)} %bitcast.108), custom_call_target="tpu_custom_call" | custom-call | flops 1000000 | bytes 100000 | tf_op jit(solution)/shard_map/pick_rows/pallas_call | solution.py:640
  52.2 4.5 all-to-all-start.1
  75.4 15.1 %collective-permute-done.9 = bf16[64,5632]{1,0:T(8,128)(2,1)} collective-permute-done((bf16[64,5632]{1,0:T(8,128)(2,1)}, bf16[64,5632]{1,0:T(8,128)(2,1)}, u32[]{:S(2)}, u32[]{:S(2)}) %collective-permute-start.9) | collective-permute-done | bytes 720928 | tf_op jit(solution)/shard_map/ppermute | solution.py:194
  97.2 24.6 %collective-permute-done.12 = bf16[64,4096]{1,0:T(8,128)(2,1)} collective-permute-done((bf16[64,4096]{1,0:T(8,128)(2,1)}, bf16[64,4096]{1,0:T(8,128)(2,1)}, u32[]{:S(2)}, u32[]{:S(2)}) %collective-permute-start.12) | collective-permute-done | bytes 524320 | tf_op jit(solution)/shard_map/ppermute | solution.py:194
  131.5 4.9 collective-permute-done.15.far_w_ref
  136.4 6.8 %shift_kernel.1.q_ref.k_ref.v_ref = bf16[784,3072]{1,0:T(8,128)(2,1)S(1)} custom-call(bf16[784,512]{1,0:T(8,128)(2,1)S(1)} %get-tuple-element.495.near_ref.refs_2_, bf16[784,512]{1,0:T(8,128)(2,1)S(1)} %get-tuple-element.488.far_ref.refs_2_, bf16[512,3072]{1,0:T(8,128)(2,1)S(1)} %pad_maximum_fusion.2.near_w_ref, ...), custom_call_target="tpu_custom_call" | custom-call | flops 1000000 | bytes 100000 | tf_op jit(solution)/shard_map/shift_kernel/pallas_call | solution.py:556
  143.2 9.5 %attend.1 = (bf16[784,1024]{1,0:T(8,128)(2,1)S(1)}, f32[8,8,256]{2,1,0:T(8,128)S(1)}) custom-call(bf16[784,3072]{1,0:T(8,128)(2,1)S(1)} %shift_kernel.1.q_ref.k_ref.v_ref, bf16[784,3072]{1,0:T(8,128)(2,1)S(1)} %shift_kernel.1.q_ref.k_ref.v_ref, bf16[784,3072]{1,0:T(8,128)(2,1)S(1)} %shift_kernel.1.q_ref.k_ref.v_ref), custom_call_target="tpu_custom_call" | custom-call | flops 1000000 | bytes 100000 | tf_op jit(solution)/shard_map/attend/pallas_call | solution.py:417
  152.8 12.5 %collective-permute-done.16 = bf16[256,5632]{1,0:T(8,128)(2,1)S(1)} collective-permute-done((bf16[256,5632]{1,0:T(8,128)(2,1)S(1)}, bf16[256,5632]{1,0:T(8,128)(2,1)S(1)}, u32[]{:S(2)}, u32[]{:S(2)}) %collective-permute-start.16) | collective-permute-done | bytes 2883616 | tf_op jit(solution)/shard_map/ppermute | solution.py:200
  186.1 22.7 %expand_kernel.1 = (bf16[784,4096]{1,0:T(8,128)(2,1)}, bf16[784,4096]{1,0:T(8,128)(2,1)}) custom-call(bf16[784,512]{1,0:T(8,128)(2,1)S(1)} %get-tuple-element.455.near_ref.refs_0_, bf16[784,512]{1,0:T(8,128)(2,1)S(1)} %get-tuple-element.442.far_ref.refs_0_, bf16[512,5632]{1,0:T(8,128)(2,1)} %pad_maximum_fusion.near_w_ref, ...), custom_call_target="tpu_custom_call" | custom-call | flops 1000000 | bytes 100000 | tf_op jit(solution)/shard_map/expand_kernel/pallas_call | solution.py:556
  215.8 6.7 %weight_product.6 = bf16[512,4096]{1,0:T(8,128)(2,1)} custom-call(bf16[784,512]{1,0:T(8,128)(2,1)S(1)} %get-tuple-element.422.refs_0_.far_ref, bf16[784,4096]{1,0:T(8,128)(2,1)S(1)} %copy-done.1), custom_call_target="tpu_custom_call" | custom-call | flops 1000000 | bytes 100000 | tf_op jit(solution)/shard_map/weight_product/pallas_call | solution.py:303
  225.3 13.1 %slope_kernel.1 = (bf16[784,4096]{1,0:T(8,128)(2,1)}, f32[1,4096]{1,0:T(1,128)S(1)}) custom-call(bf16[784,512]{1,0:T(8,128)(2,1)S(1)} %copy-done.21, bf16[784,512]{1,0:T(8,128)(2,1)S(1)} %copy-done.24, bf16[512,4096]{1,0:T(8,128)(2,1)} %pad_maximum_fusion.1.near_w_ref, bf16[512,4096]{1,0:T(8,128)(2,1)} %collective-permute-done.20.far_w_ref, ...), custom_call_target="tpu_custom_call" | custom-call | flops 1000000 | bytes 100000 | tf_op jit(solution)/shard_map/slope_kernel/pallas_call | solution.py:556
  238.4 9.1 %weight_product.7 = (bf16[256,4096]{1,0:T(8,128)(2,1)S(1)}, bf16[256,4096]{1,0:T(8,128)(2,1)}) custom-call(bf16[784,512]{1,0:T(8,128)(2,1)S(1)} %copy-done.21, bf16[784,4096]{1,0:T(8,128)(2,1)} %get-tuple-element.435.refs_1_, bf16[512,4096]{1,0:T(8,128)(2,1)} %collective-permute-done.21.refs_2_), custom_call_target="tpu_custom_call" | custom-call | flops 1000000 | bytes 100000 | tf_op jit(solution)/shard_map/weight_product/pallas_call | solution.py:303
  249.6 6.7 %add_convert_fusion.8.stream_ref = bf16[784,512]{1,0:T(8,128)(2,1)} fusion(f32[784,512]{1,0:T(8,128)S(1)} %copy-done.54, bf16[784,4096]{1,0:T(8,128)(2,1)S(1)} %bitcast.105, bf16[512,4096]{1,0:T(8,128)(2,1)} %pad_maximum_fusion.1.near_w_ref, f32[512]{0:T(512)S(1)} %add.599), kind=kOutput, calls=%fused_computation.33 | convolution fusion | flops 3289538560 | bytes 13027328 | tf_op jit(solution)/shard_map/dot_general | solution.py:46
  256.3 6.8 %add_convert_fusion.7.stream_ref = bf16[784,512]{1,0:T(8,128)(2,1)} fusion(f32[784,512]{1,0:T(8,128)S(1)} %copy-done.57, bf16[784,4096]{1,0:T(8,128)(2,1)S(1)} %bitcast.105, bf16[512,4096]{1,0:T(8,128)(2,1)} %collective-permute-done.20.far_w_ref, f32[512]{0:T(512)S(1)} %add.603), kind=kOutput, calls=%fused_computation.32 | convolution fusion | flops 3289538560 | bytes 13027328 | tf_op jit(solution)/shard_map/dot_general | solution.py:46
  263.1 6.6 %weight_product.8 = bf16[512,4096]{1,0:T(8,128)(2,1)} custom-call(bf16[784,512]{1,0:T(8,128)(2,1)S(1)} %copy-done.16, bf16[784,4096]{1,0:T(8,128)(2,1)S(1)} %bitcast.101), custom_call_target="tpu_custom_call" | custom-call | flops 1000000 | bytes 100000 | tf_op jit(solution)/shard_map/weight_product/pallas_call | solution.py:303
  279.1 7.8 %fusion.2 = f32[784,512]{1,0:T(8,128)S(1)} fusion(bf16[784,4096]{1,0:T(8,128)(2,1)} %get-tuple-element.449.refs_1_, bf16[512,5632]{1,0:T(8,128)(2,1)} %pad_maximum_fusion.near_w_ref), kind=kOutput, calls=%fused_computation.4 | convolution fusion | flops 3288334336 | bytes 12222464 | tf_op jit(solution)/shard_map/dot_general | solution.py:46
  286.9 7.0 %multiply_reduce_fusion = (bf16[512]{0:T(512)(128)(2,1)}, f32[784]{0:T(1024)S(1)}, f32[784]{0:T(1024)S(1)}, bf16[512]{0:T(512)(128)(2,1)}, bf16[512]{0:T(512)(12...) fusion(f32[784,512]{1,0:T(8,128)S(1)} %copy-done.58, ...), kind=kOutput, calls=%fused_computation.20 | convolution fusion | flops 3295554560 | bytes 17066368 | tf_op jit(solution)/shard_map/dot_general | solution.py:46
  297.8 7.6 %weight_product.9 = (bf16[256,4096]{1,0:T(8,128)(2,1)S(1)}, bf16[256,4096]{1,0:T(8,128)(2,1)S(1)}) custom-call(bf16[784,512]{1,0:T(8,128)(2,1)S(1)} %get-tuple-element.455.near_ref.refs_0_, bf16[784,4096]{1,0:T(8,128)(2,1)} %get-tuple-element.449.refs_1_, bf16[512,4096]{1,0:T(8,128)(2,1)} %collective-permute-done.23.refs_2_), custom_call_target="tpu_custom_call" | custom-call | flops 1000000 | bytes 100000 | tf_op jit(solution)/shard_map/weight_product/pallas_call | solution.py:303
  315.0 19.9 %attend_back.1 = (bf16[784,3072]{1,0:T(8,128)(2,1)S(1)}, f32[8,1024]{1,0:T(8,128)S(1)}) custom-call(bf16[784,3072]{1,0:T(8,128)(2,1)S(1)} %bitcast.99, bf16[784,3072]{1,0:T(8,128)(2,1)S(1)} %bitcast.99, bf16[784,3072]{1,0:T(8,128)(2,1)S(1)} %bitcast.99, bf16[784,1024]{1,0:T(8,128)(2,1)S(1)} %add_convert_fusion.mix_ref, ...), custom_call_target="tpu_custom_call" | custom-call | flops 1000000 | bytes 100000 | tf_op jit(solution)/shard_map/attend_back/pallas_call | solution.py:473
  336.1 4.4 add_convert_fusion.3
  340.5 6.8 %weight_product.10 = bf16[512,4096]{1,0:T(8,128)(2,1)} custom-call(bf16[784,512]{1,0:T(8,128)(2,1)S(1)} %convert_element_type.334.refs_0_, bf16[784,1024]{1,0:T(8,128)(2,1)S(1)} %copy-done.27, bf16[784,512]{1,0:T(8,128)(2,1)S(1)} %copy-done.14, bf16[784,3072]{1,0:T(8,128)(2,1)S(1)} %get-tuple-element.491.refs_3_), custom_call_target="tpu_custom_call" | custom-call | flops 1000000 | bytes 100000 | tf_op jit(solution)/shard_map/weight_product/pallas_call | solution.py:303
  352.4 5.2 fusion.105
  365.6 8.9 %weight_product.11 = (bf16[256,4096]{1,0:T(8,128)(2,1)S(1)}, bf16[256,4096]{1,0:T(8,128)(2,1)}) custom-call(bf16[784,512]{1,0:T(8,128)(2,1)S(1)} %copy-done.8, bf16[784,1024]{1,0:T(8,128)(2,1)S(1)} %copy-done.28, bf16[784,512]{1,0:T(8,128)(2,1)S(1)} %copy-done.12, bf16[784,3072]{1,0:T(8,128)(2,1)} %copy-done.2, bf16[512,4096]{1,0:T(8,128)(2,1)} %collective-permute-done.29.refs_4_), custom_call_target="tpu_custom_call" | custom-call | flops 1000000 | bytes 100000 | tf_op jit(solution)/shard_map/weight_product/pallas_call | solution.py:303
  416.3 5.9 %collective-permute-done.33 = bf16[256,1408]{1,0:T(8,128)(2,1)S(1)} collective-permute-done((bf16[256,1408]{1,0:T(8,128)(2,1)S(1)}, bf16[256,1408]{1,0:T(8,128)(2,1)S(1)}, u32[]{:S(2)}, u32[]{:S(2)}) %collective-permute-start.33) | collective-permute-done | bytes 720928 | tf_op jit(solution)/shard_map/ppermute | solution.py:221
  431.4 5.0 all-to-all-start.2
  436.5 13.1 %collective-permute-done.37 = bf16[128,5504]{1,0:T(8,128)(2,1)} collective-permute-done((bf16[128,5504]{1,0:T(8,128)(2,1)}, bf16[128,5504]{1,0:T(8,128)(2,1)}, u32[]{:S(2)}, u32[]{:S(2)}) %collective-permute-start.37) | collective-permute-done | bytes 1409056 | tf_op jit(solution)/shard_map/ppermute | solution.py:232
  460.2 4.0 copy.97
  464.2 7.2 %place_rows.1 = bf16[1,4,16,49,512]{4,3,2,1,0:T(8,128)(2,1)S(1)} custom-call(s32[16]{0:T(128)S(1)} %slice_reduce_fusion.1.scale_ref, s32[16,1,49]{2,1,0:T(1,128)S(1)} %bitcast.113, bf16[16,49,512]{2,1,0:T(8,128)(2,1)S(1)} %all-to-all-done.2.rows_ref, bf16[224,512]{1,0:T(8,128)(2,1)S(1)} %copy-done.46, f32[1,512]{1,0:T(1,128)S(1)} %fusion.65.base_ref), custom_call_target="tpu_custom_call" | custom-call | flops 1000000 | bytes 100000 | tf_op jit(solution)/shard_map/place_rows/pallas_call | solution.py:678
  474.3 8.3 %collective-permute-done.39 = bf16[32,5504]{1,0:T(8,128)(2,1)} collective-permute-done((bf16[32,5504]{1,0:T(8,128)(2,1)}, bf16[32,5504]{1,0:T(8,128)(2,1)}, u32[]{:S(2)}, u32[]{:S(2)}) %collective-permute-start.39) | collective-permute-done | bytes 352288 | tf_op jit(solution)/shard_map/ppermute | solution.py:239
  497.7 8.3 %collective-permute-start.45 = (f32[1]{0:T(128)}, f32[1]{0:T(128)}, u32[]{:S(2)}, u32[]{:S(2)}) collective-permute-start(f32[1]{0:T(128)} %add.652), channel_id=1, source_target_pairs={{0,8},{1,9},{2,10},{3,11},{4,12},{5,13},{6,14},{7,15},{8,0},{9,1},... | collective-permute-start | bytes 20 | tf_op jit(solution)/shard_map/ppermute | solution.py:151
  506.0 3.7 collective-permute-start.46
  (593 shorter events, 231.1 us)
Async XLA Ops:
  1.8 22.2 %collective-permute-start = (bf16[32,3072]{1,0:T(8,128)(2,1)S(1)}, bf16[32,3072]{1,0:T(8,128)(2,1)}, u32[]{:S(2)}, u32[]{:S(2)}) collective-permute-start(bf16[32,3072]{1,0:T(8,128)(2,1)S(1)} %convert_element_type.306), channel_id=1, source_target_pairs={{0,4},{1,5},{2,6},{3,7},{4,0},{5,1},{6,2},{7,3},{8,12},{9,13},{10,... | collective-permute-start | bytes 589832 | tf_op jit(solution)/shard_map/ppermute | solution.py:186
  12.4 18.4 %collective-permute-start.2 = (bf16[32,896]{1,0:T(8,128)(2,1)S(1)}, bf16[32,896]{1,0:T(8,128)(2,1)S(1)}, u32[]{:S(2)}, u32[]{:S(2)}) collective-permute-start(bf16[32,896]{1,0:T(8,128)(2,1)S(1)} %pad_maximum_fusion.21), channel_id=1, source_target_pairs={{0,4},{1,5},{2,6},{3,7},{4,0},{5,1},{6,2},{7,3},{8,12},{9,13},{10,... | collective-permute-start | bytes 172040 | tf_op jit(solution)/shard_map/ppermute | solution.py:186
  12.5 18.2 %collective-permute-start.3 = (bf16[32,896]{1,0:T(8,128)(2,1)S(1)}, bf16[32,896]{1,0:T(8,128)(2,1)}, u32[]{:S(2)}, u32[]{:S(2)}) collective-permute-start(bf16[32,896]{1,0:T(8,128)(2,1)S(1)} %pad_maximum_fusion.21), channel_id=1, source_target_pairs={{0,8},{1,9},{2,10},{3,11},{4,12},{5,13},{6,14},{7,15},{8,0},{9,1},... | collective-permute-start | bytes 172040 | tf_op jit(solution)/shard_map/ppermute | solution.py:186
  17.8 17.7 %all-to-all-start = ((s32[16,1,50]{2,1,0:T(1,128)}), s32[16,1,50]{2,1,0:T(1,128)S(1)}, u32[]{:S(2)}, u32[]{:S(2)}) async-start(s32[16,1,50]{2,1,0:T(1,128)} %bitcast.1), calls=%async_computation | async-start | bytes 16384 | tf_op jit(solution)/shard_map/all_to_all | solution.py:739
  25.9 30.9 %collective-permute-start.6 = (bf16[64,3072]{1,0:T(8,128)(2,1)}, bf16[64,3072]{1,0:T(8,128)(2,1)}, u32[]{:S(2)}, u32[]{:S(2)}) collective-permute-start(bf16[64,3072]{1,0:T(8,128)(2,1)} %pad_maximum_fusion.17), channel_id=1, source_target_pairs={{0,8},{1,9},{2,10},{3,11},{4,12},{5,13},{6,14},{7,15},{8,0},{9,1},... | collective-permute-start | bytes 1179656 | tf_op jit(solution)/shard_map/ppermute | solution.py:194
  47.8 42.7 %collective-permute-start.9 = (bf16[64,5632]{1,0:T(8,128)(2,1)}, bf16[64,5632]{1,0:T(8,128)(2,1)}, u32[]{:S(2)}, u32[]{:S(2)}) collective-permute-start(bf16[64,5632]{1,0:T(8,128)(2,1)} %pad_maximum_fusion.11), channel_id=1, source_target_pairs={{0,8},{1,9},{2,10},{3,11},{4,12},{5,13},{6,14},{7,15},{8,0},{9,1},... | collective-permute-start | bytes 2162696 | tf_op jit(solution)/shard_map/ppermute | solution.py:194
  48.4 44.9 %collective-permute-start.10 = (bf16[32,4096]{1,0:T(8,128)(2,1)}, bf16[32,4096]{1,0:T(8,128)(2,1)}, u32[]{:S(2)}, u32[]{:S(2)}) collective-permute-start(bf16[32,4096]{1,0:T(8,128)(2,1)} %convert_bitcast_fusion), channel_id=1, source_target_pairs={{0,4},{1,5},{2,6},{3,7},{4,0},{5,1},{6,2},{7,3},{8,12},{9,13},{10,... | collective-permute-start | bytes 786440 | tf_op jit(solution)/shard_map/ppermute | solution.py:186
  52.2 45.0 %all-to-all-start.1 = ((bf16[16,49,512]{2,1,0:T(8,128)(2,1)}), bf16[16,49,512]{2,1,0:T(8,128)(2,1)}, u32[]{:S(2)}, u32[]{:S(2)}) async-start(bf16[16,49,512]{2,1,0:T(8,128)(2,1)} %reshape.418), calls=%async_computation.1 | async-start | bytes 1835008 | tf_op jit(solution)/shard_map/all_to_all | solution.py:772
  58.9 36.2 %collective-permute-start.11 = (bf16[128,3072]{1,0:T(8,128)(2,1)}, bf16[128,3072]{1,0:T(8,128)(2,1)}, u32[]{:S(2)}, u32[]{:S(2)}) collective-permute-start(bf16[128,3072]{1,0:T(8,128)(2,1)} %pad_maximum_fusion.10), channel_id=1, source_target_pairs={{0,2},{1,3},{2,0},{3,1},{4,6},{5,7},{6,4},{7,5},{8,10},{9,11},{10,... | collective-permute-start | bytes 2359304 | tf_op jit(solution)/shard_map/ppermute | solution.py:197
  92.8 34.3 %collective-permute-start.13 = (bf16[128,5632]{1,0:T(8,128)(2,1)}, bf16[128,5632]{1,0:T(8,128)(2,1)}, u32[]{:S(2)}, u32[]{:S(2)}) collective-permute-start(bf16[128,5632]{1,0:T(8,128)(2,1)} %pad_maximum_fusion.7), channel_id=1, source_target_pairs={{0,2},{1,3},{2,0},{3,1},{4,6},{5,7},{6,4},{7,5},{8,10},{9,11},{10,... | collective-permute-start | bytes 4325384 | tf_op jit(solution)/shard_map/ppermute | solution.py:197
  95.1 26.7 %collective-permute-start.12 = (bf16[64,4096]{1,0:T(8,128)(2,1)}, bf16[64,4096]{1,0:T(8,128)(2,1)}, u32[]{:S(2)}, u32[]{:S(2)}) collective-permute-start(bf16[64,4096]{1,0:T(8,128)(2,1)} %pad_maximum_fusion.13), channel_id=1, source_target_pairs={{0,8},{1,9},{2,10},{3,11},{4,12},{5,13},{6,14},{7,15},{8,0},{9,1},... | collective-permute-start | bytes 1572872 | tf_op jit(solution)/shard_map/ppermute | solution.py:194
  96.6 32.5 %collective-permute-start.14 = (bf16[256,3072]{1,0:T(8,128)(2,1)S(1)}, bf16[256,3072]{1,0:T(8,128)(2,1)}, u32[]{:S(2)}, u32[]{:S(2)}) collective-permute-start(bf16[256,3072]{1,0:T(8,128)(2,1)S(1)} %pad_maximum_fusion.6), channel_id=1, source_target_pairs={{0,1},{1,0},{2,3},{3,2},{4,5},{5,4},{6,7},{7,6},{8,9},{9,8},{10,11... | collective-permute-start | bytes 4718600 | tf_op jit(solution)/shard_map/ppermute | solution.py:200
  130.8 34.5 %collective-permute-start.16 = (bf16[256,5632]{1,0:T(8,128)(2,1)S(1)}, bf16[256,5632]{1,0:T(8,128)(2,1)S(1)}, u32[]{:S(2)}, u32[]{:S(2)}) collective-permute-start(bf16[256,5632]{1,0:T(8,128)(2,1)S(1)} %pad_maximum_fusion.3), channel_id=1, source_target_pairs={{0,1},{1,0},{2,3},{3,2},{4,5},{5,4},{6,7},{7,6},{8,9},{9,8},{10,11... | collective-permute-start | bytes 8650760 | tf_op jit(solution)/shard_map/ppermute | solution.py:200
  185.3 26.1 %collective-permute-start.19 = (bf16[256,4096]{1,0:T(8,128)(2,1)S(1)}, bf16[256,4096]{1,0:T(8,128)(2,1)S(1)}, u32[]{:S(2)}, u32[]{:S(2)}) collective-permute-start(bf16[256,4096]{1,0:T(8,128)(2,1)S(1)} %pad_maximum_fusion.5), channel_id=1, source_target_pairs={{0,1},{1,0},{2,3},{3,2},{4,5},{5,4},{6,7},{7,6},{8,9},{9,8},{10,11... | collective-permute-start | bytes 6291464 | tf_op jit(solution)/shard_map/ppermute | solution.py:200
  248.9 26.4 %collective-permute-start.22 = (bf16[256,4096]{1,0:T(8,128)(2,1)}, bf16[256,4096]{1,0:T(8,128)(2,1)}, u32[]{:S(2)}, u32[]{:S(2)}) collective-permute-start(bf16[256,4096]{1,0:T(8,128)(2,1)} %get-tuple-element.446), channel_id=1, source_target_pairs={{0,1},{1,0},{2,3},{3,2},{4,5},{5,4},{6,7},{7,6},{8,9},{9,8},{10,11... | collective-permute-start | bytes 6291464 | tf_op jit(solution)/shard_map/ppermute | solution.py:221
  269.8 28.0 %collective-permute-start.23 = (bf16[512,4096]{1,0:T(8,128)(2,1)}, bf16[512,4096]{1,0:T(8,128)(2,1)}, u32[]{:S(2)}, u32[]{:S(2)}) collective-permute-start(bf16[512,4096]{1,0:T(8,128)(2,1)} %weight_product.8), channel_id=1, source_target_pairs={{0,16},{16,0},{1,17},{17,1},{2,18},{18,2},{3,19},{19,3},{4,20},{20... | collective-permute-start | bytes 12582920 | tf_op jit(solution)/shard_map/ppermute | solution.py:216
  277.6 28.2 %collective-permute-start.24 = (bf16[128,4096]{1,0:T(8,128)(2,1)S(1)}, bf16[128,4096]{1,0:T(8,128)(2,1)S(1)}, u32[]{:S(2)}, u32[]{:S(2)}) collective-permute-start(bf16[128,4096]{1,0:T(8,128)(2,1)S(1)} %get-tuple-element.462), channel_id=1, source_target_pairs={{0,2},{1,3},{2,0},{3,1},{4,6},{5,7},{6,4},{7,5},{8,10},{9,11},{10,... | collective-permute-start | bytes 3145736 | tf_op jit(solution)/shard_map/ppermute | solution.py:232
  305.4 30.7 %collective-permute-start.28 = (bf16[256,4096]{1,0:T(8,128)(2,1)S(1)}, bf16[256,4096]{1,0:T(8,128)(2,1)}, u32[]{:S(2)}, u32[]{:S(2)}) collective-permute-start(bf16[256,4096]{1,0:T(8,128)(2,1)S(1)} %get-tuple-element.484), channel_id=1, source_target_pairs={{0,1},{1,0},{2,3},{3,2},{4,5},{5,4},{6,7},{7,6},{8,9},{9,8},{10,11... | collective-permute-start | bytes 6291464 | tf_op jit(solution)/shard_map/ppermute | solution.py:221
  306.1 28.9 %collective-permute-start.25 = (bf16[32,4096]{1,0:T(8,128)(2,1)S(1)}, bf16[32,4096]{1,0:T(8,128)(2,1)S(1)}, u32[]{:S(2)}, u32[]{:S(2)}) collective-permute-start(bf16[32,4096]{1,0:T(8,128)(2,1)S(1)} %get-tuple-element.478), channel_id=1, source_target_pairs={{0,4},{1,5},{2,6},{3,7},{4,0},{5,1},{6,2},{7,3},{8,12},{9,13},{10,... | collective-permute-start | bytes 786440 | tf_op jit(solution)/shard_map/ppermute | solution.py:239
  306.2 28.8 %collective-permute-start.26 = (bf16[32,4096]{1,0:T(8,128)(2,1)S(1)}, bf16[32,4096]{1,0:T(8,128)(2,1)S(1)}, u32[]{:S(2)}, u32[]{:S(2)}) collective-permute-start(bf16[32,4096]{1,0:T(8,128)(2,1)S(1)} %get-tuple-element.479), channel_id=1, source_target_pairs={{0,8},{1,9},{2,10},{3,11},{4,12},{5,13},{6,14},{7,15},{8,0},{9,1},... | collective-permute-start | bytes 786440 | tf_op jit(solution)/shard_map/ppermute | solution.py:239
  308.0 27.0 %collective-permute-start.27 = (bf16[32,4096]{1,0:T(8,128)(2,1)S(1)}, bf16[32,4096]{1,0:T(8,128)(2,1)S(1)}, u32[]{:S(2)}, u32[]{:S(2)}) collective-permute-start(bf16[32,4096]{1,0:T(8,128)(2,1)S(1)} %get-tuple-element.480), channel_id=1, source_target_pairs={{0,12},{1,13},{2,14},{3,15},{4,8},{5,9},{6,10},{7,11},{8,4},{9,5},... | collective-permute-start | bytes 786440 | tf_op jit(solution)/shard_map/ppermute | solution.py:239
  351.7 22.8 %collective-permute-start.30 = (bf16[128,4096]{1,0:T(8,128)(2,1)}, bf16[128,4096]{1,0:T(8,128)(2,1)}, u32[]{:S(2)}, u32[]{:S(2)}) collective-permute-start(bf16[128,4096]{1,0:T(8,128)(2,1)} %get-tuple-element.507), channel_id=1, source_target_pairs={{0,2},{1,3},{2,0},{3,1},{4,6},{5,7},{6,4},{7,5},{8,10},{9,11},{10,... | collective-permute-start | bytes 3145736 | tf_op jit(solution)/shard_map/ppermute | solution.py:232
  386.8 18.8 %collective-permute-start.31 = (bf16[512,1408]{1,0:T(8,128)(2,1)}, bf16[512,1408]{1,0:T(8,128)(2,1)}, u32[]{:S(2)}, u32[]{:S(2)}) collective-permute-start(bf16[512,1408]{1,0:T(8,128)(2,1)} %last_product.2), channel_id=1, source_target_pairs={{0,16},{16,0},{1,17},{17,1},{2,18},{18,2},{3,19},{19,3},{4,20},{20... | collective-permute-start | bytes 4325384 | tf_op jit(solution)/shard_map/ppermute | solution.py:216
  388.2 26.4 %collective-permute-start.32 = (bf16[256,4096]{1,0:T(8,128)(2,1)}, bf16[256,4096]{1,0:T(8,128)(2,1)}, u32[]{:S(2)}, u32[]{:S(2)}) collective-permute-start(bf16[256,4096]{1,0:T(8,128)(2,1)} %get-tuple-element.532), channel_id=1, source_target_pairs={{0,1},{1,0},{2,3},{3,2},{4,5},{5,4},{6,7},{7,6},{8,9},{9,8},{10,11... | collective-permute-start | bytes 6291464 | tf_op jit(solution)/shard_map/ppermute | solution.py:221
  401.1 28.2 %collective-permute-start.34 = (bf16[32,4096]{1,0:T(8,128)(2,1)}, bf16[32,4096]{1,0:T(8,128)(2,1)}, u32[]{:S(2)}, u32[]{:S(2)}) collective-permute-start(bf16[32,4096]{1,0:T(8,128)(2,1)} %get-tuple-element.545), channel_id=1, source_target_pairs={{0,4},{1,5},{2,6},{3,7},{4,0},{5,1},{6,2},{7,3},{8,12},{9,13},{10,... | collective-permute-start | bytes 786440 | tf_op jit(solution)/shard_map/ppermute | solution.py:239
  401.2 28.2 %collective-permute-start.35 = (bf16[32,4096]{1,0:T(8,128)(2,1)}, bf16[32,4096]{1,0:T(8,128)(2,1)}, u32[]{:S(2)}, u32[]{:S(2)}) collective-permute-start(bf16[32,4096]{1,0:T(8,128)(2,1)} %get-tuple-element.546), channel_id=1, source_target_pairs={{0,8},{1,9},{2,10},{3,11},{4,12},{5,13},{6,14},{7,15},{8,0},{9,1},... | collective-permute-start | bytes 786440 | tf_op jit(solution)/shard_map/ppermute | solution.py:239
  404.5 24.9 %collective-permute-start.36 = (bf16[32,4096]{1,0:T(8,128)(2,1)}, bf16[32,4096]{1,0:T(8,128)(2,1)}, u32[]{:S(2)}, u32[]{:S(2)}) collective-permute-start(bf16[32,4096]{1,0:T(8,128)(2,1)} %get-tuple-element.547), channel_id=1, source_target_pairs={{0,12},{1,13},{2,14},{3,15},{4,8},{5,9},{6,10},{7,11},{8,4},{9,5},... | collective-permute-start | bytes 786440 | tf_op jit(solution)/shard_map/ppermute | solution.py:239
  424.5 25.1 %collective-permute-start.37 = (bf16[128,5504]{1,0:T(8,128)(2,1)}, bf16[128,5504]{1,0:T(8,128)(2,1)}, u32[]{:S(2)}, u32[]{:S(2)}) collective-permute-start(bf16[128,5504]{1,0:T(8,128)(2,1)} %get-tuple-element.551), channel_id=1, source_target_pairs={{0,2},{1,3},{2,0},{3,1},{4,6},{5,7},{6,4},{7,5},{8,10},{9,11},{10,... | collective-permute-start | bytes 4227080 | tf_op jit(solution)/shard_map/ppermute | solution.py:232
  431.4 32.7 %all-to-all-start.2 = ((bf16[16,49,512]{2,1,0:T(8,128)(2,1)}), bf16[16,49,512]{2,1,0:T(8,128)(2,1)S(1)}, u32[]{:S(2)}, u32[]{:S(2)}) async-start(bf16[16,49,512]{2,1,0:T(8,128)(2,1)} %reshape.428), calls=%async_computation.2 | async-start | bytes 1835008 | tf_op jit(solution)/shard_map/all_to_all | solution.py:1049
  452.6 21.7 %collective-permute-start.38 = (bf16[32,5504]{1,0:T(8,128)(2,1)}, bf16[32,5504]{1,0:T(8,128)(2,1)}, u32[]{:S(2)}, u32[]{:S(2)}) collective-permute-start(bf16[32,5504]{1,0:T(8,128)(2,1)} %get-tuple-element.562), channel_id=1, source_target_pairs={{0,4},{1,5},{2,6},{3,7},{4,0},{5,1},{6,2},{7,3},{8,12},{9,13},{10,... | collective-permute-start | bytes 1056776 | tf_op jit(solution)/shard_map/ppermute | solution.py:239
  452.6 30.0 %collective-permute-start.39 = (bf16[32,5504]{1,0:T(8,128)(2,1)}, bf16[32,5504]{1,0:T(8,128)(2,1)}, u32[]{:S(2)}, u32[]{:S(2)}) collective-permute-start(bf16[32,5504]{1,0:T(8,128)(2,1)} %get-tuple-element.563), channel_id=1, source_target_pairs={{0,8},{1,9},{2,10},{3,11},{4,12},{5,13},{6,14},{7,15},{8,0},{9,1},... | collective-permute-start | bytes 1056776 | tf_op jit(solution)/shard_map/ppermute | solution.py:239
  455.0 27.6 %collective-permute-start.40 = (bf16[32,5504]{1,0:T(8,128)(2,1)}, bf16[32,5504]{1,0:T(8,128)(2,1)}, u32[]{:S(2)}, u32[]{:S(2)}) collective-permute-start(bf16[32,5504]{1,0:T(8,128)(2,1)} %get-tuple-element.564), channel_id=1, source_target_pairs={{0,12},{1,13},{2,14},{3,15},{4,8},{5,9},{6,10},{7,11},{8,4},{9,5},... | collective-permute-start | bytes 1056776 | tf_op jit(solution)/shard_map/ppermute | solution.py:239
  (158 other events, 1457.0 us)
